TPU v7x, 32 devices: a whole 2x2x4 slice. The times are simulated.
32 devices in a mesh: wide: 8 (over z, core), narrow: 4 (over y, x).
Axes of the slice: x: 2, y: 2, z: 4, core: 2. Of those that a mesh axis runs over, the one named last changes fastest.
Arguments:
- a_blocks: float32 [4, 48, 128, 128], P('narrow', 'wide'), may hold values from -1.2 to 1.2
- a_index: int32 [4, 2, 48], P('narrow', None, 'wide'), may hold values from -1 to 1023, as said below
- b_blocks: float32 [4, 192, 128, 128], P('narrow', 'wide'), may hold values from -1.2 to 1.2
- b_index: int32 [4, 2, 192], P('narrow', None, 'wide'), may hold values from -1 to 1023, as said below
Outputs:
- product: float32 [4, 2, 8, 4, 128, 128], P('narrow', None, 'wide')
Inputs may be any that keep to these rules, and one draw needn't show every extreme that they name: Slot s of a_index[r] is empty, with both entries -1, or names a block row congruent to r modulo 4 and a block column congruent to s // 6 modulo 8; no block is named twice. Slot s of b_index[r] is empty, with both entries -1, or names a block row congruent to r modulo 4 and a window block column congruent to s // 24 modulo 8; no block is named twice.
All inputs are finite; a program needn't handle non-finite values.
Results may differ from a plain program's by a relative error of at most 0.0001.
Values sent between devices are 32-bit elements; how exact they have to be, the bound alone decides.
No kernel may reach another device: no remote copies, remote signals or barrier semaphores. Data moves between devices by JAX's collectives and lax.ppermute only.
A program may use at most 128 MiB of HBM per device.

v0:
```python
import jax
import jax.numpy as jnp
from jax import lax
from jax.sharding import PartitionSpec as P

RL = 2
CL = 4


def broadcast(block, axis, owner):
    block = jnp.where(lax.axis_index(axis) == owner, block, jnp.zeros_like(block))
    return lax.psum(block, axis)


def shifted(value, axis, by):
    size = lax.axis_size(axis)
    return lax.ppermute(value, axis, [(i, (i + by) % size) for i in range(size)])


def accumulate(accumulated, first_vals, first_idx, second_vals, second_idx, narrow_size, wide_size):
    slot_count = first_vals.shape[0]
    row_local = jnp.floor_divide(first_idx[0], narrow_size)
    first_ok = first_idx[0] >= 0
    second_ok = second_idx[0] >= 0
    levels = jnp.arange(accumulated.shape[0])
    matched = (first_idx[1][None, None, :] == second_idx[0][:, None, None]) & (
        row_local[None, None, :] == levels[None, :, None]
    )
    matched = matched & first_ok[None, None, :] & second_ok[:, None, None]
    picked = jnp.sum(jnp.where(matched, jnp.arange(slot_count)[None, None, :], 0), axis=2)
    present = jnp.any(matched, axis=2)
    row_panel = jnp.take(first_vals, picked, axis=0) * present[:, :, None, None].astype(jnp.float32)
    partial_value = jnp.einsum(
        "blxy,byz->blxz", row_panel, second_vals, precision=lax.Precision.HIGHEST
    )
    column_local = jnp.floor_divide(second_idx[1], wide_size)
    placing = (
        (column_local[:, None] == jnp.arange(accumulated.shape[1])[None, :]) & second_ok[:, None]
    ).astype(jnp.float32)
    return accumulated + jnp.einsum(
        "bm,blxz->lmxz", placing, partial_value, precision=lax.Precision.HIGHEST
    )


def local(a_blocks, a_index, b_blocks, b_index):
    narrow_size = lax.axis_size("narrow")
    wide_size = lax.axis_size("wide")
    my_row = lax.axis_index("narrow")
    edge = a_blocks.shape[-1]
    slots_first = a_blocks.shape[1]
    slots_second = b_blocks.shape[1]
    first_vals = a_blocks.reshape(slots_first, edge, edge)
    first_idx = a_index.reshape(2, slots_first)
    second_vals = b_blocks.reshape(slots_second, edge, edge)
    second_idx = b_index.reshape(2, slots_second)
    owners = wide_size // narrow_size
    accumulated = jnp.zeros((RL, CL, edge, edge), jnp.float32)
    slab = (second_vals, second_idx)
    for step_id in range(narrow_size):
        if step_id > 0:
            slab = shifted((slab[0], slab[1]), "narrow", -1)
        group_id = (my_row + step_id) % narrow_size
        value_list = []
        index_list = []
        for owner_id in range(owners):
            source = group_id + owner_id * narrow_size
            got_vals, got_idx = (
                broadcast(first_vals, "wide", source),
                broadcast(first_idx, "wide", source),
            )
            value_list.append(got_vals)
            index_list.append(got_idx)
        piece_vals = jnp.concatenate(value_list, axis=0)
        piece_idx = jnp.concatenate(index_list, axis=1)
        accumulated = accumulate(
            accumulated, piece_vals, piece_idx, slab[0], slab[1], narrow_size, wide_size
        )
    return accumulated.reshape(1, RL, 1, CL, edge, edge)


def solution(mesh):
    return jax.shard_map(
        local,
        mesh=mesh,
        in_specs=(
            P("narrow", "wide", None, None),
            P("narrow", None, "wide"),
            P("narrow", "wide", None, None),
            P("narrow", None, "wide"),
        ),
        out_specs=P("narrow", None, "wide", None, None, None),
        check_vma=False,
    )
```

profile of v0, /device:TPU:0, one launch (start us, length us, event | category | flops | bytes accessed | tf_op | source)
XLA Modules:
  0.0 157.3 jit_solution(187671038013596646)
XLA Ops:
  6.5 3.9 %collective-permute-start = (s32[2,24]{1,0:T(2,128)}, s32[2,24]{1,0:T(2,128)S(1)}, u32[]{:S(2)}, u32[]{:S(2)}) collective-permute-start(s32[2,24]{1,0:T(2,128)} %bitcast.179), channel_id=1, source_target_pairs={{0,3},{1,0},{2,1},{3,2},{4,7},{5,4},{6,5},{7,6},{8,11},{9,8},{10,9... | collective-permute-start | bytes 584 | tf_op jit(solution)/shard_map/ppermute | solution.py:17
  10.4 0.5 collective-permute-start.1
  11.0 2.7 %select_bitcast_fusion.1 = (f32[6,128,128]{2,1,0:T(8,128)}, f32[6,128,128]{2,1,0:T(8,128)}, f32[6,128,128]{2,1,0:T(8,128)}, f32[6,128,128]{2,1,0:T(8,128)}, f32[...) fusion(f32[1,6,128,128]{3,2,1,0:T(8,128)} %param.6, ...), kind=kLoop, calls=%fused_computation.45 | loop fusion | flops 786432 | bytes 3538952 | tf_op jit(solution)/shard_map/jit(_where)/select_n | solution.py:11
  13.7 9.4 %all-reduce = (s32[2,6]{1,0:T(2,128)S(1)}, s32[2,6]{1,0:T(2,128)S(1)}, s32[2,6]{1,0:T(2,128)S(1)}, s32[2,6]{1,0:T(2,128)S(1)}, s32[2,6]{1,0:T(2,128)S(1)}, /*ind...) all-reduce(s32[2,6]{1,0:T(2,128)S(1)} %get-tuple-element.33, ...), channel_id=1, replica_groups=mesh['wide'=8,'narrow'=4] {'wide'}, use_global_device_ids=true, to_apply=%region_9.11 | all-reduce | flops 96 | bytes 768 | tf_op jit(solution)/shard_map/psum | solution.py:12
  24.2 0.1 copy.8
  24.9 1.5 collective-permute-start.2
  26.5 0.1 copy.13
  26.6 20.0 %collective-permute-done.2 = s32[2,24]{1,0:T(2,128)S(1)} collective-permute-done((s32[2,24]{1,0:T(2,128)S(1)}, s32[2,24]{1,0:T(2,128)S(1)}, u32[]{:S(2)}, u32[]{:S(2)}) %collective-permute-start.2) | collective-permute-done | bytes 224 | tf_op jit(solution)/shard_map/ppermute | solution.py:17
  47.0 1.5 collective-permute-start.4
  48.7 0.1 copy.18
  48.8 1.8 %collective-permute-done.4 = s32[2,24]{1,0:T(2,128)S(1)} collective-permute-done((s32[2,24]{1,0:T(2,128)S(1)}, s32[2,24]{1,0:T(2,128)S(1)}, u32[]{:S(2)}, u32[]{:S(2)}) %collective-permute-start.4) | collective-permute-done | bytes 224 | tf_op jit(solution)/shard_map/ppermute | solution.py:17
  50.8 2.4 %collective-permute-start.3 = (f32[24,128,128]{2,1,0:T(8,128)}, f32[24,128,128]{2,1,0:T(8,128)}, u32[]{:S(2)}, u32[]{:S(2)}) collective-permute-start(f32[24,128,128]{2,1,0:T(8,128)} %collective-permute-done.1), channel_id=1, source_target_pairs={{0,3},{1,0},{2,1},{3,2},{4,7},{5,4},{6,5},{7,6},{8,11},{9,8},{10,9... | collective-permute-start | bytes 4718600 | tf_op jit(solution)/shard_map/ppermute | solution.py:17
  53.4 0.1 fusion.43
  53.6 0.1 copy.23
  53.7 39.9 %all-reduce.4.cloned.1.call-done = (f32[6,128,128]{2,1,0:T(8,128)}, f32[6,128,128]{2,1,0:T(8,128)}, f32[6,128,128]{2,1,0:T(8,128)}, f32[6,128,128]{2,1,0:T(8,128...) async-done(((f32[6,128,128]{2,1,0:T(8,128)}, f32[6,128,128]{2,1,0:T(8,128)}, f32[6,128,128]{2,1,0:T(8,128)}, ...) | async-done | bytes 3145744 | tf_op jit(solution)/shard_map/psum | solution.py:12
  93.6 1.5 pad_maximum_fusion
  95.0 2.4 %gather_fusion.1 = f32[48,128,128]{2,1,0:T(8,128)} fusion(f32[12,128,128]{2,1,0:T(8,128)S(1)} %get-tuple-element.39, s32[1024]{0:T(1024)S(1)} %pad_clamp_fusion.2), kind=kCustom, calls=%fused_computation.1.clone | custom fusion | bytes 6291648 | tf_op jit(solution)/shard_map/jit(_take)/gather | solution.py:32
  97.5 5.0 %fusion.10 = f32[24,2,128,128]{3,2,1,0:T(8,128)S(1)} fusion(f32[24,2,128,128]{3,2,1,0:T(8,128)} %bitcast.177, f32[24,128,128]{2,1,0:T(8,128)} %collective-permute-done.1, f32[24,2]{1,0:T(8,128)S(1)} %copy.15, pred[24,2]{1,0:T(8,128)(4,1)S(1)} %copy.13), kind=kOutput, calls=%fused_computation.17 | convolution fusion | flops 1209532416 | bytes 7864560 | tf_op jit(solution)/shard_map/blxy,byz->blxz/dot_general | solution.py:33
  102.5 2.9 %fusion.4 = f32[2,128,128,4]{2,3,1,0:T(4,128)S(1)} fusion(f32[24,2,128,128]{3,2,1,0:T(8,128)S(1)} %fusion.10, s32[24]{0:T(128)S(1)} %and_select_fusion.4, pred[24]{0:T(512)(128)(4,1)S(1)} %broadcast_compare_fusion.6), kind=kOutput, calls=%fused_computation.8 | convolution fusion | flops 37748928 | bytes 3670136 | tf_op jit(solution)/shard_map/bm,blxz->lmxz/dot_general | solution.py:40
  105.4 2.4 %collective-permute-start.5 = (f32[24,128,128]{2,1,0:T(8,128)}, f32[24,128,128]{2,1,0:T(8,128)}, u32[]{:S(2)}, u32[]{:S(2)}) collective-permute-start(f32[24,128,128]{2,1,0:T(8,128)} %collective-permute-done.3), channel_id=1, source_target_pairs={{0,3},{1,0},{2,1},{3,2},{4,7},{5,4},{6,5},{7,6},{8,11},{9,8},{10,9... | collective-permute-start | bytes 4718600 | tf_op jit(solution)/shard_map/ppermute | solution.py:17
  107.8 0.1 pad_maximum_fusion.2
  107.9 2.5 %gather_fusion = f32[48,128,128]{2,1,0:T(8,128)} fusion(f32[12,128,128]{2,1,0:T(8,128)S(1)} %get-tuple-element.38, s32[1024]{0:T(1024)S(1)} %pad_clamp_fusion.3), kind=kCustom, calls=%fused_computation.clone | custom fusion | bytes 6291648 | tf_op jit(solution)/shard_map/jit(_take)/gather | solution.py:32
  110.4 2.4 %gather_fusion.2 = f32[48,128,128]{2,1,0:T(8,128)} fusion(f32[12,128,128]{2,1,0:T(8,128)S(1)} %get-tuple-element.40, s32[1024]{0:T(1024)S(1)} %pad_clamp_fusion.1), kind=kCustom, calls=%fused_computation.2.clone | custom fusion | bytes 6291648 | tf_op jit(solution)/shard_map/jit(_take)/gather | solution.py:32
  112.8 2.4 %gather_fusion.3 = f32[48,128,128]{2,1,0:T(8,128)} fusion(f32[12,128,128]{2,1,0:T(8,128)S(1)} %get-tuple-element.41, s32[1024]{0:T(1024)S(1)} %pad_clamp_fusion), kind=kCustom, calls=%fused_computation.3.clone | custom fusion | bytes 6291648 | tf_op jit(solution)/shard_map/jit(_take)/gather | solution.py:32
  115.3 5.2 %fusion.11 = f32[24,2,128,128]{3,2,1,0:T(8,128)S(1)} fusion(f32[24,2,128,128]{3,2,1,0:T(8,128)} %bitcast.176, f32[1,24,128,128]{3,2,1,0:T(8,128)} %param.8, f32[24,2]{1,0:T(8,128)S(1)} %copy.10, pred[24,2]{1,0:T(8,128)(4,1)S(1)} %copy.8), kind=kOutput, calls=%fused_computation.19 | convolution fusion | flops 1209532416 | bytes 7864560 | tf_op jit(solution)/shard_map/blxy,byz->blxz/dot_general | solution.py:33
  120.5 2.9 %fusion.28 = f32[2,128,128,4]{2,3,1,0:T(4,128)S(1)} fusion(f32[2,128,128,4]{2,3,1,0:T(4,128)S(1)} %fusion.4, f32[24,2,128,128]{3,2,1,0:T(8,128)S(1)} %fusion.11, s32[24]{0:T(128)S(1)} %and_select_fusion.6, pred[24]{0:T(512)(128)(4,1)S(1)} %broadcast_compare_fusion.7), kind=kOutput, calls=%fused_computation.36 | convolution fusion | flops 37880000 | bytes 4194424 | tf_op jit(solution)/shard_map/bm,blxz->lmxz/dot_general | solution.py:40
  123.4 4.9 %fusion.9 = f32[24,2,128,128]{3,2,1,0:T(8,128)S(1)} fusion(f32[24,2,128,128]{3,2,1,0:T(8,128)S(1)} %bitcast.175, f32[24,128,128]{2,1,0:T(8,128)} %collective-permute-done.3, f32[24,2]{1,0:T(8,128)S(1)} %copy.20, pred[24,2]{1,0:T(8,128)(4,1)S(1)} %copy.18), kind=kOutput, calls=%fused_computation.15 | convolution fusion | flops 1209532416 | bytes 7864560 | tf_op jit(solution)/shard_map/blxy,byz->blxz/dot_general | solution.py:33
  128.3 2.9 %fusion.31 = f32[2,128,128,4]{2,3,1,0:T(4,128)S(1)} fusion(f32[2,128,128,4]{2,3,1,0:T(4,128)S(1)} %fusion.28, f32[24,2,128,128]{3,2,1,0:T(8,128)S(1)} %fusion.9, s32[24]{0:T(128)S(1)} %and_select_fusion.2, pred[24]{0:T(512)(128)(4,1)S(1)} %broadcast_compare_fusion.4), kind=kOutput, calls=%fused_computation.37 | convolution fusion | flops 37880000 | bytes 4194424 | tf_op jit(solution)/shard_map/bm,blxz->lmxz/dot_general | solution.py:40
  131.2 10.4 %collective-permute-done.5 = f32[24,128,128]{2,1,0:T(8,128)} collective-permute-done((f32[24,128,128]{2,1,0:T(8,128)}, f32[24,128,128]{2,1,0:T(8,128)}, u32[]{:S(2)}, u32[]{:S(2)}) %collective-permute-start.5) | collective-permute-done | bytes 1572896 | tf_op jit(solution)/shard_map/ppermute | solution.py:17
  141.6 5.1 %fusion.8 = f32[24,2,128,128]{3,2,1,0:T(8,128)S(1)} fusion(f32[24,2,128,128]{3,2,1,0:T(8,128)S(1)} %bitcast.174, f32[24,128,128]{2,1,0:T(8,128)} %collective-permute-done.5, f32[24,2]{1,0:T(8,128)S(1)} %copy.25, pred[24,2]{1,0:T(8,128)(4,1)S(1)} %copy.23), kind=kOutput, calls=%fused_computation.13 | convolution fusion | flops 1209532416 | bytes 7864560 | tf_op jit(solution)/shard_map/blxy,byz->blxz/dot_general | solution.py:33
  146.7 2.9 %fusion.37 = f32[1,2,1,4,128,128]{5,3,4,1,2,0:T(4,128)S(1)} fusion(f32[2,128,128,4]{2,3,1,0:T(4,128)S(1)} %fusion.31, f32[24,2,128,128]{3,2,1,0:T(8,128)S(1)} %fusion.8, s32[24]{0:T(128)S(1)} %and_select_fusion, pred[24]{0:T(512)(128)(4,1)S(1)} %broadcast_compare_fusion.5), kind=kOutput, calls=%fused_computation.39 | convolution fusion | flops 37880000 | bytes 4194424 | tf_op jit(solution)/shard_map/bm,blxz->lmxz/dot_general | solution.py:40
  149.6 0.8 copy.27
  (93 shorter events, 2.7 us)
Async XLA Ops:
  6.5 87.0 %all-reduce.4.cloned.1.call-start = ((), (), s32[]{:S(2)}) async-start(), calls=%async_computation | async-start | bytes 6291456 | tf_op jit(solution)/shard_map/psum | solution.py:12
  6.5 17.8 %collective-permute-start = (s32[2,24]{1,0:T(2,128)}, s32[2,24]{1,0:T(2,128)S(1)}, u32[]{:S(2)}, u32[]{:S(2)}) collective-permute-start(s32[2,24]{1,0:T(2,128)} %bitcast.179), channel_id=1, source_target_pairs={{0,3},{1,0},{2,1},{3,2},{4,7},{5,4},{6,5},{7,6},{8,11},{9,8},{10,9... | collective-permute-start | bytes 584 | tf_op jit(solution)/shard_map/ppermute | solution.py:17
  10.4 40.4 %collective-permute-start.1 = (f32[24,128,128]{2,1,0:T(8,128)}, f32[24,128,128]{2,1,0:T(8,128)}, u32[]{:S(2)}, u32[]{:S(2)}) collective-permute-start(f32[24,128,128]{2,1,0:T(8,128)} %bitcast.178), channel_id=1, source_target_pairs={{0,3},{1,0},{2,1},{3,2},{4,7},{5,4},{6,5},{7,6},{8,11},{9,8},{10,9... | collective-permute-start | bytes 4718600 | tf_op jit(solution)/shard_map/ppermute | solution.py:17
  11.0 2.7 %copy-start.6 = (s32[1,2,6]{2,1,0:T(2,128)S(1)}, s32[1,2,6]{2,1,0:T(2,128)}, u32[]{:S(2)}) copy-start(s32[1,2,6]{2,1,0:T(2,128)} %param.7) | copy-start | bytes 148
  11.0 12.3 %copy-start.7 = (s32[1,2,24]{2,1,0:T(2,128)S(1)}, s32[1,2,24]{2,1,0:T(2,128)}, u32[]{:S(2)}) copy-start(s32[1,2,24]{2,1,0:T(2,128)} %param.9) | copy-start | bytes 580
  24.9 21.7 %collective-permute-start.2 = (s32[2,24]{1,0:T(2,128)S(1)}, s32[2,24]{1,0:T(2,128)S(1)}, u32[]{:S(2)}, u32[]{:S(2)}) collective-permute-start(s32[2,24]{1,0:T(2,128)S(1)} %collective-permute-done), channel_id=1, source_target_pairs={{0,3},{1,0},{2,1},{3,2},{4,7},{5,4},{6,5},{7,6},{8,11},{9,8},{10,9... | collective-permute-start | bytes 584 | tf_op jit(solution)/shard_map/ppermute | solution.py:17
  47.0 3.6 %collective-permute-start.4 = (s32[2,24]{1,0:T(2,128)S(1)}, s32[2,24]{1,0:T(2,128)S(1)}, u32[]{:S(2)}, u32[]{:S(2)}) collective-permute-start(s32[2,24]{1,0:T(2,128)S(1)} %collective-permute-done.2), channel_id=1, source_target_pairs={{0,3},{1,0},{2,1},{3,2},{4,7},{5,4},{6,5},{7,6},{8,11},{9,8},{10,9... | collective-permute-start | bytes 584 | tf_op jit(solution)/shard_map/ppermute | solution.py:17
  50.8 54.6 %collective-permute-start.3 = (f32[24,128,128]{2,1,0:T(8,128)}, f32[24,128,128]{2,1,0:T(8,128)}, u32[]{:S(2)}, u32[]{:S(2)}) collective-permute-start(f32[24,128,128]{2,1,0:T(8,128)} %collective-permute-done.1), channel_id=1, source_target_pairs={{0,3},{1,0},{2,1},{3,2},{4,7},{5,4},{6,5},{7,6},{8,11},{9,8},{10,9... | collective-permute-start | bytes 4718600 | tf_op jit(solution)/shard_map/ppermute | solution.py:17
  102.5 5.4 %copy-start.2 = (f32[6,128,128]{2,1,0:T(8,128)S(1)}, f32[6,128,128]{2,1,0:T(8,128)}, u32[]{:S(2)}) copy-start(f32[6,128,128]{2,1,0:T(8,128)} %get-tuple-element.18) | copy-start | bytes 1179652
  102.5 5.4 %copy-start.3 = (f32[6,128,128]{2,1,0:T(8,128)S(1)}, f32[6,128,128]{2,1,0:T(8,128)}, u32[]{:S(2)}) copy-start(f32[6,128,128]{2,1,0:T(8,128)} %get-tuple-element.19) | copy-start | bytes 1179652
  102.5 5.3 %copy-start.4 = (f32[6,128,128]{2,1,0:T(8,128)S(1)}, f32[6,128,128]{2,1,0:T(8,128)}, u32[]{:S(2)}) copy-start(f32[6,128,128]{2,1,0:T(8,128)} %get-tuple-element.20) | copy-start | bytes 1179652
  102.5 5.3 %copy-start.5 = (f32[6,128,128]{2,1,0:T(8,128)S(1)}, f32[6,128,128]{2,1,0:T(8,128)}, u32[]{:S(2)}) copy-start(f32[6,128,128]{2,1,0:T(8,128)} %get-tuple-element.21) | copy-start | bytes 1179652
  105.4 36.2 %collective-permute-start.5 = (f32[24,128,128]{2,1,0:T(8,128)}, f32[24,128,128]{2,1,0:T(8,128)}, u32[]{:S(2)}, u32[]{:S(2)}) collective-permute-start(f32[24,128,128]{2,1,0:T(8,128)} %collective-permute-done.3), channel_id=1, source_target_pairs={{0,3},{1,0},{2,1},{3,2},{4,7},{5,4},{6,5},{7,6},{8,11},{9,8},{10,9... | collective-permute-start | bytes 4718600 | tf_op jit(solution)/shard_map/ppermute | solution.py:17
  120.5 2.9 %copy-start.1 = (f32[48,128,128]{2,1,0:T(8,128)S(1)}, f32[48,128,128]{2,1,0:T(8,128)}, u32[]{:S(2)}) copy-start(f32[48,128,128]{2,1,0:T(8,128)} %gather_fusion.2) | copy-start | bytes 9437188
  128.3 13.3 %copy-start = (f32[48,128,128]{2,1,0:T(8,128)S(1)}, f32[48,128,128]{2,1,0:T(8,128)}, u32[]{:S(2)}) copy-start(f32[48,128,128]{2,1,0:T(8,128)} %gather_fusion.3) | copy-start | bytes 9437188
Sparse Core Ops, SparseCore 0:
  13.8 79.6 all-reduce.3
where the time goes:
time: 158 us; the launch traced here: 157 us
  waiting for transfers between devices  72.1 us (46%)
  matrix products  31.8 us (20%)
  between operations  13.8 us (9%)
  starting transfers between devices  12.3 us (8%)
  local copies, waits for them, and re-layouts  12.1 us (8%)
  blocking collectives  9.4 us (6%)
  other arithmetic  5.9 us (4%)
    psum x1, waiting for transfers between devices, broadcast(): return lax.psum(block, axis)  39.9 us
    ppermute x6, waiting for transfers between devices, shifted(): lax.ppermute(value, axis, [(i, (i + by) % size) for i in range(size)])  32.3 us
    dot_general x4, matrix products, accumulate(): jnp.einsum('blxy,byz->blxz', row_panel, second_vals, precision=lax.Precis...  20.2 us
    ppermute x6, starting transfers between devices, shifted(): lax.ppermute(value, axis, [(i, (i + by) % size) for i in range(size)])  12.3 us
    dot_general x4, matrix products, accumulate(): jnp.einsum('bm,blxz->lmxz', placing, partial_value, precision=lax.Precisi...  11.6 us
    gather x4, local copies, waits for them, and re-layouts, accumulate(): jnp.take(first_vals, picked, axis=0)  9.73 us
    psum x1, blocking collectives, broadcast(): return lax.psum(block, axis)  9.4 us
  transfers between devices with their start and end apart: 7, of which 4 were waited for; matrix products, arithmetic and copies ran while one was open for 26% of the time, Pallas kernels for 0%

commit v1 on v0

v1 whole, which is shorter than its diff:
```python
import functools

import jax
import jax.numpy as jnp
from jax import lax
from jax.experimental import pallas as pl
from jax.experimental.pallas import tpu as pltpu
from jax.sharding import PartitionSpec as P

RL = 2
CL = 4
KBLOCKS = 1024
PAD = 8
AXES = ("wide", "narrow")
VMEM_LIMIT = 32 * 1024 * 1024


def split(value):
    high = value.astype(jnp.bfloat16)
    low = (value - high.astype(jnp.float32)).astype(jnp.bfloat16)
    return high, low


def split_kernel(b_ref, high_ref, low_ref):
    slots, edge = b_ref.shape[0], b_ref.shape[2]

    def one(slot, _):
        high, low = split(b_ref[slot])
        rows = pl.ds(pl.multiple_of(slot * edge, edge), edge)
        high_ref[rows, :] = high
        low_ref[rows, :] = low
        return 0

    lax.fori_loop(0, slots, one, 0)
    high_ref[slots * edge :, :] = jnp.zeros((edge, edge), jnp.bfloat16)
    low_ref[slots * edge :, :] = jnp.zeros((edge, edge), jnp.bfloat16)


def split_blocks(b_blocks):
    slots, edge, _ = b_blocks.shape
    shape = jax.ShapeDtypeStruct(((slots + 1) * edge, edge), jnp.bfloat16)
    return pl.pallas_call(
        split_kernel,
        out_shape=(shape, shape),
        compiler_params=pltpu.CompilerParams(vmem_limit_bytes=VMEM_LIMIT),
    )(b_blocks)


def product_kernel(
    edge, slots, table_ref, one_ref, two_ref, high_ref, low_ref, out_ref,
    a_ref, index_ref, left_high, left_low, right_high, right_low, block_sems, index_sems,
):
    shares = (one_ref, two_ref)
    rows = slots * edge
    index_copies = [
        pltpu.make_async_copy(ref.at[pl.ds(rows, PAD)], index_ref.at[n], index_sems.at[n])
        for n, ref in enumerate(shares)
    ]
    block_copies = [
        pltpu.make_async_copy(ref.at[pl.ds(0, rows)], a_ref.at[n], block_sems.at[n])
        for n, ref in enumerate(shares)
    ]
    for copy in index_copies + block_copies:
        copy.start()
    for copy in index_copies:
        copy.wait()
    for n in range(len(shares)):
        for slot in range(slots):
            at = (n * slots + slot) * edge
            inner = index_ref[n, 1, slot].astype(jnp.int32)
            for m in range(CL):
                block = table_ref[inner * CL + m]
                source = pl.ds(pl.multiple_of(block * edge, edge), edge)
                right_high[at : at + edge, m * edge : (m + 1) * edge] = high_ref[source, :]
                right_low[at : at + edge, m * edge : (m + 1) * edge] = low_ref[source, :]
    left_high[...] = jnp.zeros_like(left_high)
    left_low[...] = jnp.zeros_like(left_low)
    for copy in block_copies:
        copy.wait()
    for n in range(len(shares)):
        for slot in range(slots):
            at = (n * slots + slot) * edge
            line = index_ref[n, 0, slot].astype(jnp.int32)
            high, low = split(a_ref[n, slot * edge : (slot + 1) * edge, :])
            target = pl.ds(pl.multiple_of(line * edge, edge), edge)
            left_high[target, at : at + edge] = high
            left_low[target, at : at + edge] = low
    dot = functools.partial(jnp.dot, preferred_element_type=jnp.float32)
    for m in range(0, CL, 2):
        columns = slice(m * edge, (m + 2) * edge)
        value = (
            dot(left_high[...], right_high[:, columns])
            + dot(left_low[...], right_high[:, columns])
            + dot(left_high[...], right_low[:, columns])
        )
        for l in range(RL):
            for n in range(2):
                out_ref[l * CL + m + n] = value[l * edge : (l + 1) * edge, n * edge : (n + 1) * edge]


def product(table, one, two, high, low, slots):
    edge = high.shape[1]
    depth = 2 * slots * edge
    return pl.pallas_call(
        functools.partial(product_kernel, edge, slots),
        out_shape=jax.ShapeDtypeStruct((RL * CL, edge, edge), jnp.float32),
        in_specs=[
            pl.BlockSpec(memory_space=pltpu.SMEM),
            pl.BlockSpec(memory_space=pl.ANY),
            pl.BlockSpec(memory_space=pl.ANY),
            pl.BlockSpec(memory_space=pltpu.VMEM),
            pl.BlockSpec(memory_space=pltpu.VMEM),
        ],
        out_specs=pl.BlockSpec(memory_space=pltpu.VMEM),
        scratch_shapes=[
            pltpu.VMEM((2, slots * edge, edge), jnp.float32),
            pltpu.SMEM((2, PAD, edge), jnp.float32),
            pltpu.VMEM((RL * edge, depth), jnp.bfloat16),
            pltpu.VMEM((RL * edge, depth), jnp.bfloat16),
            pltpu.VMEM((depth, CL * edge), jnp.bfloat16),
            pltpu.VMEM((depth, CL * edge), jnp.bfloat16),
            pltpu.SemaphoreType.DMA((2,)),
            pltpu.SemaphoreType.DMA((2,)),
        ],
        compiler_params=pltpu.CompilerParams(vmem_limit_bytes=VMEM_LIMIT),
        cost_estimate=pl.CostEstimate(
            flops=6 * RL * depth * CL * edge * edge, bytes_accessed=4 * 1024 * 1024, transcendentals=0
        ),
    )(table, one, two, high, low)


def local(a_blocks, a_index, b_blocks, b_index):
    narrow = lax.axis_size("narrow")
    wide = lax.axis_size("wide")
    slots = a_blocks.shape[1]
    edge = a_blocks.shape[-1]
    slots_second = b_blocks.shape[1]

    def device(row, column):
        return column * narrow + row

    stored = a_index[0, 0] >= 0
    line = jnp.where(stored, a_index[0, 0] // narrow, 0)
    inner = jnp.where(stored, a_index[0, 1] // narrow, KBLOCKS // narrow)
    index = jnp.stack([line, inner]).astype(jnp.float32)
    index = jnp.pad(index, ((0, PAD - 2), (0, edge - slots)))
    share = jnp.concatenate([a_blocks.reshape(slots * edge, edge), index], axis=0)

    table = jnp.arange((KBLOCKS // narrow + 1) * CL)[:, None]
    wanted = b_index[0, 0] // narrow * CL + b_index[0, 1] // wide
    hit = (table == wanted[None, :]) & (b_index[0, 0] >= 0)[None, :]
    table = slots_second + jnp.sum(jnp.where(hit, jnp.arange(slots_second)[None, :] - slots_second, 0), axis=1)
    table = table.astype(jnp.int32)
    high, low = split_blocks(b_blocks[0])

    total = None
    for step in range(narrow):
        spread = []
        for column in range(wide):
            target = column % narrow
            half = column // narrow
            for row in range(narrow):
                plane = row ^ target ^ step
                spread.append((device(row, column), device(target, plane * 2 + half)))
        mine = lax.ppermute(share, AXES, spread)
        swap = [(device(r, c), device(r, c ^ 1)) for r in range(narrow) for c in range(wide)]
        other = lax.ppermute(mine, AXES, swap)
        partial_value = product(table, mine, other, high, low, slots)
        back = [
            (device(r, c), device(r ^ (c // 2) ^ step, c)) for r in range(narrow) for c in range(wide)
        ]
        got = lax.ppermute(partial_value, AXES, back)
        total = got if total is None else total + got
    return total.reshape(1, RL, 1, CL, edge, edge)


def solution(mesh):
    return jax.shard_map(
        local,
        mesh=mesh,
        in_specs=(
            P("narrow", "wide", None, None),
            P("narrow", None, "wide"),
            P("narrow", "wide", None, None),
            P("narrow", None, "wide"),
        ),
        out_specs=P("narrow", None, "wide", None, None, None),
        check_vma=False,
    )
```

time: 158 us -> 91 us (0.58)
  waiting for transfers between devices: 72.1 us -> 17.2 us
  starting transfers between devices: 12.3 us -> 53.2 us
  matrix products: 31.8 us -> 0 us
  Pallas kernels: 0 us -> 14.2 us
  between operations: 13.8 us -> 0.21 us
  local copies, waits for them, and re-layouts: 12.1 us -> 1.41 us
  blocking collectives: 9.4 us -> 0 us
  other arithmetic: 5.9 us -> 4.29 us
    ppermute x6 -> x12, starting transfers between devices: 12.3 us -> 53.2 us  [the longest x4 25.2 us: local(): other = lax.ppermute(mine, AXES, swap)]
    psum x1 -> x0, waiting for transfers between devices: 39.9 us -> none  [broadcast(): return lax.psum(block, axis)]
    dot_general x8 -> x0, matrix products: 31.8 us -> none  [the longest x4 20.2 us: accumulate(): jnp.einsum('blxy,byz->blxz', row_panel, second_vals, precision=lax.Precis...]
    ppermute x6 -> x12, waiting for transfers between devices: 32.3 us -> 17.2 us  [the longest x4 17.2 us: local(): got = lax.ppermute(partial_value, AXES, back)]
    pallas_call x0 -> x5, Pallas kernels: none -> 14.2 us  [the longest x4 14 us: product(): pl.pallas_call(functools.partial(product_kernel, edge, slots), out_shape=...]
    gather x4 -> x0, local copies, waits for them, and re-layouts: 9.73 us -> none  [accumulate(): jnp.take(first_vals, picked, axis=0)]
    psum x1 -> x0, blocking collectives: 9.4 us -> none  [broadcast(): return lax.psum(block, axis)]
    select_n x14 -> x1, other arithmetic: 2.82 us -> 0.76 us  [local(): line = jnp.where(stored, a_index[0, 0] // narrow, 0)]
  transfers between devices with their start and end apart: 7 -> 12, of which waited for: 4 -> 1; matrix products, arithmetic and copies ran while one was open for 26% -> 2% of each run, Pallas kernels for 0% -> 16%
where the time goes in v1:
time: 91 us; the launch traced here: 90.6 us
  starting transfers between devices  53.2 us (58%)
  waiting for transfers between devices  17.2 us (19%)
  Pallas kernels  14.2 us (16%)
  other arithmetic  4.29 us (5%)
  local copies, waits for them, and re-layouts  1.41 us (2%)
    ppermute x4, starting transfers between devices, local(): other = lax.ppermute(mine, AXES, swap)  25.2 us
    ppermute x4, starting transfers between devices, local(): mine = lax.ppermute(share, AXES, spread)  18.1 us
    ppermute x4, waiting for transfers between devices, local(): got = lax.ppermute(partial_value, AXES, back)  17.2 us
    pallas_call x4, Pallas kernels, product(): pl.pallas_call(functools.partial(product_kernel, edge, slots), out_shape=...  14 us
    ppermute x4, starting transfers between devices, local(): got = lax.ppermute(partial_value, AXES, back)  9.91 us
  transfers between devices with their start and end apart: 12, of which 1 were waited for; matrix products, arithmetic and copies ran while one was open for 2% of the time, Pallas kernels for 16%

profile of v1, /device:TPU:0, one launch (start us, length us, event | category | flops | bytes accessed | tf_op | source)
XLA Modules:
  0.0 90.6 jit_solution(756118747116473449)
XLA Ops:
  0.0 0.8 compare_select_fusion.13
  0.8 1.0 %select_maximum_fusion = f32[776,128]{1,0:T(8,128)S(1)} fusion(f32[2,6]{1,0:T(2,128)S(1)} %add_convert_fusion, f32[768,128]{1,0:T(8,128)} %bitcast.46), kind=kLoop, calls=%fused_computation.1 | loop fusion | flops 297984 | bytes 790576 | tf_op jit(solution)/shard_map/concatenate | solution.py:147
  1.8 0.7 collective-permute-start
  2.5 8.7 %collective-permute-start.3 = (f32[776,128]{1,0:T(8,128)S(1)}, f32[776,128]{1,0:T(8,128)S(1)}, u32[]{:S(2)}, u32[]{:S(2)}) collective-permute-start(f32[776,128]{1,0:T(8,128)S(1)} %select_maximum_fusion), channel_id=1, source_target_pairs={{0,8},{1,0},{2,24},{3,16},{4,1},{5,9},{6,17},{7,25},{8,26},{9,18},... | collective-permute-start | bytes 1191944 | tf_op jit(solution)/shard_map/ppermute | solution.py:165
  11.2 5.0 %collective-permute-start.6 = (f32[776,128]{1,0:T(8,128)S(1)}, f32[776,128]{1,0:T(8,128)S(1)}, u32[]{:S(2)}, u32[]{:S(2)}) collective-permute-start(f32[776,128]{1,0:T(8,128)S(1)} %select_maximum_fusion), channel_id=1, source_target_pairs={{0,16},{1,24},{2,0},{3,8},{4,25},{5,17},{6,9},{7,1},{8,2},{9,10},{... | collective-permute-start | bytes 1191944 | tf_op jit(solution)/shard_map/ppermute | solution.py:165
  16.2 3.7 %collective-permute-start.9 = (f32[776,128]{1,0:T(8,128)S(1)}, f32[776,128]{1,0:T(8,128)S(1)}, u32[]{:S(2)}, u32[]{:S(2)}) collective-permute-start(f32[776,128]{1,0:T(8,128)S(1)} %select_maximum_fusion), channel_id=1, source_target_pairs={{0,24},{1,16},{2,8},{3,0},{4,17},{5,25},{6,1},{7,9},{8,10},{9,2},{... | collective-permute-start | bytes 1191944 | tf_op jit(solution)/shard_map/ppermute | solution.py:165
  19.9 0.8 iota_add_fusion
  20.7 0.0 collective-permute-done.one_ref
  20.7 0.1 collective-permute-start.1
  20.8 0.7 bitcast_compare_fusion
  21.5 0.0 collective-permute-done.3.one_ref
  21.5 21.8 %collective-permute-start.4 = (f32[776,128]{1,0:T(8,128)S(1)}, f32[776,128]{1,0:T(8,128)S(1)}, u32[]{:S(2)}, u32[]{:S(2)}) collective-permute-start(f32[776,128]{1,0:T(8,128)S(1)} %collective-permute-done.3.one_ref), channel_id=1, source_target_pairs={{0,4},{4,0},{8,12},{12,8},{16,20},{20,16},{24,28},{28,24},{1,5},{5... | collective-permute-start | bytes 1191944 | tf_op jit(solution)/shard_map/ppermute | solution.py:167
  43.3 0.1 select_reduce_fusion
  43.4 0.0 collective-permute-done.6.one_ref
  43.4 0.1 collective-permute-start.7
  43.5 3.3 %collective-permute-start.10 = (f32[776,128]{1,0:T(8,128)S(1)}, f32[776,128]{1,0:T(8,128)S(1)}, u32[]{:S(2)}, u32[]{:S(2)}) collective-permute-start(f32[776,128]{1,0:T(8,128)S(1)} %collective-permute-done.9.one_ref), channel_id=1, source_target_pairs={{0,4},{4,0},{8,12},{12,8},{16,20},{20,16},{24,28},{28,24},{1,5},{5... | collective-permute-start | bytes 1191944 | tf_op jit(solution)/shard_map/ppermute | solution.py:167
  46.8 1.4 %copy-done = f32[1,24,128,128]{3,2,1,0:T(8,128)S(1)} copy-done((f32[1,24,128,128]{3,2,1,0:T(8,128)S(1)}, f32[1,24,128,128]{3,2,1,0:T(8,128)}, u32[]{:S(2)}) %copy-start) | copy-done | bytes 1572888
  48.2 0.3 shard_map.46
  48.4 0.0 collective-permute-done.1.two_ref
  48.5 3.5 %shard_map.47 = f32[8,128,128]{2,1,0:T(8,128)S(1)} custom-call(s32[1028]{0:T(1024)S(1)} %broadcast_add_fusion.table_ref, f32[776,128]{1,0:T(8,128)S(1)} %collective-permute-done.one_ref, f32[776,128]{1,0:T(8,128)S(1)} %collective-permute-done.1.two_ref, bf16[3200,128]{1,0:T(8,128)(2,1)S(1)} %get-tuple-element.7.high_ref, ...), custom_call_target="tpu_custom_call" | custom-call | flops 1207959552 | bytes 4194304 | tf_op jit(solution)/shard_map/pallas_call | solution.py:104
  52.0 0.7 collective-permute-start.2
  52.7 3.5 %shard_map.48 = f32[8,128,128]{2,1,0:T(8,128)S(1)} custom-call(s32[1028]{0:T(1024)S(1)} %broadcast_add_fusion.table_ref, f32[776,128]{1,0:T(8,128)S(1)} %collective-permute-done.3.one_ref, f32[776,128]{1,0:T(8,128)S(1)} %collective-permute-done.4.two_ref, bf16[3200,128]{1,0:T(8,128)(2,1)S(1)} %get-tuple-element.7.high_ref, ...), custom_call_target="tpu_custom_call" | custom-call | flops 1207959552 | bytes 4194304 | tf_op jit(solution)/shard_map/pallas_call | solution.py:104
  56.2 3.3 %collective-permute-start.5 = (f32[8,128,128]{2,1,0:T(8,128)S(1)}, f32[8,128,128]{2,1,0:T(8,128)S(1)}, u32[]{:S(2)}, u32[]{:S(2)}) collective-permute-start(f32[8,128,128]{2,1,0:T(8,128)S(1)} %shard_map.48), channel_id=1, source_target_pairs={{0,1},{4,5},{8,8},{12,12},{16,19},{20,23},{24,26},{28,30},{1,0},{5... | collective-permute-start | bytes 1572872 | tf_op jit(solution)/shard_map/ppermute | solution.py:172
  59.5 0.0 collective-permute-done.7.two_ref
  59.5 3.5 %shard_map.49 = f32[8,128,128]{2,1,0:T(8,128)S(1)} custom-call(s32[1028]{0:T(1024)S(1)} %broadcast_add_fusion.table_ref, f32[776,128]{1,0:T(8,128)S(1)} %collective-permute-done.6.one_ref, f32[776,128]{1,0:T(8,128)S(1)} %collective-permute-done.7.two_ref, bf16[3200,128]{1,0:T(8,128)(2,1)S(1)} %get-tuple-element.7.high_ref, ...), custom_call_target="tpu_custom_call" | custom-call | flops 1207959552 | bytes 4194304 | tf_op jit(solution)/shard_map/pallas_call | solution.py:104
  63.0 1.9 %collective-permute-start.8 = (f32[8,128,128]{2,1,0:T(8,128)S(1)}, f32[8,128,128]{2,1,0:T(8,128)S(1)}, u32[]{:S(2)}, u32[]{:S(2)}) collective-permute-start(f32[8,128,128]{2,1,0:T(8,128)S(1)} %shard_map.49), channel_id=1, source_target_pairs={{0,2},{4,6},{8,11},{12,15},{16,16},{20,20},{24,25},{28,29},{1,3},{... | collective-permute-start | bytes 1572872 | tf_op jit(solution)/shard_map/ppermute | solution.py:172
  64.9 3.5 %shard_map.50 = f32[8,128,128]{2,1,0:T(8,128)S(1)} custom-call(s32[1028]{0:T(1024)S(1)} %broadcast_add_fusion.table_ref, f32[776,128]{1,0:T(8,128)S(1)} %collective-permute-done.9.one_ref, f32[776,128]{1,0:T(8,128)S(1)} %collective-permute-done.10.two_ref, bf16[3200,128]{1,0:T(8,128)(2,1)S(1)} %get-tuple-element.7.high_ref, ...), custom_call_target="tpu_custom_call" | custom-call | flops 1207959552 | bytes 4194304 | tf_op jit(solution)/shard_map/pallas_call | solution.py:104
  68.4 4.0 %collective-permute-start.11 = (f32[8,128,128]{2,1,0:T(8,128)S(1)}, f32[8,128,128]{2,1,0:T(8,128)S(1)}, u32[]{:S(2)}, u32[]{:S(2)}) collective-permute-start(f32[8,128,128]{2,1,0:T(8,128)S(1)} %shard_map.50), channel_id=1, source_target_pairs={{0,3},{4,7},{8,10},{12,14},{16,17},{20,21},{24,24},{28,28},{1,2},{... | collective-permute-start | bytes 1572872 | tf_op jit(solution)/shard_map/ppermute | solution.py:172
  72.5 0.0 collective-permute-done.5
  72.5 17.2 %collective-permute-done.8 = f32[8,128,128]{2,1,0:T(8,128)S(1)} collective-permute-done((f32[8,128,128]{2,1,0:T(8,128)S(1)}, f32[8,128,128]{2,1,0:T(8,128)S(1)}, u32[]{:S(2)}, u32[]{:S(2)}) %collective-permute-start.8) | collective-permute-done | bytes 524320 | tf_op jit(solution)/shard_map/ppermute | solution.py:172
  89.7 0.0 collective-permute-done.11
  89.7 0.9 %add_add_fusion = f32[8,128,128]{2,1,0:T(8,128)} fusion(f32[8,128,128]{2,1,0:T(8,128)S(1)} %collective-permute-done.11, f32[8,128,128]{2,1,0:T(8,128)S(1)} %collective-permute-done.8, f32[8,128,128]{2,1,0:T(8,128)S(1)} %collective-permute-done.2, f32[8,128,128]{2,1,0:T(8,128)S(1)} %collective-permute-done.5), kind=kLoop, calls=%fused_computation | loop fusion | flops 393216 | bytes 2621440 | tf_op jit(solution)/shard_map/add | solution.py:173
  (7 shorter events, 0.0 us)
Async XLA Ops:
  1.8 18.9 %collective-permute-start = (f32[776,128]{1,0:T(8,128)S(1)}, f32[776,128]{1,0:T(8,128)S(1)}, u32[]{:S(2)}, u32[]{:S(2)}) collective-permute-start(f32[776,128]{1,0:T(8,128)S(1)} %select_maximum_fusion), channel_id=1, source_target_pairs={{0,0},{1,8},{2,16},{3,24},{4,9},{5,1},{6,25},{7,17},{8,18},{9,26},... | collective-permute-start | bytes 1191944 | tf_op jit(solution)/shard_map/ppermute | solution.py:165
  2.5 19.0 %collective-permute-start.3 = (f32[776,128]{1,0:T(8,128)S(1)}, f32[776,128]{1,0:T(8,128)S(1)}, u32[]{:S(2)}, u32[]{:S(2)}) collective-permute-start(f32[776,128]{1,0:T(8,128)S(1)} %select_maximum_fusion), channel_id=1, source_target_pairs={{0,8},{1,0},{2,24},{3,16},{4,1},{5,9},{6,17},{7,25},{8,26},{9,18},... | collective-permute-start | bytes 1191944 | tf_op jit(solution)/shard_map/ppermute | solution.py:165
  11.2 32.2 %collective-permute-start.6 = (f32[776,128]{1,0:T(8,128)S(1)}, f32[776,128]{1,0:T(8,128)S(1)}, u32[]{:S(2)}, u32[]{:S(2)}) collective-permute-start(f32[776,128]{1,0:T(8,128)S(1)} %select_maximum_fusion), channel_id=1, source_target_pairs={{0,16},{1,24},{2,0},{3,8},{4,25},{5,17},{6,9},{7,1},{8,2},{9,10},{... | collective-permute-start | bytes 1191944 | tf_op jit(solution)/shard_map/ppermute | solution.py:165
  16.2 27.3 %collective-permute-start.9 = (f32[776,128]{1,0:T(8,128)S(1)}, f32[776,128]{1,0:T(8,128)S(1)}, u32[]{:S(2)}, u32[]{:S(2)}) collective-permute-start(f32[776,128]{1,0:T(8,128)S(1)} %select_maximum_fusion), channel_id=1, source_target_pairs={{0,24},{1,16},{2,8},{3,0},{4,17},{5,25},{6,1},{7,9},{8,10},{9,2},{... | collective-permute-start | bytes 1191944 | tf_op jit(solution)/shard_map/ppermute | solution.py:165
  20.7 27.8 %collective-permute-start.1 = (f32[776,128]{1,0:T(8,128)S(1)}, f32[776,128]{1,0:T(8,128)S(1)}, u32[]{:S(2)}, u32[]{:S(2)}) collective-permute-start(f32[776,128]{1,0:T(8,128)S(1)} %collective-permute-done.one_ref), channel_id=1, source_target_pairs={{0,4},{4,0},{8,12},{12,8},{16,20},{20,16},{24,28},{28,24},{1,5},{5... | collective-permute-start | bytes 1191944 | tf_op jit(solution)/shard_map/ppermute | solution.py:167
  21.5 31.2 %collective-permute-start.4 = (f32[776,128]{1,0:T(8,128)S(1)}, f32[776,128]{1,0:T(8,128)S(1)}, u32[]{:S(2)}, u32[]{:S(2)}) collective-permute-start(f32[776,128]{1,0:T(8,128)S(1)} %collective-permute-done.3.one_ref), channel_id=1, source_target_pairs={{0,4},{4,0},{8,12},{12,8},{16,20},{20,16},{24,28},{28,24},{1,5},{5... | collective-permute-start | bytes 1191944 | tf_op jit(solution)/shard_map/ppermute | solution.py:167
  43.4 16.1 %collective-permute-start.7 = (f32[776,128]{1,0:T(8,128)S(1)}, f32[776,128]{1,0:T(8,128)S(1)}, u32[]{:S(2)}, u32[]{:S(2)}) collective-permute-start(f32[776,128]{1,0:T(8,128)S(1)} %collective-permute-done.6.one_ref), channel_id=1, source_target_pairs={{0,4},{4,0},{8,12},{12,8},{16,20},{20,16},{24,28},{28,24},{1,5},{5... | collective-permute-start | bytes 1191944 | tf_op jit(solution)/shard_map/ppermute | solution.py:167
  43.5 21.4 %collective-permute-start.10 = (f32[776,128]{1,0:T(8,128)S(1)}, f32[776,128]{1,0:T(8,128)S(1)}, u32[]{:S(2)}, u32[]{:S(2)}) collective-permute-start(f32[776,128]{1,0:T(8,128)S(1)} %collective-permute-done.9.one_ref), channel_id=1, source_target_pairs={{0,4},{4,0},{8,12},{12,8},{16,20},{20,16},{24,28},{28,24},{1,5},{5... | collective-permute-start | bytes 1191944 | tf_op jit(solution)/shard_map/ppermute | solution.py:167
  46.8 1.4 %copy-start = (f32[1,24,128,128]{3,2,1,0:T(8,128)S(1)}, f32[1,24,128,128]{3,2,1,0:T(8,128)}, u32[]{:S(2)}) copy-start(f32[1,24,128,128]{3,2,1,0:T(8,128)} %param.6) | copy-start | bytes 4718596
  52.0 20.5 %collective-permute-start.2 = (f32[8,128,128]{2,1,0:T(8,128)S(1)}, f32[8,128,128]{2,1,0:T(8,128)S(1)}, u32[]{:S(2)}, u32[]{:S(2)}) collective-permute-start(f32[8,128,128]{2,1,0:T(8,128)S(1)} %shard_map.47), channel_id=1, source_target_pairs={{0,0},{4,4},{8,9},{12,13},{16,18},{20,22},{24,27},{28,31},{1,1},{5... | collective-permute-start | bytes 1572872 | tf_op jit(solution)/shard_map/ppermute | solution.py:172
  56.2 16.3 %collective-permute-start.5 = (f32[8,128,128]{2,1,0:T(8,128)S(1)}, f32[8,128,128]{2,1,0:T(8,128)S(1)}, u32[]{:S(2)}, u32[]{:S(2)}) collective-permute-start(f32[8,128,128]{2,1,0:T(8,128)S(1)} %shard_map.48), channel_id=1, source_target_pairs={{0,1},{4,5},{8,8},{12,12},{16,19},{20,23},{24,26},{28,30},{1,0},{5... | collective-permute-start | bytes 1572872 | tf_op jit(solution)/shard_map/ppermute | solution.py:172
  63.0 26.7 %collective-permute-start.8 = (f32[8,128,128]{2,1,0:T(8,128)S(1)}, f32[8,128,128]{2,1,0:T(8,128)S(1)}, u32[]{:S(2)}, u32[]{:S(2)}) collective-permute-start(f32[8,128,128]{2,1,0:T(8,128)S(1)} %shard_map.49), channel_id=1, source_target_pairs={{0,2},{4,6},{8,11},{12,15},{16,16},{20,20},{24,25},{28,29},{1,3},{... | collective-permute-start | bytes 1572872 | tf_op jit(solution)/shard_map/ppermute | solution.py:172
  68.4 21.2 %collective-permute-start.11 = (f32[8,128,128]{2,1,0:T(8,128)S(1)}, f32[8,128,128]{2,1,0:T(8,128)S(1)}, u32[]{:S(2)}, u32[]{:S(2)}) collective-permute-start(f32[8,128,128]{2,1,0:T(8,128)S(1)} %shard_map.50), channel_id=1, source_target_pairs={{0,3},{4,7},{8,10},{12,14},{16,17},{20,21},{24,24},{28,28},{1,2},{... | collective-permute-start | bytes 1572872 | tf_op jit(solution)/shard_map/ppermute | solution.py:172

commit v2 on v1

v2 whole, which is shorter than its diff:
```python
import functools

import jax
import jax.numpy as jnp
from jax import lax
from jax.experimental import pallas as pl
from jax.experimental.pallas import tpu as pltpu
from jax.sharding import PartitionSpec as P

RL = 2
CL = 4
KBLOCKS = 1024
PAD = 8
AXES = ("wide", "narrow")
VMEM_LIMIT = 32 * 1024 * 1024


def split(value):
    high = value.astype(jnp.bfloat16)
    low = (value - high.astype(jnp.float32)).astype(jnp.bfloat16)
    return high, low


def product_kernel(edge, slots, has_start, *refs):
    pick_ref, table_ref, mine_one, mine_two, other_one, other_two, b_hbm = refs[:7]
    refs = refs[7:]
    if has_start:
        start_ref, refs = refs[0], refs[1:]
    (out_ref, a_ref, index_ref, b_ref, left_high, left_low, right_high, right_low,
     block_sems, index_sems, b_sem) = refs
    rows = slots * edge
    slots_second = b_hbm.shape[0]
    b_copy = pltpu.make_async_copy(b_hbm, b_ref.at[pl.ds(0, slots_second)], b_sem)

    def copies(n, ref):
        return (
            pltpu.make_async_copy(ref.at[pl.ds(rows, PAD)], index_ref.at[n], index_sems.at[n]),
            pltpu.make_async_copy(ref.at[pl.ds(0, rows)], a_ref.at[n], block_sems.at[n]),
        )

    for n, (mine, other) in enumerate(((mine_one, other_one), (mine_two, other_two))):
        @pl.when(pick_ref[0] == 0)
        def _():
            for copy in copies(n, mine):
                copy.start()

        @pl.when(pick_ref[0] != 0)
        def _():
            for copy in copies(n, other):
                copy.start()

    b_copy.start()
    b_ref[slots_second] = jnp.zeros((edge, edge), jnp.float32)
    left_high[...] = jnp.zeros_like(left_high)
    left_low[...] = jnp.zeros_like(left_low)
    waits = [copies(n, ref) for n, ref in enumerate((mine_one, mine_two))]
    for index_copy, block_copy in waits:
        index_copy.wait()
        block_copy.wait()
    for n in range(2):
        for slot in range(slots):
            at = (n * slots + slot) * edge
            line = index_ref[n, 0, slot].astype(jnp.int32)
            high, low = split(a_ref[n, slot * edge : (slot + 1) * edge, :])
            target = pl.ds(pl.multiple_of(line * edge, edge), edge)
            left_high[target, at : at + edge] = high
            left_low[target, at : at + edge] = low
    b_copy.wait()
    for n in range(2):
        for slot in range(slots):
            at = (n * slots + slot) * edge
            inner = index_ref[n, 1, slot].astype(jnp.int32)
            for m in range(CL):
                high, low = split(b_ref[table_ref[inner * CL + m]])
                right_high[at : at + edge, m * edge : (m + 1) * edge] = high
                right_low[at : at + edge, m * edge : (m + 1) * edge] = low
    dot = functools.partial(jnp.dot, preferred_element_type=jnp.float32)
    for m in range(0, CL, 2):
        columns = slice(m * edge, (m + 2) * edge)
        value = (
            dot(left_high[...], right_high[:, columns])
            + dot(left_low[...], right_high[:, columns])
            + dot(left_high[...], right_low[:, columns])
        )
        for l in range(RL):
            for n in range(2):
                at = l * CL + m + n
                piece = value[l * edge : (l + 1) * edge, n * edge : (n + 1) * edge]
                out_ref[at] = start_ref[at] + piece if has_start else piece


def product(pick, table, mine, other, b_blocks, start=None):
    slots_second, edge, _ = b_blocks.shape
    slots = (mine[0].shape[0] - PAD) // edge
    depth = 2 * slots * edge
    anywhere = pl.BlockSpec(memory_space=pl.ANY)
    operands = [pick, table, *mine, *other, b_blocks] + ([] if start is None else [start])
    return pl.pallas_call(
        functools.partial(product_kernel, edge, slots, start is not None),
        out_shape=jax.ShapeDtypeStruct((RL * CL, edge, edge), jnp.float32),
        in_specs=[pl.BlockSpec(memory_space=pltpu.SMEM)] * 2
        + [anywhere] * 5
        + ([] if start is None else [pl.BlockSpec(memory_space=pltpu.VMEM)]),
        out_specs=pl.BlockSpec(memory_space=pltpu.VMEM),
        scratch_shapes=[
            pltpu.VMEM((2, slots * edge, edge), jnp.float32),
            pltpu.SMEM((2, PAD, edge), jnp.float32),
            pltpu.VMEM((slots_second + 1, edge, edge), jnp.float32),
            pltpu.VMEM((RL * edge, depth), jnp.bfloat16),
            pltpu.VMEM((RL * edge, depth), jnp.bfloat16),
            pltpu.VMEM((depth, CL * edge), jnp.bfloat16),
            pltpu.VMEM((depth, CL * edge), jnp.bfloat16),
            pltpu.SemaphoreType.DMA((2,)),
            pltpu.SemaphoreType.DMA((2,)),
            pltpu.SemaphoreType.DMA,
        ],
        compiler_params=pltpu.CompilerParams(vmem_limit_bytes=VMEM_LIMIT),
        cost_estimate=pl.CostEstimate(
            flops=6 * RL * depth * CL * edge * edge, bytes_accessed=4 * 1024 * 1024, transcendentals=0
        ),
    )(*operands)


def block_table(b_index, narrow, wide):
    slots_second = b_index.shape[-1]
    table = jnp.arange((KBLOCKS // narrow + 1) * CL)[:, None]
    wanted = b_index[0, 0] // narrow * CL + b_index[0, 1] // wide
    hit = (table == wanted[None, :]) & (b_index[0, 0] >= 0)[None, :]
    found = jnp.where(hit, jnp.arange(slots_second)[None, :] - slots_second, 0)
    return (slots_second + jnp.sum(found, axis=1)).astype(jnp.int32)


def local(a_blocks, a_index, b_blocks, b_index):
    narrow = lax.axis_size("narrow")
    wide = lax.axis_size("wide")
    groups = narrow // 2
    planes = wide // 2
    slots = a_blocks.shape[1]
    edge = a_blocks.shape[-1]
    row = lax.axis_index("narrow")
    column = lax.axis_index("wide")
    kind = (row // 2) ^ (column // 2 % groups)

    def permute(value, to):
        pairs = []
        for r in range(narrow):
            for c in range(wide):
                target = to(r, c)
                if target is not None:
                    pairs.append((c * narrow + r, target[1] * narrow + target[0]))
        return lax.ppermute(value, AXES, pairs)

    def swap(value):
        return permute(value, lambda r, c: (r, c ^ 1))

    second = b_blocks[0]
    second_other = permute(second, lambda r, c: (r ^ 1, c))
    index_other = permute(b_index, lambda r, c: (r ^ 1, c))

    stored = a_index[0, 0] >= 0
    line = jnp.where(stored, a_index[0, 0] // narrow, 0)
    inner = jnp.where(stored, a_index[0, 1] // narrow, KBLOCKS // narrow)
    index = jnp.stack([line, inner]).astype(jnp.float32)
    index = jnp.pad(index, ((0, PAD - 2), (0, edge - slots)))
    share = jnp.concatenate([a_blocks.reshape(slots * edge, edge), index], axis=0)

    table_own = block_table(b_index, narrow, wide)
    table_other = block_table(index_other, narrow, wide)
    pick_own = (column % 2 ^ row % 2).reshape(1)
    pick_other = 1 - pick_own

    def spread(change, step):
        def to(r, c):
            plane = c // 2
            u = plane % groups
            if (r // 2) ^ u != change:
                return None
            if change == 0 and step == 0:
                return None
            return (u * 2 + r % 2, (plane ^ step) * 2 + c % 2)
        return permute(share, to)

    def gathered(change):
        result = []
        for half in range(planes // groups):
            value = None
            for step in range(groups):
                got = share if change == 0 and step == 0 and half == 0 else spread(change, half * groups + step)
                value = got if value is None else jnp.where(kind == step, got, value)
            result.append(value)
        return result

    def window(mine, other):
        value = product(pick_own, table_own, mine, other, second)
        return product(pick_other, table_other, mine, other, second_other, value)

    moved = []
    for change in range(1, groups):
        mine = gathered(change)
        moved.append((change, mine, [swap(value) for value in mine]))
    mine = gathered(0)
    other = [swap(value) for value in mine]
    received = []
    for change, mine_moved, other_moved in moved:
        value = window(mine_moved, other_moved)
        received.append(permute(value, lambda r, c: (r ^ (change * 2), c)))
    total = window(mine, other)
    for value in received:
        total = total + value
    return total.reshape(1, RL, 1, CL, edge, edge)


def solution(mesh):
    return jax.shard_map(
        local,
        mesh=mesh,
        in_specs=(
            P("narrow", "wide", None, None),
            P("narrow", None, "wide"),
            P("narrow", "wide", None, None),
            P("narrow", None, "wide"),
        ),
        out_specs=P("narrow", None, "wide", None, None, None),
        check_vma=False,
    )
```

time: 91 us -> 75.1 us (0.83)
  starting transfers between devices: 53.2 us -> 27.5 us
  waiting for transfers between devices: 17.2 us -> 30.4 us
  Pallas kernels: 14.2 us -> 12.2 us
  local copies, waits for them, and re-layouts: 1.41 us -> 0.01 us
    ppermute x12 -> x14, starting transfers between devices: 53.2 us -> 27.5 us  [permute(): return lax.ppermute(value, AXES, pairs)]
    ppermute x12 -> x14, waiting for transfers between devices: 17.2 us -> 30.4 us  [permute(): return lax.ppermute(value, AXES, pairs)]
    pallas_call x5 -> x4, Pallas kernels: 14.2 us -> 12.2 us  [product(): pl.pallas_call(functools.partial(product_kernel, edge, slots, start is no...]
    unnamed x2 -> x4, local copies, waits for them, and re-layouts: 1.41 us -> 0.01 us
  transfers between devices with their start and end apart: 12 -> 14, of which waited for: 1 -> 4; matrix products, arithmetic and copies ran while one was open for 2% -> 2% of each run, Pallas kernels for 16% -> 16%
where the time goes in v2:
time: 75.1 us; the launch traced here: 74.8 us
  waiting for transfers between devices  30.4 us (40%)
  starting transfers between devices  27.5 us (37%)
  Pallas kernels  12.2 us (16%)
  other arithmetic  4.51 us (6%)
    ppermute x14, waiting for transfers between devices, permute(): return lax.ppermute(value, AXES, pairs)  30.4 us
    ppermute x14, starting transfers between devices, permute(): return lax.ppermute(value, AXES, pairs)  27.5 us
    pallas_call x4, Pallas kernels, product(): pl.pallas_call(functools.partial(product_kernel, edge, slots, start is no...  12.2 us
  transfers between devices with their start and end apart: 14, of which 4 were waited for; matrix products, arithmetic and copies ran while one was open for 2% of the time, Pallas kernels for 16%

profile of v2, /device:TPU:0, one launch (start us, length us, event | category | flops | bytes accessed | tf_op | source)
XLA Modules:
  0.0 74.8 jit_solution(5087442906012896790)
XLA Ops:
  0.0 0.8 %compare_select_fusion.19 = (s32[1,6]{1,0:T(1,128)S(1)}, s32[1,6]{1,0:T(1,128)S(1)}) fusion(s32[1,2,6]{2,1,0:T(2,128)} %param.5), kind=kLoop, calls=%fused_computation.39 | loop fusion | flops 198 | bytes 96 | tf_op jit(solution)/shard_map/jit(_where)/select_n | solution.py:161
  0.8 1.0 %select_maximum_fusion = f32[776,128]{1,0:T(8,128)S(1)} fusion(f32[2,6]{1,0:T(2,128)S(1)} %add_convert_fusion, f32[768,128]{1,0:T(8,128)} %bitcast.70), kind=kLoop, calls=%fused_computation | loop fusion | flops 297984 | bytes 790576 | tf_op jit(solution)/shard_map/concatenate | solution.py:165
  1.8 0.7 collective-permute-start.7
  2.5 1.3 %collective-permute-start.8 = (f32[776,128]{1,0:T(8,128)S(1)}, f32[776,128]{1,0:T(8,128)S(1)}, u32[]{:S(2)}, u32[]{:S(2)}) collective-permute-start(f32[776,128]{1,0:T(8,128)S(1)} %select_maximum_fusion), channel_id=1, source_target_pairs={{8,10},{12,14},{24,26},{28,30},{9,11},{13,15},{25,27},{29,31},{2,0... | collective-permute-start | bytes 1191944 | tf_op jit(solution)/shard_map/ppermute | solution.py:151
  3.8 1.3 %collective-permute-start.10 = (f32[776,128]{1,0:T(8,128)S(1)}, f32[776,128]{1,0:T(8,128)S(1)}, u32[]{:S(2)}, u32[]{:S(2)}) collective-permute-start(f32[776,128]{1,0:T(8,128)S(1)} %select_maximum_fusion), channel_id=1, source_target_pairs={{8,26},{12,30},{24,10},{28,14},{9,27},{13,31},{25,11},{29,15},{2,1... | collective-permute-start | bytes 1191944 | tf_op jit(solution)/shard_map/ppermute | solution.py:151
  5.1 0.7 collective-permute-start.9
  5.8 3.0 %collective-permute-start = (s32[1,2,24]{2,1,0:T(2,128)}, s32[1,2,24]{2,1,0:T(2,128)S(1)}, u32[]{:S(2)}, u32[]{:S(2)}) collective-permute-start(s32[1,2,24]{2,1,0:T(2,128)} %param.7), channel_id=1, source_target_pairs={{0,1},{4,5},{8,9},{12,13},{16,17},{20,21},{24,25},{28,29},{1,0},{5... | collective-permute-start | bytes 584 | tf_op jit(solution)/shard_map/ppermute | solution.py:151
  8.8 0.7 bitcast_compare_fusion
  9.5 0.8 %fusion.2 = s32[24]{0:T(128)S(1)} fusion(s32[1,2,24]{2,1,0:T(2,128)} %param.7), kind=kLoop, calls=%fused_computation.49 | loop fusion | flops 768 | bytes 288 | tf_op jit(solution)/shard_map/add | solution.py:127
  10.3 0.2 collective-permute-done
  10.6 2.0 %collective-permute-start.6 = (f32[24,128,128]{2,1,0:T(8,128)}, f32[24,128,128]{2,1,0:T(8,128)S(1)}, u32[]{:S(2)}, u32[]{:S(2)}) collective-permute-start(f32[24,128,128]{2,1,0:T(8,128)} %bitcast.67), channel_id=1, source_target_pairs={{0,1},{4,5},{8,9},{12,13},{16,17},{20,21},{24,25},{28,29},{1,0},{5... | collective-permute-start | bytes 4718600 | tf_op jit(solution)/shard_map/ppermute | solution.py:151
  12.6 0.1 select_reduce_fusion
  12.8 0.0 copy-start.1
  12.8 11.2 %collective-permute-start.2 = (f32[776,128]{1,0:T(8,128)S(1)}, f32[776,128]{1,0:T(8,128)S(1)}, u32[]{:S(2)}, u32[]{:S(2)}) collective-permute-start(f32[776,128]{1,0:T(8,128)S(1)} %select_maximum_fusion), channel_id=1, source_target_pairs={{0,24},{4,28},{16,8},{20,12},{1,25},{5,29},{17,9},{21,13},{10,18},... | collective-permute-start | bytes 1191944 | tf_op jit(solution)/shard_map/ppermute | solution.py:151
  24.0 2.9 %collective-permute-done.8 = f32[776,128]{1,0:T(8,128)S(1)} collective-permute-done((f32[776,128]{1,0:T(8,128)S(1)}, f32[776,128]{1,0:T(8,128)S(1)}, u32[]{:S(2)}, u32[]{:S(2)}) %collective-permute-start.8) | collective-permute-done | bytes 397344 | tf_op jit(solution)/shard_map/ppermute | solution.py:151
  26.9 4.5 %collective-permute-start.3 = (f32[776,128]{1,0:T(8,128)S(1)}, f32[776,128]{1,0:T(8,128)S(1)}, u32[]{:S(2)}, u32[]{:S(2)}) collective-permute-start(f32[776,128]{1,0:T(8,128)S(1)} %select_maximum_fusion), channel_id=1, source_target_pairs={{0,16},{4,20},{16,0},{20,4},{1,17},{5,21},{17,1},{21,5},{10,26},{1... | collective-permute-start | bytes 1191944 | tf_op jit(solution)/shard_map/ppermute | solution.py:151
  31.4 0.1 broadcast_select_fusion.1.refs_2_
  31.5 0.0 copy-start
  31.5 1.4 %collective-permute-start.1 = (f32[776,128]{1,0:T(8,128)S(1)}, f32[776,128]{1,0:T(8,128)S(1)}, u32[]{:S(2)}, u32[]{:S(2)}) collective-permute-start(f32[776,128]{1,0:T(8,128)S(1)} %select_maximum_fusion), channel_id=1, source_target_pairs={{0,8},{4,12},{16,24},{20,28},{1,9},{5,13},{17,25},{21,29},{10,2},{... | collective-permute-start | bytes 1191944 | tf_op jit(solution)/shard_map/ppermute | solution.py:151
  33.0 0.1 collective-permute-start.11
  33.1 0.6 collective-permute-start.12
  33.7 19.5 %collective-permute-done.3 = f32[776,128]{1,0:T(8,128)S(1)} collective-permute-done((f32[776,128]{1,0:T(8,128)S(1)}, f32[776,128]{1,0:T(8,128)S(1)}, u32[]{:S(2)}, u32[]{:S(2)}) %collective-permute-start.3) | collective-permute-done | bytes 397344 | tf_op jit(solution)/shard_map/ppermute | solution.py:151
  53.1 0.1 broadcast_select_fusion.2.refs_3_
  53.2 0.1 collective-permute-start.5
  53.3 0.5 collective-permute-start.4
  53.9 3.0 %shard_map.48.refs_7_ = f32[8,128,128]{2,1,0:T(8,128)S(1)} custom-call(s32[1]{0:T(128)} %bitcast.refs_0_, s32[1028]{0:T(1024)S(1)} %get-tuple-element.9.refs_1_, f32[776,128]{1,0:T(8,128)S(1)} %broadcast_select_fusion.1.refs_2_, f32[776,128]{1,0:T(8,128)S(1)} %broadcast_select_fusion.refs_3_, f32[776,128]{1,0:T(8,128)S(1)} %collective-permute-done.11.refs_4_, ...), custom_call_target="tpu_custom_call" | custom-call | flops 1207959552 | bytes 4194304 | tf_op jit(solution)/shard_map/pallas_call | solution.py:98
  56.9 3.0 %shard_map.49 = f32[8,128,128]{2,1,0:T(8,128)S(1)} custom-call(s32[1]{0:T(128)S(6)} %sub.36.refs_0_, s32[1028]{0:T(1024)S(1)} %get-tuple-element.10.refs_1_, f32[776,128]{1,0:T(8,128)S(1)} %broadcast_select_fusion.1.refs_2_, f32[776,128]{1,0:T(8,128)S(1)} %broadcast_select_fusion.refs_3_, f32[776,128]{1,0:T(8,128)S(1)} %collective-permute-done.11.refs_4_, ...), custom_call_target="tpu_custom_call" | custom-call | flops 1207959552 | bytes 4194304 | tf_op jit(solution)/shard_map/pallas_call | solution.py:98
  60.0 0.1 collective-permute-start.13
  60.1 3.0 %shard_map.46.refs_7_ = f32[8,128,128]{2,1,0:T(8,128)S(1)} custom-call(s32[1]{0:T(128)} %bitcast.refs_0_, s32[1028]{0:T(1024)S(1)} %get-tuple-element.9.refs_1_, f32[776,128]{1,0:T(8,128)S(1)} %broadcast_select_fusion.3.refs_2_, f32[776,128]{1,0:T(8,128)S(1)} %broadcast_select_fusion.2.refs_3_, f32[776,128]{1,0:T(8,128)S(1)} %collective-permute-done.4.refs_4_, ...), custom_call_target="tpu_custom_call" | custom-call | flops 1207959552 | bytes 4194304 | tf_op jit(solution)/shard_map/pallas_call | solution.py:98
  63.1 3.0 %shard_map.47 = f32[8,128,128]{2,1,0:T(8,128)S(1)} custom-call(s32[1]{0:T(128)S(6)} %sub.36.refs_0_, s32[1028]{0:T(1024)S(1)} %get-tuple-element.10.refs_1_, f32[776,128]{1,0:T(8,128)S(1)} %broadcast_select_fusion.3.refs_2_, f32[776,128]{1,0:T(8,128)S(1)} %broadcast_select_fusion.2.refs_3_, f32[776,128]{1,0:T(8,128)S(1)} %collective-permute-done.4.refs_4_, ...), custom_call_target="tpu_custom_call" | custom-call | flops 1207959552 | bytes 4194304 | tf_op jit(solution)/shard_map/pallas_call | solution.py:98
  66.2 7.7 %collective-permute-done.13 = f32[8,128,128]{2,1,0:T(8,128)S(1)} collective-permute-done((f32[8,128,128]{2,1,0:T(8,128)S(1)}, f32[8,128,128]{2,1,0:T(8,128)S(1)}, u32[]{:S(2)}, u32[]{:S(2)}) %collective-permute-start.13) | collective-permute-done | bytes 524320 | tf_op jit(solution)/shard_map/ppermute | solution.py:151
  73.9 0.9 %add.86 = f32[8,128,128]{2,1,0:T(8,128)} add(f32[8,128,128]{2,1,0:T(8,128)S(1)} %shard_map.47, f32[8,128,128]{2,1,0:T(8,128)S(1)} %collective-permute-done.13) | non-fusion elementwise | flops 131072 | bytes 1572864 | tf_op jit(solution)/shard_map/add | solution.py:209
  (19 shorter events, 0.2 us)
Async XLA Ops:
  1.8 11.0 %collective-permute-start.7 = (f32[776,128]{1,0:T(8,128)S(1)}, f32[776,128]{1,0:T(8,128)S(1)}, u32[]{:S(2)}, u32[]{:S(2)}) collective-permute-start(f32[776,128]{1,0:T(8,128)S(1)} %select_maximum_fusion), channel_id=1, source_target_pairs={{8,2},{12,6},{24,18},{28,22},{9,3},{13,7},{25,19},{29,23},{2,8},{6... | collective-permute-start | bytes 1191944 | tf_op jit(solution)/shard_map/ppermute | solution.py:151
  2.5 24.4 %collective-permute-start.8 = (f32[776,128]{1,0:T(8,128)S(1)}, f32[776,128]{1,0:T(8,128)S(1)}, u32[]{:S(2)}, u32[]{:S(2)}) collective-permute-start(f32[776,128]{1,0:T(8,128)S(1)} %select_maximum_fusion), channel_id=1, source_target_pairs={{8,10},{12,14},{24,26},{28,30},{9,11},{13,15},{25,27},{29,31},{2,0... | collective-permute-start | bytes 1191944 | tf_op jit(solution)/shard_map/ppermute | solution.py:151
  3.8 27.7 %collective-permute-start.10 = (f32[776,128]{1,0:T(8,128)S(1)}, f32[776,128]{1,0:T(8,128)S(1)}, u32[]{:S(2)}, u32[]{:S(2)}) collective-permute-start(f32[776,128]{1,0:T(8,128)S(1)} %select_maximum_fusion), channel_id=1, source_target_pairs={{8,26},{12,30},{24,10},{28,14},{9,27},{13,31},{25,11},{29,15},{2,1... | collective-permute-start | bytes 1191944 | tf_op jit(solution)/shard_map/ppermute | solution.py:151
  5.1 27.9 %collective-permute-start.9 = (f32[776,128]{1,0:T(8,128)S(1)}, f32[776,128]{1,0:T(8,128)S(1)}, u32[]{:S(2)}, u32[]{:S(2)}) collective-permute-start(f32[776,128]{1,0:T(8,128)S(1)} %select_maximum_fusion), channel_id=1, source_target_pairs={{8,18},{12,22},{24,2},{28,6},{9,19},{13,23},{25,3},{29,7},{2,24},{... | collective-permute-start | bytes 1191944 | tf_op jit(solution)/shard_map/ppermute | solution.py:151
  5.8 4.8 %collective-permute-start = (s32[1,2,24]{2,1,0:T(2,128)}, s32[1,2,24]{2,1,0:T(2,128)S(1)}, u32[]{:S(2)}, u32[]{:S(2)}) collective-permute-start(s32[1,2,24]{2,1,0:T(2,128)} %param.7), channel_id=1, source_target_pairs={{0,1},{4,5},{8,9},{12,13},{16,17},{20,21},{24,25},{28,29},{1,0},{5... | collective-permute-start | bytes 584 | tf_op jit(solution)/shard_map/ppermute | solution.py:151
  10.6 46.4 %collective-permute-start.6 = (f32[24,128,128]{2,1,0:T(8,128)}, f32[24,128,128]{2,1,0:T(8,128)S(1)}, u32[]{:S(2)}, u32[]{:S(2)}) collective-permute-start(f32[24,128,128]{2,1,0:T(8,128)} %bitcast.67), channel_id=1, source_target_pairs={{0,1},{4,5},{8,9},{12,13},{16,17},{20,21},{24,25},{28,29},{1,0},{5... | collective-permute-start | bytes 4718600 | tf_op jit(solution)/shard_map/ppermute | solution.py:151
  12.8 40.5 %copy-start.1 = (f32[1,6,128,128]{3,2,1,0:T(8,128)S(1)}, f32[1,6,128,128]{3,2,1,0:T(8,128)}, u32[]{:S(2)}) copy-start(f32[1,6,128,128]{3,2,1,0:T(8,128)} %param.4) | copy-start | bytes 1179652
  12.8 20.3 %collective-permute-start.2 = (f32[776,128]{1,0:T(8,128)S(1)}, f32[776,128]{1,0:T(8,128)S(1)}, u32[]{:S(2)}, u32[]{:S(2)}) collective-permute-start(f32[776,128]{1,0:T(8,128)S(1)} %select_maximum_fusion), channel_id=1, source_target_pairs={{0,24},{4,28},{16,8},{20,12},{1,25},{5,29},{17,9},{21,13},{10,18},... | collective-permute-start | bytes 1191944 | tf_op jit(solution)/shard_map/ppermute | solution.py:151
  26.9 26.2 %collective-permute-start.3 = (f32[776,128]{1,0:T(8,128)S(1)}, f32[776,128]{1,0:T(8,128)S(1)}, u32[]{:S(2)}, u32[]{:S(2)}) collective-permute-start(f32[776,128]{1,0:T(8,128)S(1)} %select_maximum_fusion), channel_id=1, source_target_pairs={{0,16},{4,20},{16,0},{20,4},{1,17},{5,21},{17,1},{21,5},{10,26},{1... | collective-permute-start | bytes 1191944 | tf_op jit(solution)/shard_map/ppermute | solution.py:151
  31.5 22.4 %copy-start = (f32[1,24,128,128]{3,2,1,0:T(8,128)S(1)}, f32[1,24,128,128]{3,2,1,0:T(8,128)}, u32[]{:S(2)}) copy-start(f32[1,24,128,128]{3,2,1,0:T(8,128)} %param.6) | copy-start | bytes 4718596
  31.5 21.8 %collective-permute-start.1 = (f32[776,128]{1,0:T(8,128)S(1)}, f32[776,128]{1,0:T(8,128)S(1)}, u32[]{:S(2)}, u32[]{:S(2)}) collective-permute-start(f32[776,128]{1,0:T(8,128)S(1)} %select_maximum_fusion), channel_id=1, source_target_pairs={{0,8},{4,12},{16,24},{20,28},{1,9},{5,13},{17,25},{21,29},{10,2},{... | collective-permute-start | bytes 1191944 | tf_op jit(solution)/shard_map/ppermute | solution.py:151
  33.0 20.9 %collective-permute-start.11 = (f32[776,128]{1,0:T(8,128)S(1)}, f32[776,128]{1,0:T(8,128)S(1)}, u32[]{:S(2)}, u32[]{:S(2)}) collective-permute-start(f32[776,128]{1,0:T(8,128)S(1)} %broadcast_select_fusion.1.refs_2_), channel_id=1, source_target_pairs={{0,4},{4,0},{8,12},{12,8},{16,20},{20,16},{24,28},{28,24},{1,5},{5... | collective-permute-start | bytes 1191944 | tf_op jit(solution)/shard_map/ppermute | solution.py:151
  33.1 20.8 %collective-permute-start.12 = (f32[776,128]{1,0:T(8,128)S(1)}, f32[776,128]{1,0:T(8,128)S(1)}, u32[]{:S(2)}, u32[]{:S(2)}) collective-permute-start(f32[776,128]{1,0:T(8,128)S(1)} %broadcast_select_fusion.refs_3_), channel_id=1, source_target_pairs={{0,4},{4,0},{8,12},{12,8},{16,20},{20,16},{24,28},{28,24},{1,5},{5... | collective-permute-start | bytes 1191944 | tf_op jit(solution)/shard_map/ppermute | solution.py:151
  53.2 6.9 %collective-permute-start.5 = (f32[776,128]{1,0:T(8,128)S(1)}, f32[776,128]{1,0:T(8,128)S(1)}, u32[]{:S(2)}, u32[]{:S(2)}) collective-permute-start(f32[776,128]{1,0:T(8,128)S(1)} %broadcast_select_fusion.2.refs_3_), channel_id=1, source_target_pairs={{0,4},{4,0},{8,12},{12,8},{16,20},{20,16},{24,28},{28,24},{1,5},{5... | collective-permute-start | bytes 1191944 | tf_op jit(solution)/shard_map/ppermute | solution.py:151
  53.3 6.7 %collective-permute-start.4 = (f32[776,128]{1,0:T(8,128)S(1)}, f32[776,128]{1,0:T(8,128)S(1)}, u32[]{:S(2)}, u32[]{:S(2)}) collective-permute-start(f32[776,128]{1,0:T(8,128)S(1)} %broadcast_select_fusion.3.refs_2_), channel_id=1, source_target_pairs={{0,4},{4,0},{8,12},{12,8},{16,20},{20,16},{24,28},{28,24},{1,5},{5... | collective-permute-start | bytes 1191944 | tf_op jit(solution)/shard_map/ppermute | solution.py:151
  60.0 13.9 %collective-permute-start.13 = (f32[8,128,128]{2,1,0:T(8,128)S(1)}, f32[8,128,128]{2,1,0:T(8,128)S(1)}, u32[]{:S(2)}, u32[]{:S(2)}) collective-permute-start(f32[8,128,128]{2,1,0:T(8,128)S(1)} %shard_map.49), channel_id=1, source_target_pairs={{0,2},{4,6},{8,10},{12,14},{16,18},{20,22},{24,26},{28,30},{1,3},{... | collective-permute-start | bytes 1572872 | tf_op jit(solution)/shard_map/ppermute | solution.py:151

commit v3 on v2

v3 whole, which is shorter than its diff:
```python
import functools

import jax
import jax.numpy as jnp
from jax import lax
from jax.experimental import pallas as pl
from jax.experimental.pallas import tpu as pltpu
from jax.sharding import PartitionSpec as P

RL = 2
CL = 4
KBLOCKS = 1024
PAD = 8
AXES = ("wide", "narrow")
VMEM_LIMIT = 32 * 1024 * 1024


def split(value):
    high = value.astype(jnp.bfloat16)
    low = (value - high.astype(jnp.float32)).astype(jnp.bfloat16)
    return high, low


def product_kernel(edge, slots, items, choices, *refs):
    pick_ref, tables, refs = refs[0], refs[1:3], refs[3:]
    shares = [refs[n * choices : (n + 1) * choices] for n in range(items)]
    refs = refs[items * choices :]
    (b_one, b_two, out_ref, a_ref, index_ref, b_ref, left_high, left_low, right_high, right_low,
     block_sems, index_sems, b_sems) = refs
    rows = slots * edge
    slots_second = b_one.shape[0]
    b_copies = [
        pltpu.make_async_copy(ref, b_ref.at[n, pl.ds(0, slots_second)], b_sems.at[n])
        for n, ref in enumerate((b_one, b_two))
    ]

    def copies(n, ref):
        return (
            pltpu.make_async_copy(ref.at[pl.ds(rows, PAD)], index_ref.at[n], index_sems.at[n]),
            pltpu.make_async_copy(ref.at[pl.ds(0, rows)], a_ref.at[n], block_sems.at[n]),
        )

    for n in range(items):
        for choice in range(choices):
            @pl.when(pick_ref[n] == choice)
            def _():
                for copy in copies(n, shares[n][choice]):
                    copy.start()
    for copy in b_copies:
        copy.start()
    for n in range(2):
        b_ref[n, slots_second] = jnp.zeros((edge, edge), jnp.float32)
    left_high[...] = jnp.zeros_like(left_high)
    left_low[...] = jnp.zeros_like(left_low)
    dot = functools.partial(jnp.dot, preferred_element_type=jnp.float32)
    for n in range(items):
        for copy in copies(n, shares[n][0]):
            copy.wait()
        for slot in range(slots):
            at = slot * edge
            line = index_ref[n, 0, slot].astype(jnp.int32)
            high, low = split(a_ref[n, at : at + edge, :])
            target = pl.ds(pl.multiple_of(line * edge, edge), edge)
            left_high[n, target, at : at + edge] = high
            left_low[n, target, at : at + edge] = low
        which = n // (items // 2)
        if n % (items // 2) == 0:
            b_copies[which].wait()
        for slot in range(slots):
            at = slot * edge
            inner = index_ref[n, 1, slot].astype(jnp.int32)
            for m in range(CL):
                high, low = split(b_ref[which, tables[which][inner * CL + m]])
                right_high[n, at : at + edge, m * edge : (m + 1) * edge] = high
                right_low[n, at : at + edge, m * edge : (m + 1) * edge] = low
        for m in range(0, CL, 2):
            columns = slice(m * edge, (m + 2) * edge)
            value = (
                dot(left_high[n], right_high[n, :, columns])
                + dot(left_low[n], right_high[n, :, columns])
                + dot(left_high[n], right_low[n, :, columns])
            )
            for l in range(RL):
                for k in range(2):
                    at = l * CL + m + k
                    piece = value[l * edge : (l + 1) * edge, k * edge : (k + 1) * edge]
                    out_ref[at] = piece if n == 0 else out_ref[at] + piece


def product(pick, tables, shares, seconds):
    slots_second, edge, _ = seconds[0].shape
    items = len(shares)
    choices = len(shares[0])
    slots = (shares[0][0].shape[0] - PAD) // edge
    depth = slots * edge
    anywhere = pl.BlockSpec(memory_space=pl.ANY)
    return pl.pallas_call(
        functools.partial(product_kernel, edge, slots, items, choices),
        out_shape=jax.ShapeDtypeStruct((RL * CL, edge, edge), jnp.float32),
        in_specs=[pl.BlockSpec(memory_space=pltpu.SMEM)] * 3 + [anywhere] * (items * choices + 2),
        out_specs=pl.BlockSpec(memory_space=pltpu.VMEM),
        scratch_shapes=[
            pltpu.VMEM((items, depth, edge), jnp.float32),
            pltpu.SMEM((items, PAD, edge), jnp.float32),
            pltpu.VMEM((2, slots_second + 1, edge, edge), jnp.float32),
            pltpu.VMEM((items, RL * edge, depth), jnp.bfloat16),
            pltpu.VMEM((items, RL * edge, depth), jnp.bfloat16),
            pltpu.VMEM((items, depth, CL * edge), jnp.bfloat16),
            pltpu.VMEM((items, depth, CL * edge), jnp.bfloat16),
            pltpu.SemaphoreType.DMA((items,)),
            pltpu.SemaphoreType.DMA((items,)),
            pltpu.SemaphoreType.DMA((2,)),
        ],
        compiler_params=pltpu.CompilerParams(vmem_limit_bytes=VMEM_LIMIT),
        cost_estimate=pl.CostEstimate(
            flops=6 * items * RL * depth * CL * edge * edge, bytes_accessed=6 * 1024 * 1024, transcendentals=0
        ),
    )(pick, *tables, *[ref for share in shares for ref in share], *seconds)


def block_table(b_index, narrow, wide):
    slots_second = b_index.shape[-1]
    table = jnp.arange((KBLOCKS // narrow + 1) * CL)[:, None]
    wanted = b_index[0, 0] // narrow * CL + b_index[0, 1] // wide
    hit = (table == wanted[None, :]) & (b_index[0, 0] >= 0)[None, :]
    found = jnp.where(hit, jnp.arange(slots_second)[None, :] - slots_second, 0)
    return (slots_second + jnp.sum(found, axis=1)).astype(jnp.int32)


def local(a_blocks, a_index, b_blocks, b_index):
    narrow = lax.axis_size("narrow")
    wide = lax.axis_size("wide")
    groups = narrow // 2
    planes = wide // 2
    slots = a_blocks.shape[1]
    edge = a_blocks.shape[-1]
    row = lax.axis_index("narrow")
    column = lax.axis_index("wide")
    kind = (row // 2) ^ (column // 2 % groups)

    def permute(name, value, to):
        pairs = []
        for r in range(narrow):
            for c in range(wide):
                target = to(r, c)
                if target is not None:
                    pairs.append((c * narrow + r, target[1] * narrow + target[0]))
        with jax.named_scope(name):
            return lax.ppermute(value, AXES, pairs)

    def swap(name, value):
        return permute(name, value, lambda r, c: (r, c ^ 1))

    second = b_blocks[0]
    index_other = permute("second_index", b_index, lambda r, c: (r ^ 1, c))
    second_other = permute("second", second, lambda r, c: (r ^ 1, c))

    stored = a_index[0, 0] >= 0
    line = jnp.where(stored, a_index[0, 0] // narrow, 0)
    inner = jnp.where(stored, a_index[0, 1] // narrow, KBLOCKS // narrow)
    index = jnp.stack([line, inner]).astype(jnp.float32)
    index = jnp.pad(index, ((0, PAD - 2), (0, edge - slots)))
    share = jnp.concatenate([a_blocks.reshape(slots * edge, edge), index], axis=0)
    share, index_other = lax.optimization_barrier((share, index_other))

    tables = (block_table(b_index, narrow, wide), block_table(index_other, narrow, wide))

    def spread(half, share, turn):
        def to(r, c):
            plane = c // 2
            u = plane % groups
            change = (r // 2) ^ u
            return (u * 2 + r % 2, (plane ^ change ^ turn) * 2 + c % 2)
        return permute(f"share_{half}_{turn}", share, to)

    far = permute("far", share, lambda r, c: (r, (c // 2 ^ groups) * 2 + c % 2))
    turns = [[spread(half, value, turn) for turn in range(groups)] for half, value in enumerate((share, far))]
    swapped = [[swap(f"swap_{half}", value) for value in values] for half, values in enumerate(turns)]
    candidates = [[ref for pair in zip(*values) for ref in pair] for values in zip(turns, swapped)]
    crossed = (column ^ row) % 2

    def window(change):
        at = (kind ^ change) * 2
        pick = jnp.stack([at + crossed, at + crossed, at + 1 - crossed, at + 1 - crossed])
        return product(pick, tables, candidates * 2, (second, second_other))

    received = []
    for change in range(1, groups):
        value = window(change)
        received.append(permute(f"window_{change}", value, lambda r, c: (r ^ (change * 2), c)))
    total = window(0)
    for value in received:
        total = total + value
    return total.reshape(1, RL, 1, CL, edge, edge)


def solution(mesh):
    return jax.shard_map(
        local,
        mesh=mesh,
        in_specs=(
            P("narrow", "wide", None, None),
            P("narrow", None, "wide"),
            P("narrow", "wide", None, None),
            P("narrow", None, "wide"),
        ),
        out_specs=P("narrow", None, "wide", None, None, None),
        check_vma=False,
    )
```

time: 75.1 us -> 64.6 us (0.86)
  starting transfers between devices: 27.5 us -> 13.3 us
  local copies, waits for them, and re-layouts: 0.01 us -> 2.82 us
  other arithmetic: 4.51 us -> 5.48 us
  Pallas kernels: 12.2 us -> 11.3 us
    ppermute x14 -> x12, starting transfers between devices: 27.5 us -> 13.3 us  [permute(): return lax.ppermute(value, AXES, pairs)]
    unnamed x4, local copies, waits for them, and re-layouts: 0.01 us -> 2.82 us
    add x1, other arithmetic: 0.86 us -> 1.91 us  [local(): total = total + value]
    pallas_call x4 -> x2, Pallas kernels: 12.2 us -> 11.3 us  [product(): pl.pallas_call(functools.partial(product_kernel, edge, slots, items, choi...]
    ppermute x14 -> x12, waiting for transfers between devices: 30.4 us -> 30.6 us  [permute(): return lax.ppermute(value, AXES, pairs)]
  transfers between devices with their start and end apart: 14 -> 12, of which waited for: 4 -> 6; matrix products, arithmetic and copies ran while one was open for 2% -> 6% of each run, Pallas kernels for 16% -> 8%
where the time goes in v3:
time: 64.6 us; the launch traced here: 63.6 us
  waiting for transfers between devices  30.6 us (47%)
  starting transfers between devices  13.3 us (21%)
  Pallas kernels  11.3 us (17%)
  other arithmetic  5.48 us (8%)
  local copies, waits for them, and re-layouts  2.82 us (4%)
    ppermute x12, waiting for transfers between devices, permute(): return lax.ppermute(value, AXES, pairs)  30.6 us
    ppermute x12, starting transfers between devices, permute(): return lax.ppermute(value, AXES, pairs)  13.3 us
    pallas_call x2, Pallas kernels, product(): pl.pallas_call(functools.partial(product_kernel, edge, slots, items, choi...  11.3 us
    unnamed x4, local copies, waits for them, and re-layouts  2.82 us
    add x1, other arithmetic, local(): total = total + value  1.91 us
  transfers between devices with their start and end apart: 12, of which 6 were waited for; matrix products, arithmetic and copies ran while one was open for 6% of the time, Pallas kernels for 8%

profile of v3, /device:TPU:0, one launch (start us, length us, event | category | flops | bytes accessed | tf_op | source)
XLA Modules:
  0.0 63.6 jit_solution(11763940485870235543)
XLA Ops:
  0.0 2.9 %collective-permute-start = (s32[1,2,24]{2,1,0:T(2,128)}, s32[1,2,24]{2,1,0:T(2,128)S(1)}, u32[]{:S(2)}, u32[]{:S(2)}) collective-permute-start(s32[1,2,24]{2,1,0:T(2,128)} %param.7), channel_id=1, source_target_pairs={{0,1},{4,5},{8,9},{12,13},{16,17},{20,21},{24,25},{28,29},{1,0},{5... | collective-permute-start | bytes 584 | tf_op jit(solution)/shard_map/second_index/ppermute | solution.py:149
  2.9 0.0 collective-permute-start.10
  3.0 0.8 %compare_select_fusion.19 = (s32[1,6]{1,0:T(1,128)S(1)}, s32[1,6]{1,0:T(1,128)S(1)}) fusion(s32[1,2,6]{2,1,0:T(2,128)} %param.5), kind=kLoop, calls=%fused_computation.35 | loop fusion | flops 198 | bytes 96 | tf_op jit(solution)/shard_map/jit(_where)/select_n | solution.py:159
  3.8 1.0 %select_maximum_fusion = f32[776,128]{1,0:T(8,128)S(1)} fusion(f32[2,6]{1,0:T(2,128)S(1)} %add_convert_fusion, f32[768,128]{1,0:T(8,128)} %bitcast.73), kind=kLoop, calls=%fused_computation | loop fusion | flops 297984 | bytes 790576 | tf_op jit(solution)/shard_map/concatenate | solution.py:163
  4.8 0.0 collective-permute-done
  4.8 3.2 %collective-permute-start.5 = (f32[776,128]{1,0:T(8,128)S(1)}, f32[776,128]{1,0:T(8,128)S(1)}, u32[]{:S(2)}, u32[]{:S(2)}) collective-permute-start(f32[776,128]{1,0:T(8,128)S(1)} %select_maximum_fusion), channel_id=1, source_target_pairs={{0,16},{4,20},{8,24},{12,28},{16,0},{20,4},{24,8},{28,12},{1,17},{... | collective-permute-start | bytes 1191944 | tf_op jit(solution)/shard_map/far/ppermute | solution.py:149
  8.0 0.1 pad_add_fusion.1.refs_0_
  8.0 0.7 %bitcast_compare_fusion.1 = pred[24]{0:T(512)(128)(4,1)S(1)} fusion(s32[1,2,24]{2,1,0:T(2,128)} %param.7), kind=kLoop, calls=%fused_computation.45 | loop fusion | flops 24 | bytes 120 | tf_op jit(solution)/shard_map/ge | solution.py:125
  8.7 1.6 %collective-permute-start.3 = (f32[776,128]{1,0:T(8,128)S(1)}, f32[776,128]{1,0:T(8,128)S(1)}, u32[]{:S(2)}, u32[]{:S(2)}) collective-permute-start(f32[776,128]{1,0:T(8,128)S(1)} %select_maximum_fusion), channel_id=1, source_target_pairs={{0,8},{4,12},{8,10},{12,14},{16,24},{20,28},{24,26},{28,30},{1,9},... | collective-permute-start | bytes 1191944 | tf_op jit(solution)/shard_map/share_0_1/ppermute | solution.py:149
  10.3 0.7 %collective-permute-start.1 = (f32[776,128]{1,0:T(8,128)S(1)}, f32[776,128]{1,0:T(8,128)S(1)}, u32[]{:S(2)}, u32[]{:S(2)}) collective-permute-start(f32[776,128]{1,0:T(8,128)S(1)} %select_maximum_fusion), channel_id=1, source_target_pairs={{0,0},{4,4},{8,2},{12,6},{16,16},{20,20},{24,18},{28,22},{1,1},{5,... | collective-permute-start | bytes 1191944 | tf_op jit(solution)/shard_map/share_0_0/ppermute | solution.py:149
  11.0 14.2 %collective-permute-done.5 = f32[776,128]{1,0:T(8,128)S(1)} collective-permute-done((f32[776,128]{1,0:T(8,128)S(1)}, f32[776,128]{1,0:T(8,128)S(1)}, u32[]{:S(2)}, u32[]{:S(2)}) %collective-permute-start.5) | collective-permute-done | bytes 397344 | tf_op jit(solution)/shard_map/far/ppermute | solution.py:149
  25.2 0.6 collective-permute-start.8
  25.8 0.7 %collective-permute-start.6 = (f32[776,128]{1,0:T(8,128)S(1)}, f32[776,128]{1,0:T(8,128)S(1)}, u32[]{:S(2)}, u32[]{:S(2)}) collective-permute-start(f32[776,128]{1,0:T(8,128)S(1)} %collective-permute-done.5), channel_id=1, source_target_pairs={{0,0},{4,4},{8,2},{12,6},{16,16},{20,20},{24,18},{28,22},{1,1},{5,... | collective-permute-start | bytes 1191944 | tf_op jit(solution)/shard_map/share_1_0/ppermute | solution.py:149
  26.5 0.8 %fusion.3 = s32[24]{0:T(128)S(1)} fusion(s32[1,2,24]{2,1,0:T(2,128)} %param.7), kind=kLoop, calls=%fused_computation.49 | loop fusion | flops 768 | bytes 288 | tf_op jit(solution)/shard_map/add | solution.py:124
  27.3 0.0 collective-permute-done.3.refs_5_.refs_13_
  27.3 0.1 collective-permute-start.4
  27.4 0.5 collective-permute-start.2
  27.9 7.3 %collective-permute-done.8.refs_9_.refs_17_ = f32[776,128]{1,0:T(8,128)S(1)} collective-permute-done((f32[776,128]{1,0:T(8,128)S(1)}, f32[776,128]{1,0:T(8,128)S(1)}, u32[]{:S(2)}, u32[]{:S(2)}) %collective-permute-start.8) | collective-permute-done | bytes 397344 | tf_op jit(solution)/shard_map/share_1_1/ppermute | solution.py:149
  35.2 0.5 collective-permute-start.7
  35.7 0.1 select_reduce_fusion
  35.9 0.0 collective-permute-done.4.refs_6_.refs_14_
  35.9 1.0 %collective-permute-done.9.refs_10_.refs_18_ = f32[776,128]{1,0:T(8,128)S(1)} collective-permute-done((f32[776,128]{1,0:T(8,128)S(1)}, f32[776,128]{1,0:T(8,128)S(1)}, u32[]{:S(2)}, u32[]{:S(2)}) %collective-permute-start.9) | collective-permute-done | bytes 397344 | tf_op jit(solution)/shard_map/swap_1/ppermute | solution.py:149
  36.9 0.6 collective-permute-done.7.refs_8_.refs_16_
  37.5 1.6 %collective-permute-done.10.refs_20_ = f32[24,128,128]{2,1,0:T(8,128)} collective-permute-done((f32[24,128,128]{2,1,0:T(8,128)}, f32[24,128,128]{2,1,0:T(8,128)}, u32[]{:S(2)}, u32[]{:S(2)}) %collective-permute-start.10) | collective-permute-done | bytes 1572896 | tf_op jit(solution)/shard_map/second/ppermute | solution.py:149
  39.1 1.4 %copy-done = f32[1,24,128,128]{3,2,1,0:T(8,128)S(1)} copy-done((f32[1,24,128,128]{3,2,1,0:T(8,128)S(1)}, f32[1,24,128,128]{3,2,1,0:T(8,128)}, u32[]{:S(2)}) %copy-start) | copy-done | bytes 1572888
  40.5 6.0 %shard_map.47 = f32[8,128,128]{2,1,0:T(8,128)} custom-call(s32[4]{0:T(128)S(1)} %pad_add_fusion.1.refs_0_, s32[1028]{0:T(1024)S(1)} %get-tuple-element.14.refs_1_, s32[1028]{0:T(1024)S(1)} %get-tuple-element.13.refs_2_, f32[776,128]{1,0:T(8,128)S(1)} %collective-permute-done.1.refs_3_.refs_11_, f32[776,128]{1,0:T(8,128)S(1)} %collective-permute-done.2.refs_4_.refs_12_, ...), custom_call_target="tpu_custom_call" | custom-call | flops 2415919104 | bytes 6291456 | tf_op jit(solution)/shard_map/pallas_call | solution.py:97
  46.6 2.6 %collective-permute-start.11 = (f32[8,128,128]{2,1,0:T(8,128)}, f32[8,128,128]{2,1,0:T(8,128)}, u32[]{:S(2)}, u32[]{:S(2)}) collective-permute-start(f32[8,128,128]{2,1,0:T(8,128)} %shard_map.47), channel_id=1, source_target_pairs={{0,2},{4,6},{8,10},{12,14},{16,18},{20,22},{24,26},{28,30},{1,3},{... | collective-permute-start | bytes 1572872 | tf_op jit(solution)/shard_map/window_1/ppermute | solution.py:149
  49.1 0.1 pad_add_fusion.refs_0_
  49.2 1.4 %copy-done.1 = f32[1,24,128,128]{3,2,1,0:T(8,128)S(1)} copy-done((f32[1,24,128,128]{3,2,1,0:T(8,128)S(1)}, f32[1,24,128,128]{3,2,1,0:T(8,128)}, u32[]{:S(2)}) %copy-start.1) | copy-done | bytes 1572888
  50.6 5.2 %shard_map.46 = f32[8,128,128]{2,1,0:T(8,128)S(1)} custom-call(s32[4]{0:T(128)S(1)} %pad_add_fusion.refs_0_, s32[1028]{0:T(1024)S(1)} %get-tuple-element.14.refs_1_, s32[1028]{0:T(1024)S(1)} %get-tuple-element.13.refs_2_, f32[776,128]{1,0:T(8,128)S(1)} %collective-permute-done.1.refs_3_.refs_11_, f32[776,128]{1,0:T(8,128)S(1)} %collective-permute-done.2.refs_4_.refs_12_, ...), custom_call_target="tpu_custom_call" | custom-call | flops 2415919104 | bytes 6291456 | tf_op jit(solution)/shard_map/pallas_call | solution.py:97
  55.8 5.8 %collective-permute-done.11 = f32[8,128,128]{2,1,0:T(8,128)} collective-permute-done((f32[8,128,128]{2,1,0:T(8,128)}, f32[8,128,128]{2,1,0:T(8,128)}, u32[]{:S(2)}, u32[]{:S(2)}) %collective-permute-start.11) | collective-permute-done | bytes 524320 | tf_op jit(solution)/shard_map/window_1/ppermute | solution.py:149
  61.7 1.9 %add.102 = f32[8,128,128]{2,1,0:T(8,128)} add(f32[8,128,128]{2,1,0:T(8,128)S(1)} %shard_map.46, f32[8,128,128]{2,1,0:T(8,128)} %collective-permute-done.11) | non-fusion elementwise | flops 131072 | bytes 1572864 | tf_op jit(solution)/shard_map/add | solution.py:193
  (11 shorter events, 0.0 us)
Async XLA Ops:
  0.0 4.8 %collective-permute-start = (s32[1,2,24]{2,1,0:T(2,128)}, s32[1,2,24]{2,1,0:T(2,128)S(1)}, u32[]{:S(2)}, u32[]{:S(2)}) collective-permute-start(s32[1,2,24]{2,1,0:T(2,128)} %param.7), channel_id=1, source_target_pairs={{0,1},{4,5},{8,9},{12,13},{16,17},{20,21},{24,25},{28,29},{1,0},{5... | collective-permute-start | bytes 584 | tf_op jit(solution)/shard_map/second_index/ppermute | solution.py:149
  2.9 36.2 %collective-permute-start.10 = (f32[24,128,128]{2,1,0:T(8,128)}, f32[24,128,128]{2,1,0:T(8,128)}, u32[]{:S(2)}, u32[]{:S(2)}) collective-permute-start(f32[24,128,128]{2,1,0:T(8,128)} %bitcast.70), channel_id=1, source_target_pairs={{0,1},{4,5},{8,9},{12,13},{16,17},{20,21},{24,25},{28,29},{1,0},{5... | collective-permute-start | bytes 4718600 | tf_op jit(solution)/shard_map/second/ppermute | solution.py:149
  4.8 20.4 %collective-permute-start.5 = (f32[776,128]{1,0:T(8,128)S(1)}, f32[776,128]{1,0:T(8,128)S(1)}, u32[]{:S(2)}, u32[]{:S(2)}) collective-permute-start(f32[776,128]{1,0:T(8,128)S(1)} %select_maximum_fusion), channel_id=1, source_target_pairs={{0,16},{4,20},{8,24},{12,28},{16,0},{20,4},{24,8},{28,12},{1,17},{... | collective-permute-start | bytes 1191944 | tf_op jit(solution)/shard_map/far/ppermute | solution.py:149
  8.7 18.6 %collective-permute-start.3 = (f32[776,128]{1,0:T(8,128)S(1)}, f32[776,128]{1,0:T(8,128)S(1)}, u32[]{:S(2)}, u32[]{:S(2)}) collective-permute-start(f32[776,128]{1,0:T(8,128)S(1)} %select_maximum_fusion), channel_id=1, source_target_pairs={{0,8},{4,12},{8,10},{12,14},{16,24},{20,28},{24,26},{28,30},{1,9},... | collective-permute-start | bytes 1191944 | tf_op jit(solution)/shard_map/share_0_1/ppermute | solution.py:149
  10.3 17.1 %collective-permute-start.1 = (f32[776,128]{1,0:T(8,128)S(1)}, f32[776,128]{1,0:T(8,128)S(1)}, u32[]{:S(2)}, u32[]{:S(2)}) collective-permute-start(f32[776,128]{1,0:T(8,128)S(1)} %select_maximum_fusion), channel_id=1, source_target_pairs={{0,0},{4,4},{8,2},{12,6},{16,16},{20,20},{24,18},{28,22},{1,1},{5,... | collective-permute-start | bytes 1191944 | tf_op jit(solution)/shard_map/share_0_0/ppermute | solution.py:149
  25.2 9.9 %collective-permute-start.8 = (f32[776,128]{1,0:T(8,128)S(1)}, f32[776,128]{1,0:T(8,128)S(1)}, u32[]{:S(2)}, u32[]{:S(2)}) collective-permute-start(f32[776,128]{1,0:T(8,128)S(1)} %collective-permute-done.5), channel_id=1, source_target_pairs={{0,8},{4,12},{8,10},{12,14},{16,24},{20,28},{24,26},{28,30},{1,9},... | collective-permute-start | bytes 1191944 | tf_op jit(solution)/shard_map/share_1_1/ppermute | solution.py:149
  25.8 9.3 %collective-permute-start.6 = (f32[776,128]{1,0:T(8,128)S(1)}, f32[776,128]{1,0:T(8,128)S(1)}, u32[]{:S(2)}, u32[]{:S(2)}) collective-permute-start(f32[776,128]{1,0:T(8,128)S(1)} %collective-permute-done.5), channel_id=1, source_target_pairs={{0,0},{4,4},{8,2},{12,6},{16,16},{20,20},{24,18},{28,22},{1,1},{5,... | collective-permute-start | bytes 1191944 | tf_op jit(solution)/shard_map/share_1_0/ppermute | solution.py:149
  27.3 8.5 %collective-permute-start.4 = (f32[776,128]{1,0:T(8,128)S(1)}, f32[776,128]{1,0:T(8,128)S(1)}, u32[]{:S(2)}, u32[]{:S(2)}) collective-permute-start(f32[776,128]{1,0:T(8,128)S(1)} %collective-permute-done.3.refs_5_.refs_13_), channel_id=1, source_target_pairs={{0,4},{4,0},{8,12},{12,8},{16,20},{20,16},{24,28},{28,24},{1,5},{5... | collective-permute-start | bytes 1191944 | tf_op jit(solution)/shard_map/swap_0/ppermute | solution.py:149
  27.4 8.4 %collective-permute-start.2 = (f32[776,128]{1,0:T(8,128)S(1)}, f32[776,128]{1,0:T(8,128)S(1)}, u32[]{:S(2)}, u32[]{:S(2)}) collective-permute-start(f32[776,128]{1,0:T(8,128)S(1)} %collective-permute-done.1.refs_3_.refs_11_), channel_id=1, source_target_pairs={{0,4},{4,0},{8,12},{12,8},{16,20},{20,16},{24,28},{28,24},{1,5},{5... | collective-permute-start | bytes 1191944 | tf_op jit(solution)/shard_map/swap_0/ppermute | solution.py:149
  35.2 1.7 %collective-permute-start.9 = (f32[776,128]{1,0:T(8,128)S(1)}, f32[776,128]{1,0:T(8,128)S(1)}, u32[]{:S(2)}, u32[]{:S(2)}) collective-permute-start(f32[776,128]{1,0:T(8,128)S(1)} %collective-permute-done.8.refs_9_.refs_17_), channel_id=1, source_target_pairs={{0,4},{4,0},{8,12},{12,8},{16,20},{20,16},{24,28},{28,24},{1,5},{5... | collective-permute-start | bytes 1191944 | tf_op jit(solution)/shard_map/swap_1/ppermute | solution.py:149
  35.2 2.3 %collective-permute-start.7 = (f32[776,128]{1,0:T(8,128)S(1)}, f32[776,128]{1,0:T(8,128)S(1)}, u32[]{:S(2)}, u32[]{:S(2)}) collective-permute-start(f32[776,128]{1,0:T(8,128)S(1)} %collective-permute-done.6.refs_7_.refs_15_), channel_id=1, source_target_pairs={{0,4},{4,0},{8,12},{12,8},{16,20},{20,16},{24,28},{28,24},{1,5},{5... | collective-permute-start | bytes 1191944 | tf_op jit(solution)/shard_map/swap_1/ppermute | solution.py:149
  39.1 1.4 %copy-start = (f32[1,24,128,128]{3,2,1,0:T(8,128)S(1)}, f32[1,24,128,128]{3,2,1,0:T(8,128)}, u32[]{:S(2)}) copy-start(f32[1,24,128,128]{3,2,1,0:T(8,128)} %param.6) | copy-start | bytes 4718596
  46.6 15.1 %collective-permute-start.11 = (f32[8,128,128]{2,1,0:T(8,128)}, f32[8,128,128]{2,1,0:T(8,128)}, u32[]{:S(2)}, u32[]{:S(2)}) collective-permute-start(f32[8,128,128]{2,1,0:T(8,128)} %shard_map.47), channel_id=1, source_target_pairs={{0,2},{4,6},{8,10},{12,14},{16,18},{20,22},{24,26},{28,30},{1,3},{... | collective-permute-start | bytes 1572872 | tf_op jit(solution)/shard_map/window_1/ppermute | solution.py:149
  49.2 1.4 %copy-start.1 = (f32[1,24,128,128]{3,2,1,0:T(8,128)S(1)}, f32[1,24,128,128]{3,2,1,0:T(8,128)}, u32[]{:S(2)}) copy-start(f32[1,24,128,128]{3,2,1,0:T(8,128)} %param.6) | copy-start | bytes 4718596

commit v4 on v3

v4 whole, which is shorter than its diff:
```python
import functools

import jax
import jax.numpy as jnp
from jax import lax
from jax.experimental import pallas as pl
from jax.experimental.pallas import tpu as pltpu
from jax.sharding import PartitionSpec as P

RL = 2
CL = 4
KBLOCKS = 1024
PAD = 8
AXES = ("wide", "narrow")
VMEM_LIMIT = 16 * 1024 * 1024


def split(value):
    high = value.astype(jnp.bfloat16)
    low = (value - high.astype(jnp.float32)).astype(jnp.bfloat16)
    return high, low


def product_kernel(edge, slots, narrow, change, crossing, items, choices, has_start, *refs):
    table_ref, refs = refs[0], refs[1:]
    row, column = lax.axis_index("narrow"), lax.axis_index("wide")
    turn = (row // 2) ^ (column // 2 % (choices // 2)) ^ change
    pick = turn * 2 + ((row ^ column) % 2 ^ crossing)
    shares = [refs[n * choices : (n + 1) * choices] for n in range(items)]
    refs = refs[items * choices :]
    b_ref, refs = refs[0], refs[1:]
    if has_start:
        start_ref, refs = refs[0], refs[1:]
    out_ref, a_ref, index_ref, left_high, left_low, right_high, right_low, block_sems, index_sems = refs
    rows = slots * edge
    last = b_ref.shape[0] - 1

    def copies(n, ref):
        return (
            pltpu.make_async_copy(ref.at[pl.ds(rows, PAD)], index_ref.at[n], index_sems.at[n]),
            pltpu.make_async_copy(ref.at[pl.ds(0, rows)], a_ref.at[n], block_sems.at[n]),
        )

    for n in range(items):
        for choice in range(choices):
            @pl.when(pick == choice)
            def _():
                for copy in copies(n, shares[n][choice]):
                    copy.start()
    left_high[...] = jnp.zeros_like(left_high)
    left_low[...] = jnp.zeros_like(left_low)
    waits = [copies(n, shares[n][0]) for n in range(items)]
    for index_copy, _ in waits:
        index_copy.wait()
    for n in range(items):
        for slot in range(slots):
            at = (n * slots + slot) * edge
            inner = index_ref[n, 1, slot].astype(jnp.int32)
            inner = jnp.where(inner < 0, KBLOCKS // narrow, lax.div(jnp.maximum(inner, 0), narrow))
            for m in range(CL):
                block = table_ref[inner * CL + m]
                high, low = split(jnp.where(block <= last, b_ref[jnp.minimum(block, last)], 0.0))
                right_high[at : at + edge, m * edge : (m + 1) * edge] = high
                right_low[at : at + edge, m * edge : (m + 1) * edge] = low
    for _, block_copy in waits:
        block_copy.wait()
    for n in range(items):
        for slot in range(slots):
            at = (n * slots + slot) * edge
            line = lax.div(jnp.maximum(index_ref[n, 0, slot].astype(jnp.int32), 0), narrow)
            high, low = split(a_ref[n, slot * edge : (slot + 1) * edge, :])
            target = pl.ds(pl.multiple_of(line * edge, edge), edge)
            left_high[target, at : at + edge] = high
            left_low[target, at : at + edge] = low
    dot = functools.partial(jnp.dot, preferred_element_type=jnp.float32)
    for m in range(0, CL, 2):
        columns = slice(m * edge, (m + 2) * edge)
        value = (
            dot(left_high[...], right_high[:, columns])
            + dot(left_low[...], right_high[:, columns])
            + dot(left_high[...], right_low[:, columns])
        )
        for l in range(RL):
            for k in range(2):
                at = l * CL + m + k
                piece = value[l * edge : (l + 1) * edge, k * edge : (k + 1) * edge]
                out_ref[at] = start_ref[at] + piece if has_start else piece


def product(narrow, change, crossing, table, shares, second, start=None):
    edge = second.shape[1]
    items = len(shares)
    choices = len(shares[0])
    slots = (shares[0][0].shape[0] - PAD) // edge
    depth = items * slots * edge
    scalars = pl.BlockSpec(memory_space=pltpu.SMEM)
    anywhere = pl.BlockSpec(memory_space=pl.ANY)
    whole = pl.BlockSpec(memory_space=pltpu.VMEM)
    starts = [] if start is None else [start]
    return pl.pallas_call(
        functools.partial(product_kernel, edge, slots, narrow, change, crossing, items, choices, start is not None),
        out_shape=jax.ShapeDtypeStruct((RL * CL, edge, edge), jnp.float32),
        in_specs=[scalars] + [anywhere] * (items * choices) + [whole] * (1 + len(starts)),
        out_specs=whole,
        scratch_shapes=[
            pltpu.VMEM((items, slots * edge, edge), jnp.float32),
            pltpu.SMEM((items, PAD, edge), jnp.float32),
            pltpu.VMEM((RL * edge, depth), jnp.bfloat16),
            pltpu.VMEM((RL * edge, depth), jnp.bfloat16),
            pltpu.VMEM((depth, CL * edge), jnp.bfloat16),
            pltpu.VMEM((depth, CL * edge), jnp.bfloat16),
            pltpu.SemaphoreType.DMA((items,)),
            pltpu.SemaphoreType.DMA((items,)),
        ],
        compiler_params=pltpu.CompilerParams(vmem_limit_bytes=VMEM_LIMIT),
        cost_estimate=pl.CostEstimate(
            flops=6 * RL * depth * CL * edge * edge, bytes_accessed=4 * 1024 * 1024, transcendentals=0
        ),
    )(table, *[ref for share in shares for ref in share], second, *starts)


def share_kernel(a_hbm, index_hbm, out_hbm, tile_ref, index_ref, block_sem, tile_sem, index_sem):
    slots, edge, _ = a_hbm.shape
    copies = [
        pltpu.make_async_copy(a_hbm.at[slot], out_hbm.at[pl.ds(slot * edge, edge)], block_sem.at[slot])
        for slot in range(slots)
    ]
    index_copy = pltpu.make_async_copy(index_hbm, index_ref, index_sem)
    index_copy.start()
    for copy in copies:
        copy.start()
    index_copy.wait()
    shape = tile_ref.shape
    row = lax.broadcasted_iota(jnp.int32, shape, 0)
    column = lax.broadcasted_iota(jnp.int32, shape, 1)
    tile = jnp.zeros(shape, jnp.float32)
    for n in range(2):
        for slot in range(slots):
            tile = jnp.where((row == n) & (column == slot), index_ref[0, n, slot].astype(jnp.float32), tile)
    tile_ref[...] = tile
    tile_copy = pltpu.make_async_copy(tile_ref, out_hbm.at[pl.ds(slots * edge, shape[0])], tile_sem)
    tile_copy.start()
    for copy in copies:
        copy.wait()
    tile_copy.wait()


def build_share(a_blocks, a_index):
    slots, edge, _ = a_blocks.shape
    return pl.pallas_call(
        share_kernel,
        out_shape=jax.ShapeDtypeStruct((slots * edge + PAD, edge), jnp.float32),
        in_specs=[pl.BlockSpec(memory_space=pl.ANY)] * 2,
        out_specs=pl.BlockSpec(memory_space=pl.ANY),
        scratch_shapes=[
            pltpu.VMEM((PAD, edge), jnp.float32),
            pltpu.SMEM(a_index.shape, jnp.int32),
            pltpu.SemaphoreType.DMA((slots,)),
            pltpu.SemaphoreType.DMA,
            pltpu.SemaphoreType.DMA,
        ],
        compiler_params=pltpu.CompilerParams(vmem_limit_bytes=1024 * 1024),
    )(pltpu.with_memory_space_constraint(a_blocks, pltpu.HBM), pltpu.with_memory_space_constraint(a_index, pltpu.HBM))


def block_table(b_index, narrow, wide):
    slots_second = b_index.shape[-1]
    table = jnp.arange((KBLOCKS // narrow + 1) * CL)[:, None]
    wanted = b_index[0, 0] // narrow * CL + b_index[0, 1] // wide
    hit = (table == wanted[None, :]) & (b_index[0, 0] >= 0)[None, :]
    found = jnp.where(hit, jnp.arange(slots_second)[None, :] - slots_second, 0)
    return (slots_second + jnp.sum(found, axis=1)).astype(jnp.int32)


def local(a_blocks, a_index, b_blocks, b_index):
    narrow = lax.axis_size("narrow")
    wide = lax.axis_size("wide")
    groups = narrow // 2
    planes = wide // 2
    slots = a_blocks.shape[1]
    edge = a_blocks.shape[-1]

    def permute(name, value, to):
        pairs = []
        for r in range(narrow):
            for c in range(wide):
                target = to(r, c)
                if target is not None:
                    pairs.append((c * narrow + r, target[1] * narrow + target[0]))
        with jax.named_scope(name):
            return lax.ppermute(value, AXES, pairs)

    def swap(name, value):
        return permute(name, value, lambda r, c: (r, c ^ 1))

    second = b_blocks[0]
    second_other = permute("second", second, lambda r, c: (r ^ 1, c))

    share = build_share(a_blocks[0], a_index)
    table = block_table(b_index, narrow, wide)
    tables = (table, permute("second_table", table, lambda r, c: (r ^ 1, c)))

    def spread(half, share, turn):
        def to(r, c):
            plane = c // 2
            u = plane % groups
            change = (r // 2) ^ u
            return (u * 2 + r % 2, (plane ^ change ^ turn) * 2 + c % 2)
        return permute(f"share_{half}_{turn}", share, to)

    far = permute("far", share, lambda r, c: (r, (c // 2 ^ groups) * 2 + c % 2))
    turns = [[spread(half, value, turn) for turn in range(groups)] for half, value in enumerate((share, far))]
    swapped = [[swap(f"swap_{half}", value) for value in values] for half, values in enumerate(turns)]
    candidates = [[ref for pair in zip(*values) for ref in pair] for values in zip(turns, swapped)]
    def window(change):
        value = product(narrow, change, 0, tables[0], candidates, second)
        return product(narrow, change, 1, tables[1], candidates, second_other, value)

    received = []
    for change in range(1, groups):
        value = window(change)
        received.append(permute(f"window_{change}", value, lambda r, c: (r ^ (change * 2), c)))
    total = window(0)
    for value in received:
        total = total + value
    return total.reshape(1, RL, 1, CL, edge, edge)


def solution(mesh):
    return jax.shard_map(
        local,
        mesh=mesh,
        in_specs=(
            P("narrow", "wide", None, None),
            P("narrow", None, "wide"),
            P("narrow", "wide", None, None),
            P("narrow", None, "wide"),
        ),
        out_specs=P("narrow", None, "wide", None, None, None),
        check_vma=False,
    )
```

time: 64.6 us -> 63.1 us (0.977)
  Pallas kernels: 11.3 us -> 15 us
  other arithmetic: 5.48 us -> 2.42 us
  waiting for transfers between devices: 30.6 us -> 28.4 us
  starting transfers between devices: 13.3 us -> 14.8 us
  local copies, waits for them, and re-layouts: 2.82 us -> 1.41 us
    pallas_call x2 -> x5, Pallas kernels: 11.3 us -> 15 us  [the longest x4 14 us: product(): pl.pallas_call(functools.partial(product_kernel, edge, slots, narrow, cha...]
    ppermute x12, waiting for transfers between devices: 30.6 us -> 28.4 us  [permute(): return lax.ppermute(value, AXES, pairs)]
    ppermute x12, starting transfers between devices: 13.3 us -> 14.8 us  [permute(): return lax.ppermute(value, AXES, pairs)]
    unnamed x4, local copies, waits for them, and re-layouts: 2.82 us -> 1.41 us
    add x1, other arithmetic: 1.91 us -> 0.87 us  [local(): total = total + value]
    concatenate x1 -> x0, other arithmetic: 1.03 us -> none  [local(): jnp.concatenate([a_blocks.reshape(slots * edge, edge), index], axis=0)]
    add x2 -> x0, other arithmetic: 0.78 us -> none  [block_table(): wanted = b_index[0, 0] // narrow * CL + b_index[0, 1] // wide]
    sub x1, other arithmetic: 0.01 us -> 0.77 us  [block_table(): found = jnp.where(hit, jnp.arange(slots_second)[None, :] - slots_second, 0)]
  transfers between devices with their start and end apart: 12 -> 12, of which waited for: 6 -> 4; matrix products, arithmetic and copies ran while one was open for 6% -> 3% of each run, Pallas kernels for 8% -> 19%
where the time goes in v4:
time: 63.1 us; the launch traced here: 62.2 us
  waiting for transfers between devices  28.4 us (45%)
  Pallas kernels  15 us (24%)
  starting transfers between devices  14.8 us (23%)
  other arithmetic  2.42 us (4%)
  local copies, waits for them, and re-layouts  1.41 us (2%)
    ppermute x12, waiting for transfers between devices, permute(): return lax.ppermute(value, AXES, pairs)  28.4 us
    ppermute x12, starting transfers between devices, permute(): return lax.ppermute(value, AXES, pairs)  14.8 us
    pallas_call x4, Pallas kernels, product(): pl.pallas_call(functools.partial(product_kernel, edge, slots, narrow, cha...  14 us
    unnamed x4, local copies, waits for them, and re-layouts  1.41 us
  transfers between devices with their start and end apart: 12, of which 4 were waited for; matrix products, arithmetic and copies ran while one was open for 3% of the time, Pallas kernels for 19%

profile of v4, /device:TPU:0, one launch (start us, length us, event | category | flops | bytes accessed | tf_op | source)
XLA Modules:
  0.0 62.2 jit_solution(18318552566930259881)
XLA Ops:
  0.0 2.9 %collective-permute-start.10 = (f32[24,128,128]{2,1,0:T(8,128)}, f32[24,128,128]{2,1,0:T(8,128)S(1)}, u32[]{:S(2)}, u32[]{:S(2)}) collective-permute-start(f32[24,128,128]{2,1,0:T(8,128)} %bitcast.26), channel_id=1, source_target_pairs={{0,1},{4,5},{8,9},{12,13},{16,17},{20,21},{24,25},{28,29},{1,0},{5... | collective-permute-start | bytes 4718600 | tf_op jit(solution)/shard_map/second/ppermute | solution.py:191
  2.9 1.1 %shard_map.46 = f32[776,128]{1,0:T(8,128)S(1)} custom-call(f32[6,128,128]{2,1,0:T(8,128)} %bitcast.29, s32[1,2,6]{2,1,0:T(2,128)} %index_hbm.1), custom_call_target="tpu_custom_call" | custom-call | tf_op jit(solution)/shard_map/pallas_call | solution.py:150
  4.0 2.7 %collective-permute-start.5 = (f32[776,128]{1,0:T(8,128)S(1)}, f32[776,128]{1,0:T(8,128)S(1)}, u32[]{:S(2)}, u32[]{:S(2)}) collective-permute-start(f32[776,128]{1,0:T(8,128)S(1)} %shard_map.46), channel_id=1, source_target_pairs={{0,16},{4,20},{8,24},{12,28},{16,0},{20,4},{24,8},{28,12},{1,17},{... | collective-permute-start | bytes 1191944 | tf_op jit(solution)/shard_map/far/ppermute | solution.py:191
  6.7 1.6 %collective-permute-start.3 = (f32[776,128]{1,0:T(8,128)S(1)}, f32[776,128]{1,0:T(8,128)S(1)}, u32[]{:S(2)}, u32[]{:S(2)}) collective-permute-start(f32[776,128]{1,0:T(8,128)S(1)} %shard_map.46), channel_id=1, source_target_pairs={{0,8},{4,12},{8,10},{12,14},{16,24},{20,28},{24,26},{28,30},{1,9},... | collective-permute-start | bytes 1191944 | tf_op jit(solution)/shard_map/share_0_1/ppermute | solution.py:191
  8.2 0.7 %collective-permute-start.1 = (f32[776,128]{1,0:T(8,128)S(1)}, f32[776,128]{1,0:T(8,128)S(1)}, u32[]{:S(2)}, u32[]{:S(2)}) collective-permute-start(f32[776,128]{1,0:T(8,128)S(1)} %shard_map.46), channel_id=1, source_target_pairs={{0,0},{4,4},{8,2},{12,6},{16,16},{20,20},{24,18},{28,22},{1,1},{5,... | collective-permute-start | bytes 1191944 | tf_op jit(solution)/shard_map/share_0_0/ppermute | solution.py:191
  8.9 15.3 %collective-permute-done.5 = f32[776,128]{1,0:T(8,128)S(1)} collective-permute-done((f32[776,128]{1,0:T(8,128)S(1)}, f32[776,128]{1,0:T(8,128)S(1)}, u32[]{:S(2)}, u32[]{:S(2)}) %collective-permute-start.5) | collective-permute-done | bytes 397344 | tf_op jit(solution)/shard_map/far/ppermute | solution.py:191
  24.3 0.6 collective-permute-start.8
  24.8 0.7 %collective-permute-start.6 = (f32[776,128]{1,0:T(8,128)S(1)}, f32[776,128]{1,0:T(8,128)S(1)}, u32[]{:S(2)}, u32[]{:S(2)}) collective-permute-start(f32[776,128]{1,0:T(8,128)S(1)} %collective-permute-done.5), channel_id=1, source_target_pairs={{0,0},{4,4},{8,2},{12,6},{16,16},{20,20},{24,18},{28,22},{1,1},{5,... | collective-permute-start | bytes 1191944 | tf_op jit(solution)/shard_map/share_1_0/ppermute | solution.py:191
  25.5 0.8 %iota_add_fusion = (s32[24]{0:T(128)S(1)}, s32[24]{0:T(128)S(1)}) fusion(s32[1,2,24]{2,1,0:T(2,128)} %param.7), kind=kLoop, calls=%fused_computation.15 | loop fusion | flops 792 | bytes 384 | tf_op jit(solution)/shard_map/sub | solution.py:171
  26.3 0.0 collective-permute-done.3.refs_3_
  26.3 0.1 collective-permute-start.4
  26.4 0.0 collective-permute-done.1.refs_1_
  26.4 0.5 collective-permute-start.2
  26.9 7.4 %collective-permute-done.8.refs_7_ = f32[776,128]{1,0:T(8,128)S(1)} collective-permute-done((f32[776,128]{1,0:T(8,128)S(1)}, f32[776,128]{1,0:T(8,128)S(1)}, u32[]{:S(2)}, u32[]{:S(2)}) %collective-permute-start.8) | collective-permute-done | bytes 397344 | tf_op jit(solution)/shard_map/share_1_1/ppermute | solution.py:191
  34.3 0.0 collective-permute-done.6.refs_5_
  34.3 0.5 collective-permute-start.7
  34.8 0.7 %bitcast_compare_fusion = pred[24]{0:T(512)(128)(4,1)S(1)} fusion(s32[1,2,24]{2,1,0:T(2,128)} %param.7), kind=kLoop, calls=%fused_computation.13 | loop fusion | flops 24 | bytes 120 | tf_op jit(solution)/shard_map/ge | solution.py:170
  35.5 0.1 select_reduce_fusion
  35.6 0.0 collective-permute-done.4.refs_4_
  35.6 0.6 collective-permute-start
  36.2 0.4 collective-permute-done.7.refs_6_
  36.6 1.4 %copy-done = f32[1,24,128,128]{3,2,1,0:T(8,128)S(1)} copy-done((f32[1,24,128,128]{3,2,1,0:T(8,128)S(1)}, f32[1,24,128,128]{3,2,1,0:T(8,128)}, u32[]{:S(2)}) %copy-start) | copy-done | bytes 1572888
  38.0 3.5 %shard_map.49.refs_10_ = f32[8,128,128]{2,1,0:T(8,128)S(1)} custom-call(s32[1028]{0:T(1024)S(1)} %broadcast_add_fusion.refs_0_, f32[776,128]{1,0:T(8,128)S(1)} %collective-permute-done.1.refs_1_, f32[776,128]{1,0:T(8,128)S(1)} %collective-permute-done.2.refs_2_, f32[776,128]{1,0:T(8,128)S(1)} %collective-permute-done.3.refs_3_, ...), custom_call_target="tpu_custom_call" | custom-call | flops 1207959552 | bytes 4194304 | tf_op jit(solution)/shard_map/pallas_call | solution.py:100
  41.5 0.0 copy-start.1
  41.5 0.0 collective-permute-done.refs_0_
  41.5 0.0 collective-permute-done.10.refs_9_
  41.5 3.5 %shard_map.50 = f32[8,128,128]{2,1,0:T(8,128)S(1)} custom-call(s32[1028]{0:T(1024)S(1)} %collective-permute-done.refs_0_, f32[776,128]{1,0:T(8,128)S(1)} %collective-permute-done.1.refs_1_, f32[776,128]{1,0:T(8,128)S(1)} %collective-permute-done.2.refs_2_, f32[776,128]{1,0:T(8,128)S(1)} %collective-permute-done.3.refs_3_, ...), custom_call_target="tpu_custom_call" | custom-call | flops 1207959552 | bytes 4194304 | tf_op jit(solution)/shard_map/pallas_call | solution.py:100
  45.0 4.1 %collective-permute-start.11 = (f32[8,128,128]{2,1,0:T(8,128)S(1)}, f32[8,128,128]{2,1,0:T(8,128)S(1)}, u32[]{:S(2)}, u32[]{:S(2)}) collective-permute-start(f32[8,128,128]{2,1,0:T(8,128)S(1)} %shard_map.50), channel_id=1, source_target_pairs={{0,2},{4,6},{8,10},{12,14},{16,18},{20,22},{24,26},{28,30},{1,3},{... | collective-permute-start | bytes 1572872 | tf_op jit(solution)/shard_map/window_1/ppermute | solution.py:191
  49.1 3.5 %shard_map.47.refs_10_ = f32[8,128,128]{2,1,0:T(8,128)S(1)} custom-call(s32[1028]{0:T(1024)S(1)} %broadcast_add_fusion.refs_0_, f32[776,128]{1,0:T(8,128)S(1)} %collective-permute-done.1.refs_1_, f32[776,128]{1,0:T(8,128)S(1)} %collective-permute-done.2.refs_2_, f32[776,128]{1,0:T(8,128)S(1)} %collective-permute-done.3.refs_3_, ...), custom_call_target="tpu_custom_call" | custom-call | flops 1207959552 | bytes 4194304 | tf_op jit(solution)/shard_map/pallas_call | solution.py:100
  52.6 3.5 %shard_map.48 = f32[8,128,128]{2,1,0:T(8,128)S(1)} custom-call(s32[1028]{0:T(1024)S(1)} %collective-permute-done.refs_0_, f32[776,128]{1,0:T(8,128)S(1)} %collective-permute-done.1.refs_1_, f32[776,128]{1,0:T(8,128)S(1)} %collective-permute-done.2.refs_2_, f32[776,128]{1,0:T(8,128)S(1)} %collective-permute-done.3.refs_3_, ...), custom_call_target="tpu_custom_call" | custom-call | flops 1207959552 | bytes 4194304 | tf_op jit(solution)/shard_map/pallas_call | solution.py:100
  56.1 5.2 %collective-permute-done.11 = f32[8,128,128]{2,1,0:T(8,128)S(1)} collective-permute-done((f32[8,128,128]{2,1,0:T(8,128)S(1)}, f32[8,128,128]{2,1,0:T(8,128)S(1)}, u32[]{:S(2)}, u32[]{:S(2)}) %collective-permute-start.11) | collective-permute-done | bytes 524320 | tf_op jit(solution)/shard_map/window_1/ppermute | solution.py:191
  61.3 0.9 %add.35 = f32[8,128,128]{2,1,0:T(8,128)} add(f32[8,128,128]{2,1,0:T(8,128)S(1)} %shard_map.48, f32[8,128,128]{2,1,0:T(8,128)S(1)} %collective-permute-done.11) | non-fusion elementwise | flops 131072 | bytes 1572864 | tf_op jit(solution)/shard_map/add | solution.py:225
  (6 shorter events, 0.0 us)
Async XLA Ops:
  0.0 41.5 %collective-permute-start.10 = (f32[24,128,128]{2,1,0:T(8,128)}, f32[24,128,128]{2,1,0:T(8,128)S(1)}, u32[]{:S(2)}, u32[]{:S(2)}) collective-permute-start(f32[24,128,128]{2,1,0:T(8,128)} %bitcast.26), channel_id=1, source_target_pairs={{0,1},{4,5},{8,9},{12,13},{16,17},{20,21},{24,25},{28,29},{1,0},{5... | collective-permute-start | bytes 4718600 | tf_op jit(solution)/shard_map/second/ppermute | solution.py:191
  4.0 20.2 %collective-permute-start.5 = (f32[776,128]{1,0:T(8,128)S(1)}, f32[776,128]{1,0:T(8,128)S(1)}, u32[]{:S(2)}, u32[]{:S(2)}) collective-permute-start(f32[776,128]{1,0:T(8,128)S(1)} %shard_map.46), channel_id=1, source_target_pairs={{0,16},{4,20},{8,24},{12,28},{16,0},{20,4},{24,8},{28,12},{1,17},{... | collective-permute-start | bytes 1191944 | tf_op jit(solution)/shard_map/far/ppermute | solution.py:191
  6.7 19.6 %collective-permute-start.3 = (f32[776,128]{1,0:T(8,128)S(1)}, f32[776,128]{1,0:T(8,128)S(1)}, u32[]{:S(2)}, u32[]{:S(2)}) collective-permute-start(f32[776,128]{1,0:T(8,128)S(1)} %shard_map.46), channel_id=1, source_target_pairs={{0,8},{4,12},{8,10},{12,14},{16,24},{20,28},{24,26},{28,30},{1,9},... | collective-permute-start | bytes 1191944 | tf_op jit(solution)/shard_map/share_0_1/ppermute | solution.py:191
  8.2 18.1 %collective-permute-start.1 = (f32[776,128]{1,0:T(8,128)S(1)}, f32[776,128]{1,0:T(8,128)S(1)}, u32[]{:S(2)}, u32[]{:S(2)}) collective-permute-start(f32[776,128]{1,0:T(8,128)S(1)} %shard_map.46), channel_id=1, source_target_pairs={{0,0},{4,4},{8,2},{12,6},{16,16},{20,20},{24,18},{28,22},{1,1},{5,... | collective-permute-start | bytes 1191944 | tf_op jit(solution)/shard_map/share_0_0/ppermute | solution.py:191
  24.3 10.0 %collective-permute-start.8 = (f32[776,128]{1,0:T(8,128)S(1)}, f32[776,128]{1,0:T(8,128)S(1)}, u32[]{:S(2)}, u32[]{:S(2)}) collective-permute-start(f32[776,128]{1,0:T(8,128)S(1)} %collective-permute-done.5), channel_id=1, source_target_pairs={{0,8},{4,12},{8,10},{12,14},{16,24},{20,28},{24,26},{28,30},{1,9},... | collective-permute-start | bytes 1191944 | tf_op jit(solution)/shard_map/share_1_1/ppermute | solution.py:191
  24.8 9.4 %collective-permute-start.6 = (f32[776,128]{1,0:T(8,128)S(1)}, f32[776,128]{1,0:T(8,128)S(1)}, u32[]{:S(2)}, u32[]{:S(2)}) collective-permute-start(f32[776,128]{1,0:T(8,128)S(1)} %collective-permute-done.5), channel_id=1, source_target_pairs={{0,0},{4,4},{8,2},{12,6},{16,16},{20,20},{24,18},{28,22},{1,1},{5,... | collective-permute-start | bytes 1191944 | tf_op jit(solution)/shard_map/share_1_0/ppermute | solution.py:191
  26.3 9.3 %collective-permute-start.4 = (f32[776,128]{1,0:T(8,128)S(1)}, f32[776,128]{1,0:T(8,128)S(1)}, u32[]{:S(2)}, u32[]{:S(2)}) collective-permute-start(f32[776,128]{1,0:T(8,128)S(1)} %collective-permute-done.3.refs_3_), channel_id=1, source_target_pairs={{0,4},{4,0},{8,12},{12,8},{16,20},{20,16},{24,28},{28,24},{1,5},{5... | collective-permute-start | bytes 1191944 | tf_op jit(solution)/shard_map/swap_0/ppermute | solution.py:191
  26.4 9.8 %collective-permute-start.2 = (f32[776,128]{1,0:T(8,128)S(1)}, f32[776,128]{1,0:T(8,128)S(1)}, u32[]{:S(2)}, u32[]{:S(2)}) collective-permute-start(f32[776,128]{1,0:T(8,128)S(1)} %collective-permute-done.1.refs_1_), channel_id=1, source_target_pairs={{0,4},{4,0},{8,12},{12,8},{16,20},{20,16},{24,28},{28,24},{1,5},{5... | collective-permute-start | bytes 1191944 | tf_op jit(solution)/shard_map/swap_0/ppermute | solution.py:191
  34.3 1.9 %collective-permute-start.9 = (f32[776,128]{1,0:T(8,128)S(1)}, f32[776,128]{1,0:T(8,128)S(1)}, u32[]{:S(2)}, u32[]{:S(2)}) collective-permute-start(f32[776,128]{1,0:T(8,128)S(1)} %collective-permute-done.8.refs_7_), channel_id=1, source_target_pairs={{0,4},{4,0},{8,12},{12,8},{16,20},{20,16},{24,28},{28,24},{1,5},{5... | collective-permute-start | bytes 1191944 | tf_op jit(solution)/shard_map/swap_1/ppermute | solution.py:191
  34.3 2.3 %collective-permute-start.7 = (f32[776,128]{1,0:T(8,128)S(1)}, f32[776,128]{1,0:T(8,128)S(1)}, u32[]{:S(2)}, u32[]{:S(2)}) collective-permute-start(f32[776,128]{1,0:T(8,128)S(1)} %collective-permute-done.6.refs_5_), channel_id=1, source_target_pairs={{0,4},{4,0},{8,12},{12,8},{16,20},{20,16},{24,28},{28,24},{1,5},{5... | collective-permute-start | bytes 1191944 | tf_op jit(solution)/shard_map/swap_1/ppermute | solution.py:191
  35.6 5.9 %collective-permute-start = (s32[1028]{0:T(1024)S(1)}, s32[1028]{0:T(1024)S(1)}, u32[]{:S(2)}, u32[]{:S(2)}) collective-permute-start(s32[1028]{0:T(1024)S(1)} %broadcast_add_fusion.refs_0_), channel_id=1, source_target_pairs={{0,1},{4,5},{8,9},{12,13},{16,17},{20,21},{24,25},{28,29},{1,0},{5... | collective-permute-start | bytes 12344 | tf_op jit(solution)/shard_map/second_table/ppermute | solution.py:191
  36.6 1.4 %copy-start = (f32[1,24,128,128]{3,2,1,0:T(8,128)S(1)}, f32[1,24,128,128]{3,2,1,0:T(8,128)}, u32[]{:S(2)}) copy-start(f32[1,24,128,128]{3,2,1,0:T(8,128)} %param.6) | copy-start | bytes 4718596
  41.5 7.6 %copy-start.1 = (f32[1,24,128,128]{3,2,1,0:T(8,128)S(1)}, f32[1,24,128,128]{3,2,1,0:T(8,128)}, u32[]{:S(2)}) copy-start(f32[1,24,128,128]{3,2,1,0:T(8,128)} %param.6) | copy-start | bytes 4718596
  45.0 16.3 %collective-permute-start.11 = (f32[8,128,128]{2,1,0:T(8,128)S(1)}, f32[8,128,128]{2,1,0:T(8,128)S(1)}, u32[]{:S(2)}, u32[]{:S(2)}) collective-permute-start(f32[8,128,128]{2,1,0:T(8,128)S(1)} %shard_map.50), channel_id=1, source_target_pairs={{0,2},{4,6},{8,10},{12,14},{16,18},{20,22},{24,26},{28,30},{1,3},{... | collective-permute-start | bytes 1572872 | tf_op jit(solution)/shard_map/window_1/ppermute | solution.py:191

commit v5 on v4

v5 whole, which is shorter than its diff:
```python
import functools

import jax
import jax.numpy as jnp
from jax import lax
from jax.experimental import pallas as pl
from jax.experimental.pallas import tpu as pltpu
from jax.sharding import PartitionSpec as P

RL = 2
CL = 4
KBLOCKS = 1024
PAD = 8
AXES = ("wide", "narrow")
VMEM_LIMIT = 20 * 1024 * 1024


def split(value):
    high = value.astype(jnp.bfloat16)
    low = (value - high.astype(jnp.float32)).astype(jnp.bfloat16)
    return high, low


def product_kernel(edge, slots, narrow, wide, change, choices, crossings, has_start, *refs):
    items = len(crossings)
    classes = sorted(set(crossings))
    empty_ref, refs = refs[0], refs[1:]
    shares = [refs[n * choices : (n + 1) * choices] for n in range(items)]
    refs = refs[items * choices :]
    second_refs, refs = dict(zip(classes, refs)), refs[len(classes) :]
    if has_start:
        start_ref, refs = refs[0], refs[1:]
    (out_ref, a_ref, index_ref, second_index, tables, left_high, left_low, right_high, right_low,
     block_sems, index_sems, second_sems, table_sems) = refs
    row, column = lax.axis_index("narrow"), lax.axis_index("wide")
    turn = (row // 2) ^ (column // 2 % (choices // 2)) ^ change
    rows = slots * edge
    slots_second = second_refs[classes[0]].shape[0] // edge
    table_copies = []
    for crossing in classes:
        tile = pl.ds(slots_second * edge, PAD)
        table_copies.append(
            pltpu.make_async_copy(second_refs[crossing].at[tile], second_index.at[crossing], second_sems.at[crossing])
        )
        table_copies.append(pltpu.make_async_copy(empty_ref, tables.at[crossing], table_sems.at[crossing]))

    def copies(n, ref):
        return (
            pltpu.make_async_copy(ref.at[pl.ds(rows, PAD)], index_ref.at[n], index_sems.at[n]),
            pltpu.make_async_copy(ref.at[pl.ds(0, rows)], a_ref.at[n], block_sems.at[n]),
        )

    for copy in table_copies:
        copy.start()
    for n, crossing in enumerate(crossings):
        pick = turn * 2 + ((row ^ column) % 2 ^ crossing)
        for choice in range(choices):
            @pl.when(pick == choice)
            def _():
                for copy in copies(n, shares[n][choice]):
                    copy.start()
    left_high[...] = jnp.zeros_like(left_high)
    left_low[...] = jnp.zeros_like(left_low)
    for copy in table_copies:
        copy.wait()
    for crossing in classes:
        for slot in range(slots_second):
            inner = second_index[crossing, 0, slot].astype(jnp.int32)
            outer = second_index[crossing, 1, slot].astype(jnp.int32)
            place = lax.div(jnp.maximum(inner, 0), narrow) * CL + lax.div(jnp.maximum(outer, 0), wide)
            tables[crossing, jnp.where(inner < 0, (KBLOCKS // narrow + 1) * CL, place)] = slot
    waits = [copies(n, shares[n][0]) for n in range(items)]
    for index_copy, _ in waits:
        index_copy.wait()
    for n, crossing in enumerate(crossings):
        for slot in range(slots):
            at = (n * slots + slot) * edge
            inner = index_ref[n, 1, slot].astype(jnp.int32)
            inner = jnp.where(inner < 0, KBLOCKS // narrow, lax.div(jnp.maximum(inner, 0), narrow))
            for m in range(CL):
                block = tables[crossing, inner * CL + m]
                source = pl.ds(pl.multiple_of(jnp.minimum(block, slots_second - 1) * edge, edge), edge)
                high, low = split(jnp.where(block < slots_second, second_refs[crossing][source, :], 0.0))
                right_high[at : at + edge, m * edge : (m + 1) * edge] = high
                right_low[at : at + edge, m * edge : (m + 1) * edge] = low
    for _, block_copy in waits:
        block_copy.wait()
    for n in range(items):
        for slot in range(slots):
            at = (n * slots + slot) * edge
            line = lax.div(jnp.maximum(index_ref[n, 0, slot].astype(jnp.int32), 0), narrow)
            high, low = split(a_ref[n, slot * edge : (slot + 1) * edge, :])
            target = pl.ds(pl.multiple_of(line * edge, edge), edge)
            left_high[target, at : at + edge] = high
            left_low[target, at : at + edge] = low
    dot = functools.partial(jnp.dot, preferred_element_type=jnp.float32)
    for m in range(0, CL, 2):
        columns = slice(m * edge, (m + 2) * edge)
        value = (
            dot(left_high[...], right_high[:, columns])
            + dot(left_low[...], right_high[:, columns])
            + dot(left_high[...], right_low[:, columns])
        )
        for l in range(RL):
            for k in range(2):
                at = l * CL + m + k
                piece = value[l * edge : (l + 1) * edge, k * edge : (k + 1) * edge]
                out_ref[at] = start_ref[at] + piece if has_start else piece


def product(narrow, wide, change, crossings, shares, seconds, start=None):
    edge = shares[0][0].shape[1]
    items = len(shares)
    choices = len(shares[0])
    slots = (shares[0][0].shape[0] - PAD) // edge
    depth = items * slots * edge
    anywhere = pl.BlockSpec(memory_space=pl.ANY)
    whole = pl.BlockSpec(memory_space=pltpu.VMEM)
    places = (KBLOCKS // narrow + 2) * CL
    empty = jnp.full((places,), seconds[0].shape[0] // edge, jnp.int32)
    operands = [seconds[crossing] for crossing in sorted(set(crossings))]
    if start is not None:
        operands.append(start)
    return pl.pallas_call(
        functools.partial(product_kernel, edge, slots, narrow, wide, change, choices, crossings, start is not None),
        out_shape=jax.ShapeDtypeStruct((RL * CL, edge, edge), jnp.float32),
        in_specs=[anywhere] * (1 + items * choices) + [whole] * len(operands),
        out_specs=whole,
        scratch_shapes=[
            pltpu.VMEM((items, slots * edge, edge), jnp.float32),
            pltpu.SMEM((items, PAD, edge), jnp.float32),
            pltpu.SMEM((2, PAD, edge), jnp.float32),
            pltpu.SMEM((2, places), jnp.int32),
            pltpu.VMEM((RL * edge, depth), jnp.bfloat16),
            pltpu.VMEM((RL * edge, depth), jnp.bfloat16),
            pltpu.VMEM((depth, CL * edge), jnp.bfloat16),
            pltpu.VMEM((depth, CL * edge), jnp.bfloat16),
            pltpu.SemaphoreType.DMA((items,)),
            pltpu.SemaphoreType.DMA((items,)),
            pltpu.SemaphoreType.DMA((2,)),
            pltpu.SemaphoreType.DMA((2,)),
        ],
        compiler_params=pltpu.CompilerParams(vmem_limit_bytes=VMEM_LIMIT),
        cost_estimate=pl.CostEstimate(
            flops=6 * RL * depth * CL * edge * edge, bytes_accessed=4 * 1024 * 1024, transcendentals=0
        ),
    )(empty, *[ref for share in shares for ref in share], *operands)


def share_kernel(*refs):
    arrays = len(refs) // 7
    parts = [refs[n * arrays : (n + 1) * arrays] for n in range(7)]
    waits = []
    for blocks_hbm, index_hbm, out_hbm, tile_ref, index_ref, block_sem, index_sem in zip(*parts):
        slots, edge, _ = blocks_hbm.shape
        copies = [
            pltpu.make_async_copy(blocks_hbm.at[slot], out_hbm.at[pl.ds(slot * edge, edge)], block_sem.at[slot])
            for slot in range(slots)
        ]
        index_copy = pltpu.make_async_copy(index_hbm, index_ref, index_sem)
        index_copy.start()
        for copy in copies:
            copy.start()
        waits += copies
    for blocks_hbm, index_hbm, out_hbm, tile_ref, index_ref, block_sem, index_sem in zip(*parts):
        slots, edge, _ = blocks_hbm.shape
        pltpu.make_async_copy(index_hbm, index_ref, index_sem).wait()
        shape = tile_ref.shape
        row = lax.broadcasted_iota(jnp.int32, shape, 0)
        column = lax.broadcasted_iota(jnp.int32, shape, 1)
        tile = jnp.zeros(shape, jnp.float32)
        for n in range(2):
            for slot in range(slots):
                tile = jnp.where((row == n) & (column == slot), index_ref[0, n, slot].astype(jnp.float32), tile)
        tile_ref[...] = tile
        tile_copy = pltpu.make_async_copy(tile_ref, out_hbm.at[pl.ds(slots * edge, PAD)], block_sem.at[slots])
        tile_copy.start()
        waits.append(tile_copy)
    for copy in waits:
        copy.wait()


def build_shares(blocks, indices):
    anywhere = pl.BlockSpec(memory_space=pl.ANY)
    return pl.pallas_call(
        share_kernel,
        out_shape=tuple(
            jax.ShapeDtypeStruct((value.shape[0] * value.shape[1] + PAD, value.shape[2]), jnp.float32) for value in blocks
        ),
        in_specs=[anywhere] * (2 * len(blocks)),
        out_specs=(anywhere,) * len(blocks),
        scratch_shapes=[pltpu.VMEM((PAD, value.shape[2]), jnp.float32) for value in blocks]
        + [pltpu.SMEM(value.shape, jnp.int32) for value in indices]
        + [pltpu.SemaphoreType.DMA((value.shape[0] + 1,)) for value in blocks]
        + [pltpu.SemaphoreType.DMA for _ in blocks],
        compiler_params=pltpu.CompilerParams(vmem_limit_bytes=1024 * 1024),
    )(*[pltpu.with_memory_space_constraint(value, pltpu.HBM) for value in (*blocks, *indices)])


def local(a_blocks, a_index, b_blocks, b_index):
    narrow = lax.axis_size("narrow")
    wide = lax.axis_size("wide")
    groups = narrow // 2
    planes = wide // 2
    slots = a_blocks.shape[1]
    edge = a_blocks.shape[-1]

    def permute(name, value, to):
        pairs = []
        for r in range(narrow):
            for c in range(wide):
                target = to(r, c)
                if target is not None:
                    pairs.append((c * narrow + r, target[1] * narrow + target[0]))
        with jax.named_scope(name):
            return lax.ppermute(value, AXES, pairs)

    def swap(name, value):
        return permute(name, value, lambda r, c: (r, c ^ 1))

    share, second = build_shares((a_blocks[0], b_blocks[0]), (a_index, b_index))
    second_other = permute("second", second, lambda r, c: (r ^ 1, c))

    def spread(half, share, turn):
        def to(r, c):
            plane = c // 2
            u = plane % groups
            change = (r // 2) ^ u
            return (u * 2 + r % 2, (plane ^ change ^ turn) * 2 + c % 2)
        return permute(f"share_{half}_{turn}", share, to)

    far = permute("far", share, lambda r, c: (r, (c // 2 ^ groups) * 2 + c % 2))
    turns = [[spread(half, value, turn) for turn in range(groups)] for half, value in enumerate((share, far))]
    swapped = [[swap(f"swap_{half}", value) for value in values] for half, values in enumerate(turns)]
    candidates = [[ref for pair in zip(*values) for ref in pair] for values in zip(turns, swapped)]
    seconds = (second, second_other)
    received = []
    for change in range(1, groups):
        value = product(narrow, wide, change, (0, 0, 1, 1), candidates * 2, seconds)
        received.append(permute(f"window_{change}", value, lambda r, c: (r ^ (change * 2), c)))
    total = product(narrow, wide, 0, (0, 0), candidates, seconds)
    total = product(narrow, wide, 0, (1, 1), candidates, seconds, total)
    for value in received:
        total = total + value
    return total.reshape(1, RL, 1, CL, edge, edge)


def solution(mesh):
    return jax.shard_map(
        local,
        mesh=mesh,
        in_specs=(
            P("narrow", "wide", None, None),
            P("narrow", None, "wide"),
            P("narrow", "wide", None, None),
            P("narrow", None, "wide"),
        ),
        out_specs=P("narrow", None, "wide", None, None, None),
        check_vma=False,
    )
```

time: 63.1 us -> 61 us (0.967)
  waiting for transfers between devices: 28.4 us -> 33.5 us
  starting transfers between devices: 14.8 us -> 12.3 us
  Pallas kernels: 15 us -> 13.3 us
  other arithmetic: 2.42 us -> 0.85 us
  local copies, waits for them, and re-layouts: 1.41 us -> 0.01 us
    ppermute x12 -> x11, waiting for transfers between devices: 28.4 us -> 33.5 us  [permute(): return lax.ppermute(value, AXES, pairs)]
    ppermute x12 -> x11, starting transfers between devices: 14.8 us -> 12.3 us  [permute(): return lax.ppermute(value, AXES, pairs)]
    pallas_call x5 -> x4, Pallas kernels: 15 us -> 13.3 us  [the longest x3 11.5 us: product(): pl.pallas_call(functools.partial(product_kernel, edge, slots, narrow, wid...]
    unnamed x4 -> x0, local copies, waits for them, and re-layouts: 1.41 us -> none
    sub x1 -> x0, other arithmetic: 0.77 us -> none  [block_table(): found = jnp.where(hit, jnp.arange(slots_second)[None, :] - slots_second, 0)]
    ge x1 -> x0, other arithmetic: 0.68 us -> none  [block_table(): hit = (table == wanted[None, :]) & (b_index[0, 0] >= 0)[None, :]]
  transfers between devices with their start and end apart: 12 -> 11, of which waited for: 4 -> 6; matrix products, arithmetic and copies ran while one was open for 3% -> 0% of each run, Pallas kernels for 19% -> 10%
where the time goes in v5:
time: 61 us; the launch traced here: 60.1 us
  waiting for transfers between devices  33.5 us (55%)
  Pallas kernels  13.3 us (22%)
  starting transfers between devices  12.3 us (20%)
  other arithmetic  0.85 us (1%)
    ppermute x11, waiting for transfers between devices, permute(): return lax.ppermute(value, AXES, pairs)  33.5 us
    ppermute x11, starting transfers between devices, permute(): return lax.ppermute(value, AXES, pairs)  12.3 us
    pallas_call x3, Pallas kernels, product(): pl.pallas_call(functools.partial(product_kernel, edge, slots, narrow, wid...  11.5 us
    pallas_call x1, Pallas kernels, build_shares(): pl.pallas_call(share_kernel, out_shape=tuple((jax.ShapeDtypeStruct((value...  1.83 us
  transfers between devices with their start and end apart: 11, of which 6 were waited for; matrix products, arithmetic and copies ran while one was open for 0% of the time, Pallas kernels for 10%

profile of v5, /device:TPU:0, one launch (start us, length us, event | category | flops | bytes accessed | tf_op | source)
XLA Modules:
  0.0 60.1 jit_solution(9365596851935647162)
XLA Ops:
  0.0 1.8 %shard_map.46 = (f32[776,128]{1,0:T(8,128)S(1)}, f32[3080,128]{1,0:T(8,128)S(1)}) custom-call(f32[6,128,128]{2,1,0:T(8,128)} %bitcast.6, f32[24,128,128]{2,1,0:T(8,128)} %bitcast.5, s32[1,2,6]{2,1,0:T(2,128)} %refs_2_.1, s32[1,2,24]{2,1,0:T(2,128)} %refs_3_.1), custom_call_target="tpu_custom_call" | custom-call | tf_op jit(solution)/shard_map/pallas_call | solution.py:185
  1.8 3.0 %collective-permute-start.9 = (f32[3080,128]{1,0:T(8,128)S(1)}, f32[3080,128]{1,0:T(8,128)S(1)}, u32[]{:S(2)}, u32[]{:S(2)}) collective-permute-start(f32[3080,128]{1,0:T(8,128)S(1)} %get-tuple-element.8.refs_9_.refs_17_), channel_id=1, source_target_pairs={{0,1},{4,5},{8,9},{12,13},{16,17},{20,21},{24,25},{28,29},{1,0},{5... | collective-permute-start | bytes 4730888 | tf_op jit(solution)/shard_map/second/ppermute | solution.py:216
  4.8 2.6 %collective-permute-start.4 = (f32[776,128]{1,0:T(8,128)S(1)}, f32[776,128]{1,0:T(8,128)S(1)}, u32[]{:S(2)}, u32[]{:S(2)}) collective-permute-start(f32[776,128]{1,0:T(8,128)S(1)} %get-tuple-element.7), channel_id=1, source_target_pairs={{0,16},{4,20},{8,24},{12,28},{16,0},{20,4},{24,8},{28,12},{1,17},{... | collective-permute-start | bytes 1191944 | tf_op jit(solution)/shard_map/far/ppermute | solution.py:216
  7.4 1.6 %collective-permute-start.2 = (f32[776,128]{1,0:T(8,128)S(1)}, f32[776,128]{1,0:T(8,128)S(1)}, u32[]{:S(2)}, u32[]{:S(2)}) collective-permute-start(f32[776,128]{1,0:T(8,128)S(1)} %get-tuple-element.7), channel_id=1, source_target_pairs={{0,8},{4,12},{8,10},{12,14},{16,24},{20,28},{24,26},{28,30},{1,9},... | collective-permute-start | bytes 1191944 | tf_op jit(solution)/shard_map/share_0_1/ppermute | solution.py:216
  9.0 0.7 %collective-permute-start = (f32[776,128]{1,0:T(8,128)S(1)}, f32[776,128]{1,0:T(8,128)S(1)}, u32[]{:S(2)}, u32[]{:S(2)}) collective-permute-start(f32[776,128]{1,0:T(8,128)S(1)} %get-tuple-element.7), channel_id=1, source_target_pairs={{0,0},{4,4},{8,2},{12,6},{16,16},{20,20},{24,18},{28,22},{1,1},{5,... | collective-permute-start | bytes 1191944 | tf_op jit(solution)/shard_map/share_0_0/ppermute | solution.py:216
  9.7 15.3 %collective-permute-done.4 = f32[776,128]{1,0:T(8,128)S(1)} collective-permute-done((f32[776,128]{1,0:T(8,128)S(1)}, f32[776,128]{1,0:T(8,128)S(1)}, u32[]{:S(2)}, u32[]{:S(2)}) %collective-permute-start.4) | collective-permute-done | bytes 397344 | tf_op jit(solution)/shard_map/far/ppermute | solution.py:216
  25.0 0.6 collective-permute-start.7
  25.6 0.7 %collective-permute-start.5 = (f32[776,128]{1,0:T(8,128)S(1)}, f32[776,128]{1,0:T(8,128)S(1)}, u32[]{:S(2)}, u32[]{:S(2)}) collective-permute-start(f32[776,128]{1,0:T(8,128)S(1)} %collective-permute-done.4), channel_id=1, source_target_pairs={{0,0},{4,4},{8,2},{12,6},{16,16},{20,20},{24,18},{28,22},{1,1},{5,... | collective-permute-start | bytes 1191944 | tf_op jit(solution)/shard_map/share_1_0/ppermute | solution.py:216
  26.3 0.0 collective-permute-done.2.refs_3_.refs_11_
  26.3 0.1 collective-permute-start.3
  26.4 0.0 collective-permute-done.refs_1_.refs_9_
  26.4 0.5 collective-permute-start.1
  26.9 8.2 %collective-permute-done.7.refs_7_.refs_15_ = f32[776,128]{1,0:T(8,128)S(1)} collective-permute-done((f32[776,128]{1,0:T(8,128)S(1)}, f32[776,128]{1,0:T(8,128)S(1)}, u32[]{:S(2)}, u32[]{:S(2)}) %collective-permute-start.7) | collective-permute-done | bytes 397344 | tf_op jit(solution)/shard_map/share_1_1/ppermute | solution.py:216
  35.0 0.0 collective-permute-start.8
  35.0 0.0 collective-permute-done.5.refs_5_.refs_13_
  35.0 0.5 collective-permute-start.6
  35.5 0.0 collective-permute-done.3.refs_4_.refs_12_
  35.5 0.0 collective-permute-done.1.refs_2_.refs_10_
  35.5 1.2 %collective-permute-done.8.refs_8_.refs_16_ = f32[776,128]{1,0:T(8,128)S(1)} collective-permute-done((f32[776,128]{1,0:T(8,128)S(1)}, f32[776,128]{1,0:T(8,128)S(1)}, u32[]{:S(2)}, u32[]{:S(2)}) %collective-permute-start.8) | collective-permute-done | bytes 397344 | tf_op jit(solution)/shard_map/swap_1/ppermute | solution.py:216
  36.8 0.6 collective-permute-done.6.refs_6_.refs_14_
  37.3 2.0 %collective-permute-done.9.refs_9_.refs_18_ = f32[3080,128]{1,0:T(8,128)S(1)} collective-permute-done((f32[3080,128]{1,0:T(8,128)S(1)}, f32[3080,128]{1,0:T(8,128)S(1)}, u32[]{:S(2)}, u32[]{:S(2)}) %collective-permute-start.9) | collective-permute-done | bytes 1576992 | tf_op jit(solution)/shard_map/second/ppermute | solution.py:216
  39.3 5.6 %shard_map.49 = f32[8,128,128]{2,1,0:T(8,128)S(1)} custom-call(s32[1032]{0:T(1024)S(1)} %broadcast_1_refs_0_.2.refs_0_, f32[776,128]{1,0:T(8,128)S(1)} %collective-permute-done.refs_1_.refs_9_, f32[776,128]{1,0:T(8,128)S(1)} %collective-permute-done.1.refs_2_.refs_10_, f32[776,128]{1,0:T(8,128)S(1)} %collective-permute-done.2.refs_3_.refs_11_, ...), custom_call_target="tpu_custom_call" | custom-call | flops 2415919104 | bytes 4194304 | tf_op jit(solution)/shard_map/pallas_call | solution.py:124
  44.9 2.1 %collective-permute-start.10 = (f32[8,128,128]{2,1,0:T(8,128)S(1)}, f32[8,128,128]{2,1,0:T(8,128)S(1)}, u32[]{:S(2)}, u32[]{:S(2)}) collective-permute-start(f32[8,128,128]{2,1,0:T(8,128)S(1)} %shard_map.49), channel_id=1, source_target_pairs={{0,2},{4,6},{8,10},{12,14},{16,18},{20,22},{24,26},{28,30},{1,3},{... | collective-permute-start | bytes 1572872 | tf_op jit(solution)/shard_map/window_1/ppermute | solution.py:216
  47.0 2.9 %shard_map.47.refs_10_ = f32[8,128,128]{2,1,0:T(8,128)S(1)} custom-call(s32[1032]{0:T(1024)S(1)} %broadcast_1_refs_0_.2.refs_0_, f32[776,128]{1,0:T(8,128)S(1)} %collective-permute-done.refs_1_.refs_9_, f32[776,128]{1,0:T(8,128)S(1)} %collective-permute-done.1.refs_2_.refs_10_, f32[776,128]{1,0:T(8,128)S(1)} %collective-permute-done.2.refs_3_.refs_11_, ...), custom_call_target="tpu_custom_call" | custom-call | flops 1207959552 | bytes 4194304 | tf_op jit(solution)/shard_map/pallas_call | solution.py:124
  50.0 3.0 %shard_map.48 = f32[8,128,128]{2,1,0:T(8,128)S(1)} custom-call(s32[1032]{0:T(1024)S(1)} %broadcast_1_refs_0_.2.refs_0_, f32[776,128]{1,0:T(8,128)S(1)} %collective-permute-done.refs_1_.refs_9_, f32[776,128]{1,0:T(8,128)S(1)} %collective-permute-done.1.refs_2_.refs_10_, f32[776,128]{1,0:T(8,128)S(1)} %collective-permute-done.2.refs_3_.refs_11_, ...), custom_call_target="tpu_custom_call" | custom-call | flops 1207959552 | bytes 4194304 | tf_op jit(solution)/shard_map/pallas_call | solution.py:124
  53.0 6.2 %collective-permute-done.10 = f32[8,128,128]{2,1,0:T(8,128)S(1)} collective-permute-done((f32[8,128,128]{2,1,0:T(8,128)S(1)}, f32[8,128,128]{2,1,0:T(8,128)S(1)}, u32[]{:S(2)}, u32[]{:S(2)}) %collective-permute-start.10) | collective-permute-done | bytes 524320 | tf_op jit(solution)/shard_map/window_1/ppermute | solution.py:216
  59.2 0.8 %add.3 = f32[8,128,128]{2,1,0:T(8,128)} add(f32[8,128,128]{2,1,0:T(8,128)S(1)} %shard_map.48, f32[8,128,128]{2,1,0:T(8,128)S(1)} %collective-permute-done.10) | non-fusion elementwise | flops 131072 | bytes 1572864 | tf_op jit(solution)/shard_map/add | solution.py:244
  (1 shorter events, 0.0 us)
Async XLA Ops:
  1.8 37.5 %collective-permute-start.9 = (f32[3080,128]{1,0:T(8,128)S(1)}, f32[3080,128]{1,0:T(8,128)S(1)}, u32[]{:S(2)}, u32[]{:S(2)}) collective-permute-start(f32[3080,128]{1,0:T(8,128)S(1)} %get-tuple-element.8.refs_9_.refs_17_), channel_id=1, source_target_pairs={{0,1},{4,5},{8,9},{12,13},{16,17},{20,21},{24,25},{28,29},{1,0},{5... | collective-permute-start | bytes 4730888 | tf_op jit(solution)/shard_map/second/ppermute | solution.py:216
  4.8 20.2 %collective-permute-start.4 = (f32[776,128]{1,0:T(8,128)S(1)}, f32[776,128]{1,0:T(8,128)S(1)}, u32[]{:S(2)}, u32[]{:S(2)}) collective-permute-start(f32[776,128]{1,0:T(8,128)S(1)} %get-tuple-element.7), channel_id=1, source_target_pairs={{0,16},{4,20},{8,24},{12,28},{16,0},{20,4},{24,8},{28,12},{1,17},{... | collective-permute-start | bytes 1191944 | tf_op jit(solution)/shard_map/far/ppermute | solution.py:216
  7.4 18.8 %collective-permute-start.2 = (f32[776,128]{1,0:T(8,128)S(1)}, f32[776,128]{1,0:T(8,128)S(1)}, u32[]{:S(2)}, u32[]{:S(2)}) collective-permute-start(f32[776,128]{1,0:T(8,128)S(1)} %get-tuple-element.7), channel_id=1, source_target_pairs={{0,8},{4,12},{8,10},{12,14},{16,24},{20,28},{24,26},{28,30},{1,9},... | collective-permute-start | bytes 1191944 | tf_op jit(solution)/shard_map/share_0_1/ppermute | solution.py:216
  9.0 17.4 %collective-permute-start = (f32[776,128]{1,0:T(8,128)S(1)}, f32[776,128]{1,0:T(8,128)S(1)}, u32[]{:S(2)}, u32[]{:S(2)}) collective-permute-start(f32[776,128]{1,0:T(8,128)S(1)} %get-tuple-element.7), channel_id=1, source_target_pairs={{0,0},{4,4},{8,2},{12,6},{16,16},{20,20},{24,18},{28,22},{1,1},{5,... | collective-permute-start | bytes 1191944 | tf_op jit(solution)/shard_map/share_0_0/ppermute | solution.py:216
  25.0 10.0 %collective-permute-start.7 = (f32[776,128]{1,0:T(8,128)S(1)}, f32[776,128]{1,0:T(8,128)S(1)}, u32[]{:S(2)}, u32[]{:S(2)}) collective-permute-start(f32[776,128]{1,0:T(8,128)S(1)} %collective-permute-done.4), channel_id=1, source_target_pairs={{0,8},{4,12},{8,10},{12,14},{16,24},{20,28},{24,26},{28,30},{1,9},... | collective-permute-start | bytes 1191944 | tf_op jit(solution)/shard_map/share_1_1/ppermute | solution.py:216
  25.6 9.4 %collective-permute-start.5 = (f32[776,128]{1,0:T(8,128)S(1)}, f32[776,128]{1,0:T(8,128)S(1)}, u32[]{:S(2)}, u32[]{:S(2)}) collective-permute-start(f32[776,128]{1,0:T(8,128)S(1)} %collective-permute-done.4), channel_id=1, source_target_pairs={{0,0},{4,4},{8,2},{12,6},{16,16},{20,20},{24,18},{28,22},{1,1},{5,... | collective-permute-start | bytes 1191944 | tf_op jit(solution)/shard_map/share_1_0/ppermute | solution.py:216
  26.3 9.3 %collective-permute-start.3 = (f32[776,128]{1,0:T(8,128)S(1)}, f32[776,128]{1,0:T(8,128)S(1)}, u32[]{:S(2)}, u32[]{:S(2)}) collective-permute-start(f32[776,128]{1,0:T(8,128)S(1)} %collective-permute-done.2.refs_3_.refs_11_), channel_id=1, source_target_pairs={{0,4},{4,0},{8,12},{12,8},{16,20},{20,16},{24,28},{28,24},{1,5},{5... | collective-permute-start | bytes 1191944 | tf_op jit(solution)/shard_map/swap_0/ppermute | solution.py:216
  26.4 9.2 %collective-permute-start.1 = (f32[776,128]{1,0:T(8,128)S(1)}, f32[776,128]{1,0:T(8,128)S(1)}, u32[]{:S(2)}, u32[]{:S(2)}) collective-permute-start(f32[776,128]{1,0:T(8,128)S(1)} %collective-permute-done.refs_1_.refs_9_), channel_id=1, source_target_pairs={{0,4},{4,0},{8,12},{12,8},{16,20},{20,16},{24,28},{28,24},{1,5},{5... | collective-permute-start | bytes 1191944 | tf_op jit(solution)/shard_map/swap_0/ppermute | solution.py:216
  35.0 1.7 %collective-permute-start.8 = (f32[776,128]{1,0:T(8,128)S(1)}, f32[776,128]{1,0:T(8,128)S(1)}, u32[]{:S(2)}, u32[]{:S(2)}) collective-permute-start(f32[776,128]{1,0:T(8,128)S(1)} %collective-permute-done.7.refs_7_.refs_15_), channel_id=1, source_target_pairs={{0,4},{4,0},{8,12},{12,8},{16,20},{20,16},{24,28},{28,24},{1,5},{5... | collective-permute-start | bytes 1191944 | tf_op jit(solution)/shard_map/swap_1/ppermute | solution.py:216
  35.0 2.3 %collective-permute-start.6 = (f32[776,128]{1,0:T(8,128)S(1)}, f32[776,128]{1,0:T(8,128)S(1)}, u32[]{:S(2)}, u32[]{:S(2)}) collective-permute-start(f32[776,128]{1,0:T(8,128)S(1)} %collective-permute-done.5.refs_5_.refs_13_), channel_id=1, source_target_pairs={{0,4},{4,0},{8,12},{12,8},{16,20},{20,16},{24,28},{28,24},{1,5},{5... | collective-permute-start | bytes 1191944 | tf_op jit(solution)/shard_map/swap_1/ppermute | solution.py:216
  44.9 14.3 %collective-permute-start.10 = (f32[8,128,128]{2,1,0:T(8,128)S(1)}, f32[8,128,128]{2,1,0:T(8,128)S(1)}, u32[]{:S(2)}, u32[]{:S(2)}) collective-permute-start(f32[8,128,128]{2,1,0:T(8,128)S(1)} %shard_map.49), channel_id=1, source_target_pairs={{0,2},{4,6},{8,10},{12,14},{16,18},{20,22},{24,26},{28,30},{1,3},{... | collective-permute-start | bytes 1572872 | tf_op jit(solution)/shard_map/window_1/ppermute | solution.py:216

commit v6 on v5

--- a/solution.py
+++ b/solution.py
@@ -236,7 +236,8 @@
     seconds = (second, second_other)
     received = []
     for change in range(1, groups):
-        value = product(narrow, wide, change, (0, 0, 1, 1), candidates * 2, seconds)
+        value = product(narrow, wide, change, (0,), candidates[:1], seconds)
+        value = product(narrow, wide, change, (0, 1, 1), [candidates[1], *candidates], seconds, value)
         received.append(permute(f"window_{change}", value, lambda r, c: (r ^ (change * 2), c)))
     total = product(narrow, wide, 0, (0, 0), candidates, seconds)
     total = product(narrow, wide, 0, (1, 1), candidates, seconds, total)

time: 61 us -> 60 us (0.984); the launches traced: 60.1 us -> 59.8 us
  waiting for transfers between devices: 33.5 us -> 26.9 us
  starting transfers between devices: 12.3 us -> 17.9 us
  Pallas kernels: 13.3 us -> 14 us
    ppermute x11, waiting for transfers between devices: 33.5 us -> 26.9 us  [permute(): return lax.ppermute(value, AXES, pairs)]
    ppermute x11, starting transfers between devices: 12.3 us -> 17.9 us  [permute(): return lax.ppermute(value, AXES, pairs)]
    pallas_call x3 -> x4, Pallas kernels: 11.5 us -> 12.2 us  [product(): pl.pallas_call(functools.partial(product_kernel, edge, slots, narrow, wid...]
  transfers between devices with their start and end apart: 11 -> 11, of which waited for: 6 -> 3; matrix products, arithmetic and copies ran while one was open for 0% -> 0% of each run, Pallas kernels for 10% -> 13%
where the time goes in v6:
time: 60 us; the launch traced here: 59.8 us
  waiting for transfers between devices  26.9 us (45%)
  starting transfers between devices  17.9 us (30%)
  Pallas kernels  14 us (23%)
  other arithmetic  0.85 us (1%)
    ppermute x11, waiting for transfers between devices, permute(): return lax.ppermute(value, AXES, pairs)  26.9 us
    ppermute x11, starting transfers between devices, permute(): return lax.ppermute(value, AXES, pairs)  17.9 us
    pallas_call x4, Pallas kernels, product(): pl.pallas_call(functools.partial(product_kernel, edge, slots, narrow, wid...  12.2 us
    pallas_call x1, Pallas kernels, build_shares(): pl.pallas_call(share_kernel, out_shape=tuple((jax.ShapeDtypeStruct((value...  1.83 us
  transfers between devices with their start and end apart: 11, of which 3 were waited for; matrix products, arithmetic and copies ran while one was open for 0% of the time, Pallas kernels for 13%

profile of v6, /device:TPU:0, one launch (start us, length us, event | category | flops | bytes accessed | tf_op | source)
XLA Modules:
  0.0 59.8 jit_solution(13060069537827529515)
XLA Ops:
  0.0 1.8 %shard_map.46 = (f32[776,128]{1,0:T(8,128)S(1)}, f32[3080,128]{1,0:T(8,128)S(1)}) custom-call(f32[6,128,128]{2,1,0:T(8,128)} %bitcast.6, f32[24,128,128]{2,1,0:T(8,128)} %bitcast.5, s32[1,2,6]{2,1,0:T(2,128)} %refs_2_.1, s32[1,2,24]{2,1,0:T(2,128)} %refs_3_.1), custom_call_target="tpu_custom_call" | custom-call | tf_op jit(solution)/shard_map/pallas_call | solution.py:185
  1.8 3.0 %collective-permute-start.9 = (f32[3080,128]{1,0:T(8,128)S(1)}, f32[3080,128]{1,0:T(8,128)S(1)}, u32[]{:S(2)}, u32[]{:S(2)}) collective-permute-start(f32[3080,128]{1,0:T(8,128)S(1)} %get-tuple-element.8.refs_9_.refs_5_.refs_13_), channel_id=1, source_target_pairs={{0,1},{4,5},{8,9},{12,13},{16,17},{20,21},{24,25},{28,29},{1,0},{5... | collective-permute-start | bytes 4730888 | tf_op jit(solution)/shard_map/second/ppermute | solution.py:216
  4.8 2.6 %collective-permute-start.4 = (f32[776,128]{1,0:T(8,128)S(1)}, f32[776,128]{1,0:T(8,128)S(1)}, u32[]{:S(2)}, u32[]{:S(2)}) collective-permute-start(f32[776,128]{1,0:T(8,128)S(1)} %get-tuple-element.7), channel_id=1, source_target_pairs={{0,16},{4,20},{8,24},{12,28},{16,0},{20,4},{24,8},{28,12},{1,17},{... | collective-permute-start | bytes 1191944 | tf_op jit(solution)/shard_map/far/ppermute | solution.py:216
  7.4 0.7 %collective-permute-start = (f32[776,128]{1,0:T(8,128)S(1)}, f32[776,128]{1,0:T(8,128)S(1)}, u32[]{:S(2)}, u32[]{:S(2)}) collective-permute-start(f32[776,128]{1,0:T(8,128)S(1)} %get-tuple-element.7), channel_id=1, source_target_pairs={{0,0},{4,4},{8,2},{12,6},{16,16},{20,20},{24,18},{28,22},{1,1},{5,... | collective-permute-start | bytes 1191944 | tf_op jit(solution)/shard_map/share_0_0/ppermute | solution.py:216
  8.1 4.3 %collective-permute-start.2 = (f32[776,128]{1,0:T(8,128)S(1)}, f32[776,128]{1,0:T(8,128)S(1)}, u32[]{:S(2)}, u32[]{:S(2)}) collective-permute-start(f32[776,128]{1,0:T(8,128)S(1)} %get-tuple-element.7), channel_id=1, source_target_pairs={{0,8},{4,12},{8,10},{12,14},{16,24},{20,28},{24,26},{28,30},{1,9},... | collective-permute-start | bytes 1191944 | tf_op jit(solution)/shard_map/share_0_1/ppermute | solution.py:216
  12.4 12.6 %collective-permute-done.4 = f32[776,128]{1,0:T(8,128)S(1)} collective-permute-done((f32[776,128]{1,0:T(8,128)S(1)}, f32[776,128]{1,0:T(8,128)S(1)}, u32[]{:S(2)}, u32[]{:S(2)}) %collective-permute-start.4) | collective-permute-done | bytes 397344 | tf_op jit(solution)/shard_map/far/ppermute | solution.py:216
  25.0 0.7 %collective-permute-start.5 = (f32[776,128]{1,0:T(8,128)S(1)}, f32[776,128]{1,0:T(8,128)S(1)}, u32[]{:S(2)}, u32[]{:S(2)}) collective-permute-start(f32[776,128]{1,0:T(8,128)S(1)} %collective-permute-done.4), channel_id=1, source_target_pairs={{0,0},{4,4},{8,2},{12,6},{16,16},{20,20},{24,18},{28,22},{1,1},{5,... | collective-permute-start | bytes 1191944 | tf_op jit(solution)/shard_map/share_1_0/ppermute | solution.py:216
  25.7 4.3 %collective-permute-start.7 = (f32[776,128]{1,0:T(8,128)S(1)}, f32[776,128]{1,0:T(8,128)S(1)}, u32[]{:S(2)}, u32[]{:S(2)}) collective-permute-start(f32[776,128]{1,0:T(8,128)S(1)} %collective-permute-done.4), channel_id=1, source_target_pairs={{0,8},{4,12},{8,10},{12,14},{16,24},{20,28},{24,26},{28,30},{1,9},... | collective-permute-start | bytes 1191944 | tf_op jit(solution)/shard_map/share_1_1/ppermute | solution.py:216
  30.0 0.0 collective-permute-done.refs_1_.refs_5_
  30.0 0.0 collective-permute-start.1
  30.0 0.0 collective-permute-done.2.refs_3_.refs_7_
  30.0 0.5 collective-permute-start.3
  30.5 0.0 collective-permute-done.5.refs_5_.refs_1_.refs_9_
  30.5 0.1 collective-permute-start.6
  30.6 7.6 %collective-permute-done.7.refs_7_.refs_3_.refs_11_ = f32[776,128]{1,0:T(8,128)S(1)} collective-permute-done((f32[776,128]{1,0:T(8,128)S(1)}, f32[776,128]{1,0:T(8,128)S(1)}, u32[]{:S(2)}, u32[]{:S(2)}) %collective-permute-start.7) | collective-permute-done | bytes 397344 | tf_op jit(solution)/shard_map/share_1_1/ppermute | solution.py:216
  38.2 0.0 collective-permute-start.8
  38.2 0.0 collective-permute-done.1.refs_2_.refs_6_
  38.2 0.0 collective-permute-done.3.refs_4_.refs_8_
  38.2 2.0 %shard_map.49.refs_15_ = f32[8,128,128]{2,1,0:T(8,128)S(1)} custom-call(s32[1032]{0:T(1024)S(1)} %broadcast_1_refs_0_.2.refs_0_, f32[776,128]{1,0:T(8,128)S(1)} %collective-permute-done.refs_1_.refs_5_, f32[776,128]{1,0:T(8,128)S(1)} %collective-permute-done.1.refs_2_.refs_6_, f32[776,128]{1,0:T(8,128)S(1)} %collective-permute-done.2.refs_3_.refs_7_, ...), custom_call_target="tpu_custom_call" | custom-call | flops 603979776 | bytes 4194304 | tf_op jit(solution)/shard_map/pallas_call | solution.py:124
  40.2 0.0 collective-permute-done.6.refs_6_.refs_2_.refs_10_
  40.2 0.0 collective-permute-done.8.refs_8_.refs_4_.refs_12_
  40.2 0.0 collective-permute-done.9.refs_9_.refs_14_
  40.2 4.3 %shard_map.50 = f32[8,128,128]{2,1,0:T(8,128)S(1)} custom-call(s32[1032]{0:T(1024)S(1)} %broadcast_1_refs_0_.2.refs_0_, f32[776,128]{1,0:T(8,128)S(1)} %collective-permute-done.5.refs_5_.refs_1_.refs_9_, f32[776,128]{1,0:T(8,128)S(1)} %collective-permute-done.6.refs_6_.refs_2_.refs_10_, f32[776,128]{1,0:T(8,128)S(1)} %collective-permute-done.7.refs_7_.refs_3_.refs_11_, ...), custom_call_target="tpu_custom_call" | custom-call | flops 1811939328 | bytes 4194304 | tf_op jit(solution)/shard_map/pallas_call | solution.py:124
  44.5 1.8 %collective-permute-start.10 = (f32[8,128,128]{2,1,0:T(8,128)S(1)}, f32[8,128,128]{2,1,0:T(8,128)S(1)}, u32[]{:S(2)}, u32[]{:S(2)}) collective-permute-start(f32[8,128,128]{2,1,0:T(8,128)S(1)} %shard_map.50), channel_id=1, source_target_pairs={{0,2},{4,6},{8,10},{12,14},{16,18},{20,22},{24,26},{28,30},{1,3},{... | collective-permute-start | bytes 1572872 | tf_op jit(solution)/shard_map/window_1/ppermute | solution.py:216
  46.3 2.9 %shard_map.47.refs_10_ = f32[8,128,128]{2,1,0:T(8,128)S(1)} custom-call(s32[1032]{0:T(1024)S(1)} %broadcast_1_refs_0_.2.refs_0_, f32[776,128]{1,0:T(8,128)S(1)} %collective-permute-done.refs_1_.refs_5_, f32[776,128]{1,0:T(8,128)S(1)} %collective-permute-done.1.refs_2_.refs_6_, f32[776,128]{1,0:T(8,128)S(1)} %collective-permute-done.2.refs_3_.refs_7_, ...), custom_call_target="tpu_custom_call" | custom-call | flops 1207959552 | bytes 4194304 | tf_op jit(solution)/shard_map/pallas_call | solution.py:124
  49.3 3.0 %shard_map.48 = f32[8,128,128]{2,1,0:T(8,128)S(1)} custom-call(s32[1032]{0:T(1024)S(1)} %broadcast_1_refs_0_.2.refs_0_, f32[776,128]{1,0:T(8,128)S(1)} %collective-permute-done.refs_1_.refs_5_, f32[776,128]{1,0:T(8,128)S(1)} %collective-permute-done.1.refs_2_.refs_6_, f32[776,128]{1,0:T(8,128)S(1)} %collective-permute-done.2.refs_3_.refs_7_, ...), custom_call_target="tpu_custom_call" | custom-call | flops 1207959552 | bytes 4194304 | tf_op jit(solution)/shard_map/pallas_call | solution.py:124
  52.3 6.7 %collective-permute-done.10 = f32[8,128,128]{2,1,0:T(8,128)S(1)} collective-permute-done((f32[8,128,128]{2,1,0:T(8,128)S(1)}, f32[8,128,128]{2,1,0:T(8,128)S(1)}, u32[]{:S(2)}, u32[]{:S(2)}) %collective-permute-start.10) | collective-permute-done | bytes 524320 | tf_op jit(solution)/shard_map/window_1/ppermute | solution.py:216
  58.9 0.8 %add.3 = f32[8,128,128]{2,1,0:T(8,128)} add(f32[8,128,128]{2,1,0:T(8,128)S(1)} %shard_map.48, f32[8,128,128]{2,1,0:T(8,128)S(1)} %collective-permute-done.10) | non-fusion elementwise | flops 131072 | bytes 1572864 | tf_op jit(solution)/shard_map/add | solution.py:245
  (1 shorter events, 0.0 us)
Async XLA Ops:
  1.8 38.4 %collective-permute-start.9 = (f32[3080,128]{1,0:T(8,128)S(1)}, f32[3080,128]{1,0:T(8,128)S(1)}, u32[]{:S(2)}, u32[]{:S(2)}) collective-permute-start(f32[3080,128]{1,0:T(8,128)S(1)} %get-tuple-element.8.refs_9_.refs_5_.refs_13_), channel_id=1, source_target_pairs={{0,1},{4,5},{8,9},{12,13},{16,17},{20,21},{24,25},{28,29},{1,0},{5... | collective-permute-start | bytes 4730888 | tf_op jit(solution)/shard_map/second/ppermute | solution.py:216
  4.8 20.2 %collective-permute-start.4 = (f32[776,128]{1,0:T(8,128)S(1)}, f32[776,128]{1,0:T(8,128)S(1)}, u32[]{:S(2)}, u32[]{:S(2)}) collective-permute-start(f32[776,128]{1,0:T(8,128)S(1)} %get-tuple-element.7), channel_id=1, source_target_pairs={{0,16},{4,20},{8,24},{12,28},{16,0},{20,4},{24,8},{28,12},{1,17},{... | collective-permute-start | bytes 1191944 | tf_op jit(solution)/shard_map/far/ppermute | solution.py:216
  7.4 22.5 %collective-permute-start = (f32[776,128]{1,0:T(8,128)S(1)}, f32[776,128]{1,0:T(8,128)S(1)}, u32[]{:S(2)}, u32[]{:S(2)}) collective-permute-start(f32[776,128]{1,0:T(8,128)S(1)} %get-tuple-element.7), channel_id=1, source_target_pairs={{0,0},{4,4},{8,2},{12,6},{16,16},{20,20},{24,18},{28,22},{1,1},{5,... | collective-permute-start | bytes 1191944 | tf_op jit(solution)/shard_map/share_0_0/ppermute | solution.py:216
  8.1 21.9 %collective-permute-start.2 = (f32[776,128]{1,0:T(8,128)S(1)}, f32[776,128]{1,0:T(8,128)S(1)}, u32[]{:S(2)}, u32[]{:S(2)}) collective-permute-start(f32[776,128]{1,0:T(8,128)S(1)} %get-tuple-element.7), channel_id=1, source_target_pairs={{0,8},{4,12},{8,10},{12,14},{16,24},{20,28},{24,26},{28,30},{1,9},... | collective-permute-start | bytes 1191944 | tf_op jit(solution)/shard_map/share_0_1/ppermute | solution.py:216
  25.0 5.5 %collective-permute-start.5 = (f32[776,128]{1,0:T(8,128)S(1)}, f32[776,128]{1,0:T(8,128)S(1)}, u32[]{:S(2)}, u32[]{:S(2)}) collective-permute-start(f32[776,128]{1,0:T(8,128)S(1)} %collective-permute-done.4), channel_id=1, source_target_pairs={{0,0},{4,4},{8,2},{12,6},{16,16},{20,20},{24,18},{28,22},{1,1},{5,... | collective-permute-start | bytes 1191944 | tf_op jit(solution)/shard_map/share_1_0/ppermute | solution.py:216
  25.7 12.5 %collective-permute-start.7 = (f32[776,128]{1,0:T(8,128)S(1)}, f32[776,128]{1,0:T(8,128)S(1)}, u32[]{:S(2)}, u32[]{:S(2)}) collective-permute-start(f32[776,128]{1,0:T(8,128)S(1)} %collective-permute-done.4), channel_id=1, source_target_pairs={{0,8},{4,12},{8,10},{12,14},{16,24},{20,28},{24,26},{28,30},{1,9},... | collective-permute-start | bytes 1191944 | tf_op jit(solution)/shard_map/share_1_1/ppermute | solution.py:216
  30.0 8.2 %collective-permute-start.1 = (f32[776,128]{1,0:T(8,128)S(1)}, f32[776,128]{1,0:T(8,128)S(1)}, u32[]{:S(2)}, u32[]{:S(2)}) collective-permute-start(f32[776,128]{1,0:T(8,128)S(1)} %collective-permute-done.refs_1_.refs_5_), channel_id=1, source_target_pairs={{0,4},{4,0},{8,12},{12,8},{16,20},{20,16},{24,28},{28,24},{1,5},{5... | collective-permute-start | bytes 1191944 | tf_op jit(solution)/shard_map/swap_0/ppermute | solution.py:216
  30.0 8.2 %collective-permute-start.3 = (f32[776,128]{1,0:T(8,128)S(1)}, f32[776,128]{1,0:T(8,128)S(1)}, u32[]{:S(2)}, u32[]{:S(2)}) collective-permute-start(f32[776,128]{1,0:T(8,128)S(1)} %collective-permute-done.2.refs_3_.refs_7_), channel_id=1, source_target_pairs={{0,4},{4,0},{8,12},{12,8},{16,20},{20,16},{24,28},{28,24},{1,5},{5... | collective-permute-start | bytes 1191944 | tf_op jit(solution)/shard_map/swap_0/ppermute | solution.py:216
  30.5 9.7 %collective-permute-start.6 = (f32[776,128]{1,0:T(8,128)S(1)}, f32[776,128]{1,0:T(8,128)S(1)}, u32[]{:S(2)}, u32[]{:S(2)}) collective-permute-start(f32[776,128]{1,0:T(8,128)S(1)} %collective-permute-done.5.refs_5_.refs_1_.refs_9_), channel_id=1, source_target_pairs={{0,4},{4,0},{8,12},{12,8},{16,20},{20,16},{24,28},{28,24},{1,5},{5... | collective-permute-start | bytes 1191944 | tf_op jit(solution)/shard_map/swap_1/ppermute | solution.py:216
  38.2 2.0 %collective-permute-start.8 = (f32[776,128]{1,0:T(8,128)S(1)}, f32[776,128]{1,0:T(8,128)S(1)}, u32[]{:S(2)}, u32[]{:S(2)}) collective-permute-start(f32[776,128]{1,0:T(8,128)S(1)} %collective-permute-done.7.refs_7_.refs_3_.refs_11_), channel_id=1, source_target_pairs={{0,4},{4,0},{8,12},{12,8},{16,20},{20,16},{24,28},{28,24},{1,5},{5... | collective-permute-start | bytes 1191944 | tf_op jit(solution)/shard_map/swap_1/ppermute | solution.py:216
  44.5 14.4 %collective-permute-start.10 = (f32[8,128,128]{2,1,0:T(8,128)S(1)}, f32[8,128,128]{2,1,0:T(8,128)S(1)}, u32[]{:S(2)}, u32[]{:S(2)}) collective-permute-start(f32[8,128,128]{2,1,0:T(8,128)S(1)} %shard_map.50), channel_id=1, source_target_pairs={{0,2},{4,6},{8,10},{12,14},{16,18},{20,22},{24,26},{28,30},{1,3},{... | collective-permute-start | bytes 1572872 | tf_op jit(solution)/shard_map/window_1/ppermute | solution.py:216

commit v7 on v5

--- a/solution.py
+++ b/solution.py
@@ -21,7 +21,8 @@
     return high, low
 
 
-def product_kernel(edge, slots, narrow, wide, change, choices, crossings, has_start, *refs):
+def product_kernel(edge, slots, narrow, wide, change, choices, crossings, outer, has_start, *refs):
+    width = len(outer)
     items = len(crossings)
     classes = sorted(set(crossings))
     empty_ref, refs = refs[0], refs[1:]
@@ -66,25 +67,25 @@
     for crossing in classes:
         for slot in range(slots_second):
             inner = second_index[crossing, 0, slot].astype(jnp.int32)
-            outer = second_index[crossing, 1, slot].astype(jnp.int32)
-            place = lax.div(jnp.maximum(inner, 0), narrow) * CL + lax.div(jnp.maximum(outer, 0), wide)
+            across = second_index[crossing, 1, slot].astype(jnp.int32)
+            place = lax.div(jnp.maximum(inner, 0), narrow) * CL + lax.div(jnp.maximum(across, 0), wide)
             tables[crossing, jnp.where(inner < 0, (KBLOCKS // narrow + 1) * CL, place)] = slot
     waits = [copies(n, shares[n][0]) for n in range(items)]
     for index_copy, _ in waits:
         index_copy.wait()
+    for _, block_copy in waits:
+        block_copy.wait()
     for n, crossing in enumerate(crossings):
         for slot in range(slots):
             at = (n * slots + slot) * edge
             inner = index_ref[n, 1, slot].astype(jnp.int32)
             inner = jnp.where(inner < 0, KBLOCKS // narrow, lax.div(jnp.maximum(inner, 0), narrow))
-            for m in range(CL):
+            for at_column, m in enumerate(outer):
                 block = tables[crossing, inner * CL + m]
                 source = pl.ds(pl.multiple_of(jnp.minimum(block, slots_second - 1) * edge, edge), edge)
                 high, low = split(jnp.where(block < slots_second, second_refs[crossing][source, :], 0.0))
-                right_high[at : at + edge, m * edge : (m + 1) * edge] = high
-                right_low[at : at + edge, m * edge : (m + 1) * edge] = low
-    for _, block_copy in waits:
-        block_copy.wait()
+                right_high[at : at + edge, at_column * edge : (at_column + 1) * edge] = high
+                right_low[at : at + edge, at_column * edge : (at_column + 1) * edge] = low
     for n in range(items):
         for slot in range(slots):
             at = (n * slots + slot) * edge
@@ -94,7 +95,7 @@
             left_high[target, at : at + edge] = high
             left_low[target, at : at + edge] = low
     dot = functools.partial(jnp.dot, preferred_element_type=jnp.float32)
-    for m in range(0, CL, 2):
+    for m in range(0, width, 2):
         columns = slice(m * edge, (m + 2) * edge)
         value = (
             dot(left_high[...], right_high[:, columns])
@@ -103,12 +104,12 @@
         )
         for l in range(RL):
             for k in range(2):
-                at = l * CL + m + k
+                at = l * width + m + k
                 piece = value[l * edge : (l + 1) * edge, k * edge : (k + 1) * edge]
-                out_ref[at] = start_ref[at] + piece if has_start else piece
-
-
-def product(narrow, wide, change, crossings, shares, seconds, start=None):
+                out_ref[at] = start_ref[l * CL + outer[m + k]] + piece if has_start else piece
+
+
+def product(narrow, wide, change, crossings, shares, seconds, start=None, outer=tuple(range(CL))):
     edge = shares[0][0].shape[1]
     items = len(shares)
     choices = len(shares[0])
@@ -122,8 +123,8 @@
     if start is not None:
         operands.append(start)
     return pl.pallas_call(
-        functools.partial(product_kernel, edge, slots, narrow, wide, change, choices, crossings, start is not None),
-        out_shape=jax.ShapeDtypeStruct((RL * CL, edge, edge), jnp.float32),
+        functools.partial(product_kernel, edge, slots, narrow, wide, change, choices, crossings, outer, start is not None),
+        out_shape=jax.ShapeDtypeStruct((RL * len(outer), edge, edge), jnp.float32),
         in_specs=[anywhere] * (1 + items * choices) + [whole] * len(operands),
         out_specs=whole,
         scratch_shapes=[
@@ -133,8 +134,8 @@
             pltpu.SMEM((2, places), jnp.int32),
             pltpu.VMEM((RL * edge, depth), jnp.bfloat16),
             pltpu.VMEM((RL * edge, depth), jnp.bfloat16),
-            pltpu.VMEM((depth, CL * edge), jnp.bfloat16),
-            pltpu.VMEM((depth, CL * edge), jnp.bfloat16),
+            pltpu.VMEM((depth, len(outer) * edge), jnp.bfloat16),
+            pltpu.VMEM((depth, len(outer) * edge), jnp.bfloat16),
             pltpu.SemaphoreType.DMA((items,)),
             pltpu.SemaphoreType.DMA((items,)),
             pltpu.SemaphoreType.DMA((2,)),
@@ -142,7 +143,7 @@
         ],
         compiler_params=pltpu.CompilerParams(vmem_limit_bytes=VMEM_LIMIT),
         cost_estimate=pl.CostEstimate(
-            flops=6 * RL * depth * CL * edge * edge, bytes_accessed=4 * 1024 * 1024, transcendentals=0
+            flops=6 * RL * depth * len(outer) * edge * edge, bytes_accessed=4 * 1024 * 1024, transcendentals=0
         ),
     )(empty, *[ref for share in shares for ref in share], *operands)
 
@@ -236,10 +237,15 @@
     seconds = (second, second_other)
     received = []
     for change in range(1, groups):
-        value = product(narrow, wide, change, (0, 0, 1, 1), candidates * 2, seconds)
-        received.append(permute(f"window_{change}", value, lambda r, c: (r ^ (change * 2), c)))
+        start = product(narrow, wide, change, (0,), candidates[:1], seconds)
+        pieces = []
+        for outer in (tuple(range(CL // 2)), tuple(range(CL // 2, CL))):
+            value = product(narrow, wide, change, (0, 1, 1), [candidates[1], *candidates], seconds, start, outer)
+            got = permute(f"window_{change}", value, lambda r, c: (r ^ (change * 2), c))
+            pieces.append(got.reshape(RL, len(outer), edge, edge))
+        received.append(jnp.concatenate(pieces, axis=1))
     total = product(narrow, wide, 0, (0, 0), candidates, seconds)
-    total = product(narrow, wide, 0, (1, 1), candidates, seconds, total)
+    total = product(narrow, wide, 0, (1, 1), candidates, seconds, total).reshape(RL, CL, edge, edge)
     for value in received:
         total = total + value
     return total.reshape(1, RL, 1, CL, edge, edge)

time: 61 us -> 58.6 us (0.961); the launches traced: 60.1 us -> 58.4 us
  waiting for transfers between devices: 33.5 us -> 24 us
  starting transfers between devices: 12.3 us -> 18.2 us
  Pallas kernels: 13.3 us -> 15.3 us
    ppermute x11 -> x12, waiting for transfers between devices: 33.5 us -> 24 us  [permute(): return lax.ppermute(value, AXES, pairs)]
    ppermute x11 -> x12, starting transfers between devices: 12.3 us -> 18.2 us  [permute(): return lax.ppermute(value, AXES, pairs)]
    pallas_call x3 -> x5, Pallas kernels: 11.5 us -> 13.4 us  [product(): pl.pallas_call(functools.partial(product_kernel, edge, slots, narrow, wid...]
  transfers between devices with their start and end apart: 11 -> 12, of which waited for: 6 -> 3; matrix products, arithmetic and copies ran while one was open for 0% -> 0% of each run, Pallas kernels for 10% -> 18%
where the time goes in v7:
time: 58.6 us; the launch traced here: 58.4 us
  waiting for transfers between devices  24 us (41%)
  starting transfers between devices  18.2 us (31%)
  Pallas kernels  15.3 us (26%)
  other arithmetic  0.86 us (1%)
    ppermute x12, waiting for transfers between devices, permute(): return lax.ppermute(value, AXES, pairs)  24 us
    ppermute x12, starting transfers between devices, permute(): return lax.ppermute(value, AXES, pairs)  18.2 us
    pallas_call x5, Pallas kernels, product(): pl.pallas_call(functools.partial(product_kernel, edge, slots, narrow, wid...  13.4 us
    pallas_call x1, Pallas kernels, build_shares(): pl.pallas_call(share_kernel, out_shape=tuple((jax.ShapeDtypeStruct((value...  1.83 us
  transfers between devices with their start and end apart: 12, of which 3 were waited for; matrix products, arithmetic and copies ran while one was open for 0% of the time, Pallas kernels for 18%

profile of v7, /device:TPU:0, one launch (start us, length us, event | category | flops | bytes accessed | tf_op | source)
XLA Modules:
  0.0 58.4 jit_solution(5482836720579365822)
XLA Ops:
  0.0 1.8 %shard_map.46 = (f32[776,128]{1,0:T(8,128)S(1)}, f32[3080,128]{1,0:T(8,128)S(1)}) custom-call(f32[6,128,128]{2,1,0:T(8,128)} %bitcast.13, f32[24,128,128]{2,1,0:T(8,128)} %bitcast.12, s32[1,2,6]{2,1,0:T(2,128)} %refs_2_.1, s32[1,2,24]{2,1,0:T(2,128)} %refs_3_.1), custom_call_target="tpu_custom_call" | custom-call | tf_op jit(solution)/shard_map/pallas_call | solution.py:186
  1.8 3.0 %collective-permute-start.9 = (f32[3080,128]{1,0:T(8,128)S(1)}, f32[3080,128]{1,0:T(8,128)S(1)}, u32[]{:S(2)}, u32[]{:S(2)}) collective-permute-start(f32[3080,128]{1,0:T(8,128)S(1)} %get-tuple-element.8.refs_9_.refs_5_.refs_13_), channel_id=1, source_target_pairs={{0,1},{4,5},{8,9},{12,13},{16,17},{20,21},{24,25},{28,29},{1,0},{5... | collective-permute-start | bytes 4730888 | tf_op jit(solution)/shard_map/second/ppermute | solution.py:217
  4.8 2.6 %collective-permute-start.4 = (f32[776,128]{1,0:T(8,128)S(1)}, f32[776,128]{1,0:T(8,128)S(1)}, u32[]{:S(2)}, u32[]{:S(2)}) collective-permute-start(f32[776,128]{1,0:T(8,128)S(1)} %get-tuple-element.7), channel_id=1, source_target_pairs={{0,16},{4,20},{8,24},{12,28},{16,0},{20,4},{24,8},{28,12},{1,17},{... | collective-permute-start | bytes 1191944 | tf_op jit(solution)/shard_map/far/ppermute | solution.py:217
  7.4 0.7 %collective-permute-start = (f32[776,128]{1,0:T(8,128)S(1)}, f32[776,128]{1,0:T(8,128)S(1)}, u32[]{:S(2)}, u32[]{:S(2)}) collective-permute-start(f32[776,128]{1,0:T(8,128)S(1)} %get-tuple-element.7), channel_id=1, source_target_pairs={{0,0},{4,4},{8,2},{12,6},{16,16},{20,20},{24,18},{28,22},{1,1},{5,... | collective-permute-start | bytes 1191944 | tf_op jit(solution)/shard_map/share_0_0/ppermute | solution.py:217
  8.1 4.3 %collective-permute-start.2 = (f32[776,128]{1,0:T(8,128)S(1)}, f32[776,128]{1,0:T(8,128)S(1)}, u32[]{:S(2)}, u32[]{:S(2)}) collective-permute-start(f32[776,128]{1,0:T(8,128)S(1)} %get-tuple-element.7), channel_id=1, source_target_pairs={{0,8},{4,12},{8,10},{12,14},{16,24},{20,28},{24,26},{28,30},{1,9},... | collective-permute-start | bytes 1191944 | tf_op jit(solution)/shard_map/share_0_1/ppermute | solution.py:217
  12.4 12.6 %collective-permute-done.4 = f32[776,128]{1,0:T(8,128)S(1)} collective-permute-done((f32[776,128]{1,0:T(8,128)S(1)}, f32[776,128]{1,0:T(8,128)S(1)}, u32[]{:S(2)}, u32[]{:S(2)}) %collective-permute-start.4) | collective-permute-done | bytes 397344 | tf_op jit(solution)/shard_map/far/ppermute | solution.py:217
  25.0 0.7 %collective-permute-start.5 = (f32[776,128]{1,0:T(8,128)S(1)}, f32[776,128]{1,0:T(8,128)S(1)}, u32[]{:S(2)}, u32[]{:S(2)}) collective-permute-start(f32[776,128]{1,0:T(8,128)S(1)} %collective-permute-done.4), channel_id=1, source_target_pairs={{0,0},{4,4},{8,2},{12,6},{16,16},{20,20},{24,18},{28,22},{1,1},{5,... | collective-permute-start | bytes 1191944 | tf_op jit(solution)/shard_map/share_1_0/ppermute | solution.py:217
  25.7 4.3 %collective-permute-start.7 = (f32[776,128]{1,0:T(8,128)S(1)}, f32[776,128]{1,0:T(8,128)S(1)}, u32[]{:S(2)}, u32[]{:S(2)}) collective-permute-start(f32[776,128]{1,0:T(8,128)S(1)} %collective-permute-done.4), channel_id=1, source_target_pairs={{0,8},{4,12},{8,10},{12,14},{16,24},{20,28},{24,26},{28,30},{1,9},... | collective-permute-start | bytes 1191944 | tf_op jit(solution)/shard_map/share_1_1/ppermute | solution.py:217
  30.0 0.0 collective-permute-done.refs_1_.refs_5_
  30.0 0.0 collective-permute-start.1
  30.0 0.0 collective-permute-done.2.refs_3_.refs_7_
  30.0 0.5 collective-permute-start.3
  30.5 0.0 collective-permute-done.5.refs_5_.refs_1_.refs_9_
  30.5 0.1 collective-permute-start.6
  30.6 7.6 %collective-permute-done.7.refs_7_.refs_3_.refs_11_ = f32[776,128]{1,0:T(8,128)S(1)} collective-permute-done((f32[776,128]{1,0:T(8,128)S(1)}, f32[776,128]{1,0:T(8,128)S(1)}, u32[]{:S(2)}, u32[]{:S(2)}) %collective-permute-start.7) | collective-permute-done | bytes 397344 | tf_op jit(solution)/shard_map/share_1_1/ppermute | solution.py:217
  38.2 0.0 collective-permute-start.8
  38.2 0.0 collective-permute-done.1.refs_2_.refs_6_
  38.2 0.0 collective-permute-done.3.refs_4_.refs_8_
  38.2 1.9 %shard_map.49.refs_15_ = f32[8,128,128]{2,1,0:T(8,128)S(1)} custom-call(s32[1032]{0:T(1024)S(1)} %broadcast_1_refs_0_.2.refs_0_, f32[776,128]{1,0:T(8,128)S(1)} %collective-permute-done.refs_1_.refs_5_, f32[776,128]{1,0:T(8,128)S(1)} %collective-permute-done.1.refs_2_.refs_6_, f32[776,128]{1,0:T(8,128)S(1)} %collective-permute-done.2.refs_3_.refs_7_, ...), custom_call_target="tpu_custom_call" | custom-call | flops 603979776 | bytes 4194304 | tf_op jit(solution)/shard_map/pallas_call | solution.py:125
  40.1 0.0 collective-permute-done.6.refs_6_.refs_2_.refs_10_
  40.1 0.0 collective-permute-done.8.refs_8_.refs_4_.refs_12_
  40.1 0.0 collective-permute-done.9.refs_9_.refs_14_
  40.1 3.0 %shard_map.50 = f32[4,128,128]{2,1,0:T(8,128)S(1)} custom-call(s32[1032]{0:T(1024)S(1)} %broadcast_1_refs_0_.2.refs_0_, f32[776,128]{1,0:T(8,128)S(1)} %collective-permute-done.5.refs_5_.refs_1_.refs_9_, f32[776,128]{1,0:T(8,128)S(1)} %collective-permute-done.6.refs_6_.refs_2_.refs_10_, f32[776,128]{1,0:T(8,128)S(1)} %collective-permute-done.7.refs_7_.refs_3_.refs_11_, ...), custom_call_target="tpu_custom_call" | custom-call | flops 905969664 | bytes 4194304 | tf_op jit(solution)/shard_map/pallas_call | solution.py:125
  43.1 1.9 %collective-permute-start.10 = (f32[4,128,128]{2,1,0:T(8,128)S(1)}, f32[4,128,128]{2,1,0:T(8,128)S(1)}, u32[]{:S(2)}, u32[]{:S(2)}) collective-permute-start(f32[4,128,128]{2,1,0:T(8,128)S(1)} %shard_map.50), channel_id=1, source_target_pairs={{0,2},{4,6},{8,10},{12,14},{16,18},{20,22},{24,26},{28,30},{1,3},{... | collective-permute-start | bytes 786440 | tf_op jit(solution)/shard_map/window_1/ppermute | solution.py:217
  45.0 3.0 %shard_map.51 = f32[4,128,128]{2,1,0:T(8,128)S(1)} custom-call(s32[1032]{0:T(1024)S(1)} %broadcast_1_refs_0_.2.refs_0_, f32[776,128]{1,0:T(8,128)S(1)} %collective-permute-done.5.refs_5_.refs_1_.refs_9_, f32[776,128]{1,0:T(8,128)S(1)} %collective-permute-done.6.refs_6_.refs_2_.refs_10_, f32[776,128]{1,0:T(8,128)S(1)} %collective-permute-done.7.refs_7_.refs_3_.refs_11_, ...), custom_call_target="tpu_custom_call" | custom-call | flops 905969664 | bytes 4194304 | tf_op jit(solution)/shard_map/pallas_call | solution.py:125
  48.0 0.3 collective-permute-start.11
  48.3 2.8 %shard_map.47.refs_10_ = f32[8,128,128]{2,1,0:T(8,128)S(1)} custom-call(s32[1032]{0:T(1024)S(1)} %broadcast_1_refs_0_.2.refs_0_, f32[776,128]{1,0:T(8,128)S(1)} %collective-permute-done.refs_1_.refs_5_, f32[776,128]{1,0:T(8,128)S(1)} %collective-permute-done.1.refs_2_.refs_6_, f32[776,128]{1,0:T(8,128)S(1)} %collective-permute-done.2.refs_3_.refs_7_, ...), custom_call_target="tpu_custom_call" | custom-call | flops 1207959552 | bytes 4194304 | tf_op jit(solution)/shard_map/pallas_call | solution.py:125
  51.1 2.8 %shard_map.48 = f32[8,128,128]{2,1,0:T(8,128)S(1)} custom-call(s32[1032]{0:T(1024)S(1)} %broadcast_1_refs_0_.2.refs_0_, f32[776,128]{1,0:T(8,128)S(1)} %collective-permute-done.refs_1_.refs_5_, f32[776,128]{1,0:T(8,128)S(1)} %collective-permute-done.1.refs_2_.refs_6_, f32[776,128]{1,0:T(8,128)S(1)} %collective-permute-done.2.refs_3_.refs_7_, ...), custom_call_target="tpu_custom_call" | custom-call | flops 1207959552 | bytes 4194304 | tf_op jit(solution)/shard_map/pallas_call | solution.py:125
  53.8 0.0 collective-permute-done.10
  53.9 3.7 %collective-permute-done.11 = f32[4,128,128]{2,1,0:T(8,128)S(1)} collective-permute-done((f32[4,128,128]{2,1,0:T(8,128)S(1)}, f32[4,128,128]{2,1,0:T(8,128)S(1)}, u32[]{:S(2)}, u32[]{:S(2)}) %collective-permute-start.11) | collective-permute-done | bytes 262176 | tf_op jit(solution)/shard_map/window_1/ppermute | solution.py:217
  57.6 0.9 %maximum_add_fusion = f32[1,2,1,4,128,128]{5,4,3,2,1,0:T(8,128)} fusion(f32[1,2,1,4,128,128]{5,4,3,2,1,0:T(8,128)S(1)} %bitcast.11, f32[1,2,1,2,128,128]{5,4,3,2,1,0:T(8,128)S(1)} %bitcast.15, f32[1,2,1,2,128,128]{5,4,3,2,1,0:T(8,128)S(1)} %bitcast.14), kind=kLoop, calls=%fused_computation | loop fusion | flops 262144 | bytes 1572864 | tf_op jit(solution)/shard_map/add | solution.py:250
  (1 shorter events, 0.0 us)
Async XLA Ops:
  1.8 38.3 %collective-permute-start.9 = (f32[3080,128]{1,0:T(8,128)S(1)}, f32[3080,128]{1,0:T(8,128)S(1)}, u32[]{:S(2)}, u32[]{:S(2)}) collective-permute-start(f32[3080,128]{1,0:T(8,128)S(1)} %get-tuple-element.8.refs_9_.refs_5_.refs_13_), channel_id=1, source_target_pairs={{0,1},{4,5},{8,9},{12,13},{16,17},{20,21},{24,25},{28,29},{1,0},{5... | collective-permute-start | bytes 4730888 | tf_op jit(solution)/shard_map/second/ppermute | solution.py:217
  4.8 20.2 %collective-permute-start.4 = (f32[776,128]{1,0:T(8,128)S(1)}, f32[776,128]{1,0:T(8,128)S(1)}, u32[]{:S(2)}, u32[]{:S(2)}) collective-permute-start(f32[776,128]{1,0:T(8,128)S(1)} %get-tuple-element.7), channel_id=1, source_target_pairs={{0,16},{4,20},{8,24},{12,28},{16,0},{20,4},{24,8},{28,12},{1,17},{... | collective-permute-start | bytes 1191944 | tf_op jit(solution)/shard_map/far/ppermute | solution.py:217
  7.4 22.5 %collective-permute-start = (f32[776,128]{1,0:T(8,128)S(1)}, f32[776,128]{1,0:T(8,128)S(1)}, u32[]{:S(2)}, u32[]{:S(2)}) collective-permute-start(f32[776,128]{1,0:T(8,128)S(1)} %get-tuple-element.7), channel_id=1, source_target_pairs={{0,0},{4,4},{8,2},{12,6},{16,16},{20,20},{24,18},{28,22},{1,1},{5,... | collective-permute-start | bytes 1191944 | tf_op jit(solution)/shard_map/share_0_0/ppermute | solution.py:217
  8.1 21.9 %collective-permute-start.2 = (f32[776,128]{1,0:T(8,128)S(1)}, f32[776,128]{1,0:T(8,128)S(1)}, u32[]{:S(2)}, u32[]{:S(2)}) collective-permute-start(f32[776,128]{1,0:T(8,128)S(1)} %get-tuple-element.7), channel_id=1, source_target_pairs={{0,8},{4,12},{8,10},{12,14},{16,24},{20,28},{24,26},{28,30},{1,9},... | collective-permute-start | bytes 1191944 | tf_op jit(solution)/shard_map/share_0_1/ppermute | solution.py:217
  25.0 5.5 %collective-permute-start.5 = (f32[776,128]{1,0:T(8,128)S(1)}, f32[776,128]{1,0:T(8,128)S(1)}, u32[]{:S(2)}, u32[]{:S(2)}) collective-permute-start(f32[776,128]{1,0:T(8,128)S(1)} %collective-permute-done.4), channel_id=1, source_target_pairs={{0,0},{4,4},{8,2},{12,6},{16,16},{20,20},{24,18},{28,22},{1,1},{5,... | collective-permute-start | bytes 1191944 | tf_op jit(solution)/shard_map/share_1_0/ppermute | solution.py:217
  25.7 12.5 %collective-permute-start.7 = (f32[776,128]{1,0:T(8,128)S(1)}, f32[776,128]{1,0:T(8,128)S(1)}, u32[]{:S(2)}, u32[]{:S(2)}) collective-permute-start(f32[776,128]{1,0:T(8,128)S(1)} %collective-permute-done.4), channel_id=1, source_target_pairs={{0,8},{4,12},{8,10},{12,14},{16,24},{20,28},{24,26},{28,30},{1,9},... | collective-permute-start | bytes 1191944 | tf_op jit(solution)/shard_map/share_1_1/ppermute | solution.py:217
  30.0 8.2 %collective-permute-start.1 = (f32[776,128]{1,0:T(8,128)S(1)}, f32[776,128]{1,0:T(8,128)S(1)}, u32[]{:S(2)}, u32[]{:S(2)}) collective-permute-start(f32[776,128]{1,0:T(8,128)S(1)} %collective-permute-done.refs_1_.refs_5_), channel_id=1, source_target_pairs={{0,4},{4,0},{8,12},{12,8},{16,20},{20,16},{24,28},{28,24},{1,5},{5... | collective-permute-start | bytes 1191944 | tf_op jit(solution)/shard_map/swap_0/ppermute | solution.py:217
  30.0 8.2 %collective-permute-start.3 = (f32[776,128]{1,0:T(8,128)S(1)}, f32[776,128]{1,0:T(8,128)S(1)}, u32[]{:S(2)}, u32[]{:S(2)}) collective-permute-start(f32[776,128]{1,0:T(8,128)S(1)} %collective-permute-done.2.refs_3_.refs_7_), channel_id=1, source_target_pairs={{0,4},{4,0},{8,12},{12,8},{16,20},{20,16},{24,28},{28,24},{1,5},{5... | collective-permute-start | bytes 1191944 | tf_op jit(solution)/shard_map/swap_0/ppermute | solution.py:217
  30.5 9.6 %collective-permute-start.6 = (f32[776,128]{1,0:T(8,128)S(1)}, f32[776,128]{1,0:T(8,128)S(1)}, u32[]{:S(2)}, u32[]{:S(2)}) collective-permute-start(f32[776,128]{1,0:T(8,128)S(1)} %collective-permute-done.5.refs_5_.refs_1_.refs_9_), channel_id=1, source_target_pairs={{0,4},{4,0},{8,12},{12,8},{16,20},{20,16},{24,28},{28,24},{1,5},{5... | collective-permute-start | bytes 1191944 | tf_op jit(solution)/shard_map/swap_1/ppermute | solution.py:217
  38.2 2.0 %collective-permute-start.8 = (f32[776,128]{1,0:T(8,128)S(1)}, f32[776,128]{1,0:T(8,128)S(1)}, u32[]{:S(2)}, u32[]{:S(2)}) collective-permute-start(f32[776,128]{1,0:T(8,128)S(1)} %collective-permute-done.7.refs_7_.refs_3_.refs_11_), channel_id=1, source_target_pairs={{0,4},{4,0},{8,12},{12,8},{16,20},{20,16},{24,28},{28,24},{1,5},{5... | collective-permute-start | bytes 1191944 | tf_op jit(solution)/shard_map/swap_1/ppermute | solution.py:217
  43.1 10.7 %collective-permute-start.10 = (f32[4,128,128]{2,1,0:T(8,128)S(1)}, f32[4,128,128]{2,1,0:T(8,128)S(1)}, u32[]{:S(2)}, u32[]{:S(2)}) collective-permute-start(f32[4,128,128]{2,1,0:T(8,128)S(1)} %shard_map.50), channel_id=1, source_target_pairs={{0,2},{4,6},{8,10},{12,14},{16,18},{20,22},{24,26},{28,30},{1,3},{... | collective-permute-start | bytes 786440 | tf_op jit(solution)/shard_map/window_1/ppermute | solution.py:217
  48.0 9.6 %collective-permute-start.11 = (f32[4,128,128]{2,1,0:T(8,128)S(1)}, f32[4,128,128]{2,1,0:T(8,128)S(1)}, u32[]{:S(2)}, u32[]{:S(2)}) collective-permute-start(f32[4,128,128]{2,1,0:T(8,128)S(1)} %shard_map.51), channel_id=1, source_target_pairs={{0,2},{4,6},{8,10},{12,14},{16,18},{20,22},{24,26},{28,30},{1,3},{... | collective-permute-start | bytes 786440 | tf_op jit(solution)/shard_map/window_1/ppermute | solution.py:217

commit v8 on v7

--- a/solution.py
+++ b/solution.py
@@ -21,11 +21,11 @@
     return high, low
 
 
-def product_kernel(edge, slots, narrow, wide, change, choices, crossings, outer, has_start, *refs):
+def product_kernel(edge, slots, narrow, wide, change, choices, crossings, outer, has_start, afters, *refs):
     width = len(outer)
     items = len(crossings)
     classes = sorted(set(crossings))
-    empty_ref, refs = refs[0], refs[1:]
+    empty_ref, refs = refs[afters], refs[afters + 1 :]
     shares = [refs[n * choices : (n + 1) * choices] for n in range(items)]
     refs = refs[items * choices :]
     second_refs, refs = dict(zip(classes, refs)), refs[len(classes) :]
@@ -106,10 +106,10 @@
             for k in range(2):
                 at = l * width + m + k
                 piece = value[l * edge : (l + 1) * edge, k * edge : (k + 1) * edge]
-                out_ref[at] = start_ref[l * CL + outer[m + k]] + piece if has_start else piece
-
-
-def product(narrow, wide, change, crossings, shares, seconds, start=None, outer=tuple(range(CL))):
+                out_ref[at] = start_ref[at] + piece if has_start else piece
+
+
+def product(narrow, wide, change, crossings, shares, seconds, start=None, outer=tuple(range(CL)), after=None):
     edge = shares[0][0].shape[1]
     items = len(shares)
     choices = len(shares[0])
@@ -120,12 +120,13 @@
     places = (KBLOCKS // narrow + 2) * CL
     empty = jnp.full((places,), seconds[0].shape[0] // edge, jnp.int32)
     operands = [seconds[crossing] for crossing in sorted(set(crossings))]
+    afters = [] if after is None else [after]
     if start is not None:
         operands.append(start)
     return pl.pallas_call(
-        functools.partial(product_kernel, edge, slots, narrow, wide, change, choices, crossings, outer, start is not None),
+        functools.partial(product_kernel, edge, slots, narrow, wide, change, choices, crossings, outer, start is not None, len(afters)),
         out_shape=jax.ShapeDtypeStruct((RL * len(outer), edge, edge), jnp.float32),
-        in_specs=[anywhere] * (1 + items * choices) + [whole] * len(operands),
+        in_specs=[anywhere] * (len(afters) + 1 + items * choices) + [whole] * len(operands),
         out_specs=whole,
         scratch_shapes=[
             pltpu.VMEM((items, slots * edge, edge), jnp.float32),
@@ -145,7 +146,7 @@
         cost_estimate=pl.CostEstimate(
             flops=6 * RL * depth * len(outer) * edge * edge, bytes_accessed=4 * 1024 * 1024, transcendentals=0
         ),
-    )(empty, *[ref for share in shares for ref in share], *operands)
+    )(*afters, empty, *[ref for share in shares for ref in share], *operands)
 
 
 def share_kernel(*refs):
@@ -237,12 +238,15 @@
     seconds = (second, second_other)
     received = []
     for change in range(1, groups):
-        start = product(narrow, wide, change, (0,), candidates[:1], seconds)
-        pieces = []
-        for outer in (tuple(range(CL // 2)), tuple(range(CL // 2, CL))):
-            value = product(narrow, wide, change, (0, 1, 1), [candidates[1], *candidates], seconds, start, outer)
-            got = permute(f"window_{change}", value, lambda r, c: (r ^ (change * 2), c))
-            pieces.append(got.reshape(RL, len(outer), edge, edge))
+        near, other = candidates
+        first, rest = tuple(range(CL // 2)), tuple(range(CL // 2, CL))
+        early = product(narrow, wide, change, (0,), [near], seconds, outer=first)
+        pieces = [
+            product(narrow, wide, change, (0, 1, 1), [other, near, other], seconds, early, outer=first),
+            product(narrow, wide, change, (0, 0, 1, 1), [near, other] * 2, seconds, outer=rest, after=early),
+        ]
+        pieces = [permute(f"window_{change}", value, lambda r, c: (r ^ (change * 2), c)) for value in pieces]
+        pieces = [value.reshape(RL, CL // 2, edge, edge) for value in pieces]
         received.append(jnp.concatenate(pieces, axis=1))
     total = product(narrow, wide, 0, (0, 0), candidates, seconds)
     total = product(narrow, wide, 0, (1, 1), candidates, seconds, total).reshape(RL, CL, edge, edge)

time: 58.6 us -> 58.3 us (level)
  waiting for transfers between devices: 24 us -> 23 us
  Pallas kernels: 15.3 us -> 16 us
    ppermute x12, waiting for transfers between devices: 24 us -> 23 us  [permute(): return lax.ppermute(value, AXES, pairs)]
    pallas_call x5, Pallas kernels: 13.4 us -> 14.1 us  [product(): pl.pallas_call(functools.partial(product_kernel, edge, slots, narrow, wid...]
  transfers between devices with their start and end apart: 12 -> 12, of which waited for: 3 -> 4; matrix products, arithmetic and copies ran while one was open for 0% -> 0% of each run, Pallas kernels for 18% -> 19%
where the time goes in v8:
time: 58.3 us; the launch traced here: 58.1 us
  waiting for transfers between devices  23 us (39%)
  starting transfers between devices  18.2 us (31%)
  Pallas kernels  16 us (27%)
  other arithmetic  0.86 us (1%)
    ppermute x12, waiting for transfers between devices, permute(): return lax.ppermute(value, AXES, pairs)  23 us
    ppermute x12, starting transfers between devices, permute(): return lax.ppermute(value, AXES, pairs)  18.2 us
    pallas_call x5, Pallas kernels, product(): pl.pallas_call(functools.partial(product_kernel, edge, slots, narrow, wid...  14.1 us
    pallas_call x1, Pallas kernels, build_shares(): pl.pallas_call(share_kernel, out_shape=tuple((jax.ShapeDtypeStruct((value...  1.83 us
  transfers between devices with their start and end apart: 12, of which 4 were waited for; matrix products, arithmetic and copies ran while one was open for 0% of the time, Pallas kernels for 19%

profile of v8, /device:TPU:0, one launch (start us, length us, event | category | flops | bytes accessed | tf_op | source)
XLA Modules:
  0.0 58.1 jit_solution(8698506973811481071)
XLA Ops:
  0.0 1.8 %shard_map.46 = (f32[776,128]{1,0:T(8,128)S(1)}, f32[3080,128]{1,0:T(8,128)S(1)}) custom-call(f32[6,128,128]{2,1,0:T(8,128)} %bitcast.13, f32[24,128,128]{2,1,0:T(8,128)} %bitcast.12, s32[1,2,6]{2,1,0:T(2,128)} %refs_2_.1, s32[1,2,24]{2,1,0:T(2,128)} %refs_3_.1), custom_call_target="tpu_custom_call" | custom-call | tf_op jit(solution)/shard_map/pallas_call | solution.py:187
  1.8 3.0 %collective-permute-start.9 = (f32[3080,128]{1,0:T(8,128)S(1)}, f32[3080,128]{1,0:T(8,128)S(1)}, u32[]{:S(2)}, u32[]{:S(2)}) collective-permute-start(f32[3080,128]{1,0:T(8,128)S(1)} %get-tuple-element.8.refs_9_.refs_5_.refs_13_.refs_18_), channel_id=1, source_target_pairs={{0,1},{4,5},{8,9},{12,13},{16,17},{20,21},{24,25},{28,29},{1,0},{5... | collective-permute-start | bytes 4730888 | tf_op jit(solution)/shard_map/second/ppermute | solution.py:218
  4.8 2.6 %collective-permute-start.4 = (f32[776,128]{1,0:T(8,128)S(1)}, f32[776,128]{1,0:T(8,128)S(1)}, u32[]{:S(2)}, u32[]{:S(2)}) collective-permute-start(f32[776,128]{1,0:T(8,128)S(1)} %get-tuple-element.7), channel_id=1, source_target_pairs={{0,16},{4,20},{8,24},{12,28},{16,0},{20,4},{24,8},{28,12},{1,17},{... | collective-permute-start | bytes 1191944 | tf_op jit(solution)/shard_map/far/ppermute | solution.py:218
  7.4 0.7 %collective-permute-start = (f32[776,128]{1,0:T(8,128)S(1)}, f32[776,128]{1,0:T(8,128)S(1)}, u32[]{:S(2)}, u32[]{:S(2)}) collective-permute-start(f32[776,128]{1,0:T(8,128)S(1)} %get-tuple-element.7), channel_id=1, source_target_pairs={{0,0},{4,4},{8,2},{12,6},{16,16},{20,20},{24,18},{28,22},{1,1},{5,... | collective-permute-start | bytes 1191944 | tf_op jit(solution)/shard_map/share_0_0/ppermute | solution.py:218
  8.1 4.3 %collective-permute-start.2 = (f32[776,128]{1,0:T(8,128)S(1)}, f32[776,128]{1,0:T(8,128)S(1)}, u32[]{:S(2)}, u32[]{:S(2)}) collective-permute-start(f32[776,128]{1,0:T(8,128)S(1)} %get-tuple-element.7), channel_id=1, source_target_pairs={{0,8},{4,12},{8,10},{12,14},{16,24},{20,28},{24,26},{28,30},{1,9},... | collective-permute-start | bytes 1191944 | tf_op jit(solution)/shard_map/share_0_1/ppermute | solution.py:218
  12.4 12.6 %collective-permute-done.4 = f32[776,128]{1,0:T(8,128)S(1)} collective-permute-done((f32[776,128]{1,0:T(8,128)S(1)}, f32[776,128]{1,0:T(8,128)S(1)}, u32[]{:S(2)}, u32[]{:S(2)}) %collective-permute-start.4) | collective-permute-done | bytes 397344 | tf_op jit(solution)/shard_map/far/ppermute | solution.py:218
  25.0 0.7 %collective-permute-start.5 = (f32[776,128]{1,0:T(8,128)S(1)}, f32[776,128]{1,0:T(8,128)S(1)}, u32[]{:S(2)}, u32[]{:S(2)}) collective-permute-start(f32[776,128]{1,0:T(8,128)S(1)} %collective-permute-done.4), channel_id=1, source_target_pairs={{0,0},{4,4},{8,2},{12,6},{16,16},{20,20},{24,18},{28,22},{1,1},{5,... | collective-permute-start | bytes 1191944 | tf_op jit(solution)/shard_map/share_1_0/ppermute | solution.py:218
  25.7 4.3 %collective-permute-start.7 = (f32[776,128]{1,0:T(8,128)S(1)}, f32[776,128]{1,0:T(8,128)S(1)}, u32[]{:S(2)}, u32[]{:S(2)}) collective-permute-start(f32[776,128]{1,0:T(8,128)S(1)} %collective-permute-done.4), channel_id=1, source_target_pairs={{0,8},{4,12},{8,10},{12,14},{16,24},{20,28},{24,26},{28,30},{1,9},... | collective-permute-start | bytes 1191944 | tf_op jit(solution)/shard_map/share_1_1/ppermute | solution.py:218
  30.0 0.0 collective-permute-done.refs_1_.refs_5_.refs_2_.refs_10_
  30.0 0.0 collective-permute-start.1
  30.0 0.0 collective-permute-done.2.refs_3_.refs_7_.refs_4_.refs_12_
  30.0 0.5 collective-permute-start.3
  30.5 0.0 collective-permute-done.5.refs_5_.refs_1_.refs_9_.refs_6_.refs_14_
  30.5 0.1 collective-permute-start.6
  30.6 7.6 %collective-permute-done.7.refs_7_.refs_3_.refs_11_.refs_8_.refs_16_ = f32[776,128]{1,0:T(8,128)S(1)} collective-permute-done((f32[776,128]{1,0:T(8,128)S(1)}, f32[776,128]{1,0:T(8,128)S(1)}, u32[]{:S(2)}, u32[]{:S(2)}) %collective-permute-start.7) | collective-permute-done | bytes 397344 | tf_op jit(solution)/shard_map/share_1_1/ppermute | solution.py:218
  38.2 0.0 collective-permute-start.8
  38.2 0.0 collective-permute-done.1.refs_2_.refs_6_.refs_3_.refs_11_
  38.2 0.0 collective-permute-done.3.refs_4_.refs_8_.refs_5_.refs_13_
  38.2 1.6 %shard_map.49.refs_15_.refs_0_ = f32[4,128,128]{2,1,0:T(8,128)S(1)} custom-call(s32[1032]{0:T(1024)S(1)} %broadcast_1_refs_0__refs_1_.2.refs_0_.refs_1_, f32[776,128]{1,0:T(8,128)S(1)} %collective-permute-done.refs_1_.refs_5_.refs_2_.refs_10_, f32[776,128]{1,0:T(8,128)S(1)} %collective-permute-done.1.refs_2_.refs_6_.refs_3_.refs_11_, ...), custom_call_target="tpu_custom_call" | custom-call | flops 301989888 | bytes 4194304 | tf_op jit(solution)/shard_map/pallas_call | solution.py:126
  39.8 0.0 collective-permute-done.6.refs_6_.refs_2_.refs_10_.refs_7_.refs_15_
  39.8 0.1 collective-permute-done.8.refs_8_.refs_4_.refs_12_.refs_9_.refs_17_
  39.9 0.0 collective-permute-done.9.refs_9_.refs_14_.refs_19_
  39.9 3.0 %shard_map.50 = f32[4,128,128]{2,1,0:T(8,128)S(1)} custom-call(s32[1032]{0:T(1024)S(1)} %broadcast_1_refs_0__refs_1_.2.refs_0_.refs_1_, f32[776,128]{1,0:T(8,128)S(1)} %collective-permute-done.5.refs_5_.refs_1_.refs_9_.refs_6_.refs_14_, f32[776,128]{1,0:T(8,128)S(1)} %collective-permute-done.6.refs_6_.refs_2_.refs_10_.refs_7_.refs_15_, ...), custom_call_target="tpu_custom_call" | custom-call | flops 905969664 | bytes 4194304 | tf_op jit(solution)/shard_map/pallas_call | solution.py:126
  42.9 1.8 %collective-permute-start.10 = (f32[4,128,128]{2,1,0:T(8,128)S(1)}, f32[4,128,128]{2,1,0:T(8,128)S(1)}, u32[]{:S(2)}, u32[]{:S(2)}) collective-permute-start(f32[4,128,128]{2,1,0:T(8,128)S(1)} %shard_map.50), channel_id=1, source_target_pairs={{0,2},{4,6},{8,10},{12,14},{16,18},{20,22},{24,26},{28,30},{1,3},{... | collective-permute-start | bytes 786440 | tf_op jit(solution)/shard_map/window_1/ppermute | solution.py:218
  44.7 4.0 %shard_map.51 = f32[4,128,128]{2,1,0:T(8,128)S(1)} custom-call(f32[4,128,128]{2,1,0:T(8,128)S(1)} %shard_map.49.refs_15_.refs_0_, s32[1032]{0:T(1024)S(1)} %broadcast_1_refs_0__refs_1_.2.refs_0_.refs_1_, f32[776,128]{1,0:T(8,128)S(1)} %collective-permute-done.refs_1_.refs_5_.refs_2_.refs_10_, ...), custom_call_target="tpu_custom_call" | custom-call | flops 1207959552 | bytes 4194304 | tf_op jit(solution)/shard_map/pallas_call | solution.py:126
  48.7 0.3 collective-permute-start.11
  49.0 2.8 %shard_map.47.refs_10_ = f32[8,128,128]{2,1,0:T(8,128)S(1)} custom-call(s32[1032]{0:T(1024)S(1)} %broadcast_1_refs_0__refs_1_.2.refs_0_.refs_1_, f32[776,128]{1,0:T(8,128)S(1)} %collective-permute-done.refs_1_.refs_5_.refs_2_.refs_10_, f32[776,128]{1,0:T(8,128)S(1)} %collective-permute-done.1.refs_2_.refs_6_.refs_3_.refs_11_, ...), custom_call_target="tpu_custom_call" | custom-call | flops 1207959552 | bytes 4194304 | tf_op jit(solution)/shard_map/pallas_call | solution.py:126
  51.8 2.8 %shard_map.48 = f32[8,128,128]{2,1,0:T(8,128)S(1)} custom-call(s32[1032]{0:T(1024)S(1)} %broadcast_1_refs_0__refs_1_.2.refs_0_.refs_1_, f32[776,128]{1,0:T(8,128)S(1)} %collective-permute-done.refs_1_.refs_5_.refs_2_.refs_10_, f32[776,128]{1,0:T(8,128)S(1)} %collective-permute-done.1.refs_2_.refs_6_.refs_3_.refs_11_, ...), custom_call_target="tpu_custom_call" | custom-call | flops 1207959552 | bytes 4194304 | tf_op jit(solution)/shard_map/pallas_call | solution.py:126
  54.6 0.0 collective-permute-done.10
  54.6 2.7 %collective-permute-done.11 = f32[4,128,128]{2,1,0:T(8,128)S(1)} collective-permute-done((f32[4,128,128]{2,1,0:T(8,128)S(1)}, f32[4,128,128]{2,1,0:T(8,128)S(1)}, u32[]{:S(2)}, u32[]{:S(2)}) %collective-permute-start.11) | collective-permute-done | bytes 262176 | tf_op jit(solution)/shard_map/window_1/ppermute | solution.py:218
  57.3 0.9 %maximum_add_fusion = f32[1,2,1,4,128,128]{5,4,3,2,1,0:T(8,128)} fusion(f32[1,2,1,4,128,128]{5,4,3,2,1,0:T(8,128)S(1)} %bitcast.11, f32[1,2,1,2,128,128]{5,4,3,2,1,0:T(8,128)S(1)} %bitcast.15, f32[1,2,1,2,128,128]{5,4,3,2,1,0:T(8,128)S(1)} %bitcast.14), kind=kLoop, calls=%fused_computation | loop fusion | flops 262144 | bytes 1572864 | tf_op jit(solution)/shard_map/add | solution.py:254
  (1 shorter events, 0.0 us)
Async XLA Ops:
  1.8 38.1 %collective-permute-start.9 = (f32[3080,128]{1,0:T(8,128)S(1)}, f32[3080,128]{1,0:T(8,128)S(1)}, u32[]{:S(2)}, u32[]{:S(2)}) collective-permute-start(f32[3080,128]{1,0:T(8,128)S(1)} %get-tuple-element.8.refs_9_.refs_5_.refs_13_.refs_18_), channel_id=1, source_target_pairs={{0,1},{4,5},{8,9},{12,13},{16,17},{20,21},{24,25},{28,29},{1,0},{5... | collective-permute-start | bytes 4730888 | tf_op jit(solution)/shard_map/second/ppermute | solution.py:218
  4.8 20.2 %collective-permute-start.4 = (f32[776,128]{1,0:T(8,128)S(1)}, f32[776,128]{1,0:T(8,128)S(1)}, u32[]{:S(2)}, u32[]{:S(2)}) collective-permute-start(f32[776,128]{1,0:T(8,128)S(1)} %get-tuple-element.7), channel_id=1, source_target_pairs={{0,16},{4,20},{8,24},{12,28},{16,0},{20,4},{24,8},{28,12},{1,17},{... | collective-permute-start | bytes 1191944 | tf_op jit(solution)/shard_map/far/ppermute | solution.py:218
  7.4 22.5 %collective-permute-start = (f32[776,128]{1,0:T(8,128)S(1)}, f32[776,128]{1,0:T(8,128)S(1)}, u32[]{:S(2)}, u32[]{:S(2)}) collective-permute-start(f32[776,128]{1,0:T(8,128)S(1)} %get-tuple-element.7), channel_id=1, source_target_pairs={{0,0},{4,4},{8,2},{12,6},{16,16},{20,20},{24,18},{28,22},{1,1},{5,... | collective-permute-start | bytes 1191944 | tf_op jit(solution)/shard_map/share_0_0/ppermute | solution.py:218
  8.1 21.9 %collective-permute-start.2 = (f32[776,128]{1,0:T(8,128)S(1)}, f32[776,128]{1,0:T(8,128)S(1)}, u32[]{:S(2)}, u32[]{:S(2)}) collective-permute-start(f32[776,128]{1,0:T(8,128)S(1)} %get-tuple-element.7), channel_id=1, source_target_pairs={{0,8},{4,12},{8,10},{12,14},{16,24},{20,28},{24,26},{28,30},{1,9},... | collective-permute-start | bytes 1191944 | tf_op jit(solution)/shard_map/share_0_1/ppermute | solution.py:218
  25.0 5.5 %collective-permute-start.5 = (f32[776,128]{1,0:T(8,128)S(1)}, f32[776,128]{1,0:T(8,128)S(1)}, u32[]{:S(2)}, u32[]{:S(2)}) collective-permute-start(f32[776,128]{1,0:T(8,128)S(1)} %collective-permute-done.4), channel_id=1, source_target_pairs={{0,0},{4,4},{8,2},{12,6},{16,16},{20,20},{24,18},{28,22},{1,1},{5,... | collective-permute-start | bytes 1191944 | tf_op jit(solution)/shard_map/share_1_0/ppermute | solution.py:218
  25.7 12.5 %collective-permute-start.7 = (f32[776,128]{1,0:T(8,128)S(1)}, f32[776,128]{1,0:T(8,128)S(1)}, u32[]{:S(2)}, u32[]{:S(2)}) collective-permute-start(f32[776,128]{1,0:T(8,128)S(1)} %collective-permute-done.4), channel_id=1, source_target_pairs={{0,8},{4,12},{8,10},{12,14},{16,24},{20,28},{24,26},{28,30},{1,9},... | collective-permute-start | bytes 1191944 | tf_op jit(solution)/shard_map/share_1_1/ppermute | solution.py:218
  30.0 8.2 %collective-permute-start.1 = (f32[776,128]{1,0:T(8,128)S(1)}, f32[776,128]{1,0:T(8,128)S(1)}, u32[]{:S(2)}, u32[]{:S(2)}) collective-permute-start(f32[776,128]{1,0:T(8,128)S(1)} %collective-permute-done.refs_1_.refs_5_.refs_2_.refs_10_), channel_id=1, source_target_pairs={{0,4},{4,0},{8,12},{12,8},{16,20},{20,16},{24,28},{28,24},{1,5},{5... | collective-permute-start | bytes 1191944 | tf_op jit(solution)/shard_map/swap_0/ppermute | solution.py:218
  30.0 8.2 %collective-permute-start.3 = (f32[776,128]{1,0:T(8,128)S(1)}, f32[776,128]{1,0:T(8,128)S(1)}, u32[]{:S(2)}, u32[]{:S(2)}) collective-permute-start(f32[776,128]{1,0:T(8,128)S(1)} %collective-permute-done.2.refs_3_.refs_7_.refs_4_.refs_12_), channel_id=1, source_target_pairs={{0,4},{4,0},{8,12},{12,8},{16,20},{20,16},{24,28},{28,24},{1,5},{5... | collective-permute-start | bytes 1191944 | tf_op jit(solution)/shard_map/swap_0/ppermute | solution.py:218
  30.5 9.3 %collective-permute-start.6 = (f32[776,128]{1,0:T(8,128)S(1)}, f32[776,128]{1,0:T(8,128)S(1)}, u32[]{:S(2)}, u32[]{:S(2)}) collective-permute-start(f32[776,128]{1,0:T(8,128)S(1)} %collective-permute-done.5.refs_5_.refs_1_.refs_9_.refs_6_.refs_14_), channel_id=1, source_target_pairs={{0,4},{4,0},{8,12},{12,8},{16,20},{20,16},{24,28},{28,24},{1,5},{5... | collective-permute-start | bytes 1191944 | tf_op jit(solution)/shard_map/swap_1/ppermute | solution.py:218
  38.2 1.7 %collective-permute-start.8 = (f32[776,128]{1,0:T(8,128)S(1)}, f32[776,128]{1,0:T(8,128)S(1)}, u32[]{:S(2)}, u32[]{:S(2)}) collective-permute-start(f32[776,128]{1,0:T(8,128)S(1)} %collective-permute-done.7.refs_7_.refs_3_.refs_11_.refs_8_.refs_16_), channel_id=1, source_target_pairs={{0,4},{4,0},{8,12},{12,8},{16,20},{20,16},{24,28},{28,24},{1,5},{5... | collective-permute-start | bytes 1191944 | tf_op jit(solution)/shard_map/swap_1/ppermute | solution.py:218
  42.9 11.7 %collective-permute-start.10 = (f32[4,128,128]{2,1,0:T(8,128)S(1)}, f32[4,128,128]{2,1,0:T(8,128)S(1)}, u32[]{:S(2)}, u32[]{:S(2)}) collective-permute-start(f32[4,128,128]{2,1,0:T(8,128)S(1)} %shard_map.50), channel_id=1, source_target_pairs={{0,2},{4,6},{8,10},{12,14},{16,18},{20,22},{24,26},{28,30},{1,3},{... | collective-permute-start | bytes 786440 | tf_op jit(solution)/shard_map/window_1/ppermute | solution.py:218
  48.7 8.6 %collective-permute-start.11 = (f32[4,128,128]{2,1,0:T(8,128)S(1)}, f32[4,128,128]{2,1,0:T(8,128)S(1)}, u32[]{:S(2)}, u32[]{:S(2)}) collective-permute-start(f32[4,128,128]{2,1,0:T(8,128)S(1)} %shard_map.51), channel_id=1, source_target_pairs={{0,2},{4,6},{8,10},{12,14},{16,18},{20,22},{24,26},{28,30},{1,3},{... | collective-permute-start | bytes 786440 | tf_op jit(solution)/shard_map/window_1/ppermute | solution.py:218

commit v9 on v8

--- a/solution.py
+++ b/solution.py
@@ -11,6 +11,7 @@
 CL = 4
 KBLOCKS = 1024
 PAD = 8
+CHUNK = 4
 AXES = ("wide", "narrow")
 VMEM_LIMIT = 20 * 1024 * 1024
 
@@ -31,7 +32,7 @@
     second_refs, refs = dict(zip(classes, refs)), refs[len(classes) :]
     if has_start:
         start_ref, refs = refs[0], refs[1:]
-    (out_ref, a_ref, index_ref, second_index, tables, left_high, left_low, right_high, right_low,
+    (out_ref, a_ref, index_ref, second_index, tables, found_ref, left_high, left_low, right_high, right_low,
      block_sems, index_sems, second_sems, table_sems) = refs
     row, column = lax.axis_index("narrow"), lax.axis_index("wide")
     turn = (row // 2) ^ (column // 2 % (choices // 2)) ^ change
@@ -48,7 +49,7 @@
     def copies(n, ref):
         return (
             pltpu.make_async_copy(ref.at[pl.ds(rows, PAD)], index_ref.at[n], index_sems.at[n]),
-            pltpu.make_async_copy(ref.at[pl.ds(0, rows)], a_ref.at[n], block_sems.at[n]),
+            pltpu.make_async_copy(ref.at[pl.ds(0, rows)], a_ref.at[pl.ds(n * rows, rows)], block_sems.at[n]),
         )
 
     for copy in table_copies:
@@ -60,8 +61,6 @@
             def _():
                 for copy in copies(n, shares[n][choice]):
                     copy.start()
-    left_high[...] = jnp.zeros_like(left_high)
-    left_low[...] = jnp.zeros_like(left_low)
     for copy in table_copies:
         copy.wait()
     for crossing in classes:
@@ -73,40 +72,64 @@
     waits = [copies(n, shares[n][0]) for n in range(items)]
     for index_copy, _ in waits:
         index_copy.wait()
+    for n in range(RL * width):
+        out_ref[n] = start_ref[n] if has_start else jnp.zeros((edge, edge), jnp.float32)
+    counts = {}
+    for crossing in classes:
+        count = jnp.int32(0)
+        for n in range(items):
+            if crossings[n] != crossing:
+                continue
+            for slot in range(slots):
+                inner = index_ref[n, 1, slot].astype(jnp.int32)
+                inner = jnp.where(inner < 0, KBLOCKS // narrow, lax.div(jnp.maximum(inner, 0), narrow))
+                least = tables[crossing, inner * CL + outer[0]]
+                for m in outer[1:]:
+                    least = jnp.minimum(least, tables[crossing, inner * CL + m])
+                found_ref[crossing, 0, count] = n * slots + slot
+                found_ref[crossing, 1, count] = inner
+                found_ref[crossing, 2, count] = lax.div(jnp.maximum(index_ref[n, 0, slot].astype(jnp.int32), 0), narrow)
+                count = count + (least < slots_second).astype(jnp.int32)
+        counts[crossing] = count
     for _, block_copy in waits:
         block_copy.wait()
-    for n, crossing in enumerate(crossings):
-        for slot in range(slots):
-            at = (n * slots + slot) * edge
-            inner = index_ref[n, 1, slot].astype(jnp.int32)
-            inner = jnp.where(inner < 0, KBLOCKS // narrow, lax.div(jnp.maximum(inner, 0), narrow))
+    dot = functools.partial(jnp.dot, preferred_element_type=jnp.float32)
+
+    def multiply(crossing, first):
+        for k in range(CHUNK):
+            there = first + k < counts[crossing]
+            at = k * edge
+            place = jnp.where(there, found_ref[crossing, 0, first + k], 0)
+            inner = jnp.where(there, found_ref[crossing, 1, first + k], KBLOCKS // narrow)
+            line = jnp.where(there, found_ref[crossing, 2, first + k], 0)
             for at_column, m in enumerate(outer):
                 block = tables[crossing, inner * CL + m]
                 source = pl.ds(pl.multiple_of(jnp.minimum(block, slots_second - 1) * edge, edge), edge)
                 high, low = split(jnp.where(block < slots_second, second_refs[crossing][source, :], 0.0))
                 right_high[at : at + edge, at_column * edge : (at_column + 1) * edge] = high
                 right_low[at : at + edge, at_column * edge : (at_column + 1) * edge] = low
-    for n in range(items):
-        for slot in range(slots):
-            at = (n * slots + slot) * edge
-            line = lax.div(jnp.maximum(index_ref[n, 0, slot].astype(jnp.int32), 0), narrow)
-            high, low = split(a_ref[n, slot * edge : (slot + 1) * edge, :])
-            target = pl.ds(pl.multiple_of(line * edge, edge), edge)
-            left_high[target, at : at + edge] = high
-            left_low[target, at : at + edge] = low
-    dot = functools.partial(jnp.dot, preferred_element_type=jnp.float32)
-    for m in range(0, width, 2):
-        columns = slice(m * edge, (m + 2) * edge)
-        value = (
-            dot(left_high[...], right_high[:, columns])
-            + dot(left_low[...], right_high[:, columns])
-            + dot(left_high[...], right_low[:, columns])
-        )
-        for l in range(RL):
-            for k in range(2):
-                at = l * width + m + k
-                piece = value[l * edge : (l + 1) * edge, k * edge : (k + 1) * edge]
-                out_ref[at] = start_ref[at] + piece if has_start else piece
+            high, low = split(a_ref[pl.ds(pl.multiple_of(place * edge, edge), edge), :])
+            zero = jnp.zeros_like(high)
+            for l in range(RL):
+                left_high[l * edge : (l + 1) * edge, at : at + edge] = jnp.where(line == l, high, zero)
+                left_low[l * edge : (l + 1) * edge, at : at + edge] = jnp.where(line == l, low, zero)
+        for m in range(0, width, 2):
+            columns = slice(m * edge, (m + 2) * edge)
+            value = (
+                dot(left_high[...], right_high[:, columns])
+                + dot(left_low[...], right_high[:, columns])
+                + dot(left_high[...], right_low[:, columns])
+            )
+            for l in range(RL):
+                for k in range(2):
+                    at = l * width + m + k
+                    out_ref[at] += value[l * edge : (l + 1) * edge, k * edge : (k + 1) * edge]
+
+    for crossing in classes:
+        for first in range(0, crossings.count(crossing) * slots, CHUNK):
+            @pl.when(first < counts[crossing])
+            def _():
+                multiply(crossing, first)
 
 
 def product(narrow, wide, change, crossings, shares, seconds, start=None, outer=tuple(range(CL)), after=None):
@@ -129,14 +152,15 @@
         in_specs=[anywhere] * (len(afters) + 1 + items * choices) + [whole] * len(operands),
         out_specs=whole,
         scratch_shapes=[
-            pltpu.VMEM((items, slots * edge, edge), jnp.float32),
+            pltpu.VMEM((depth, edge), jnp.float32),
             pltpu.SMEM((items, PAD, edge), jnp.float32),
             pltpu.SMEM((2, PAD, edge), jnp.float32),
             pltpu.SMEM((2, places), jnp.int32),
-            pltpu.VMEM((RL * edge, depth), jnp.bfloat16),
-            pltpu.VMEM((RL * edge, depth), jnp.bfloat16),
-            pltpu.VMEM((depth, len(outer) * edge), jnp.bfloat16),
-            pltpu.VMEM((depth, len(outer) * edge), jnp.bfloat16),
+            pltpu.SMEM((2, 3, items * slots + CHUNK), jnp.int32),
+            pltpu.VMEM((RL * edge, CHUNK * edge), jnp.bfloat16),
+            pltpu.VMEM((RL * edge, CHUNK * edge), jnp.bfloat16),
+            pltpu.VMEM((CHUNK * edge, len(outer) * edge), jnp.bfloat16),
+            pltpu.VMEM((CHUNK * edge, len(outer) * edge), jnp.bfloat16),
             pltpu.SemaphoreType.DMA((items,)),
             pltpu.SemaphoreType.DMA((items,)),
             pltpu.SemaphoreType.DMA((2,)),

time: 58.3 us -> 57.8 us (level)
  no operation moved by 1% of the time
where the time goes in v9:
time: 57.8 us; the launch traced here: 57.6 us
  waiting for transfers between devices  23.2 us (40%)
  starting transfers between devices  17.9 us (31%)
  Pallas kernels  15.5 us (27%)
  other arithmetic  0.86 us (1%)
    ppermute x12, waiting for transfers between devices, permute(): return lax.ppermute(value, AXES, pairs)  23.2 us
    ppermute x12, starting transfers between devices, permute(): return lax.ppermute(value, AXES, pairs)  17.9 us
    pallas_call x5, Pallas kernels, product(): pl.pallas_call(functools.partial(product_kernel, edge, slots, narrow, wid...  13.7 us
    pallas_call x1, Pallas kernels, build_shares(): pl.pallas_call(share_kernel, out_shape=tuple((jax.ShapeDtypeStruct((value...  1.83 us
  transfers between devices with their start and end apart: 12, of which 4 were waited for; matrix products, arithmetic and copies ran while one was open for 0% of the time, Pallas kernels for 19%

profile of v9, /device:TPU:0, one launch (start us, length us, event | category | flops | bytes accessed | tf_op | source)
XLA Modules:
  0.0 57.6 jit_solution(13880760271400669452)
XLA Ops:
  0.0 1.8 %shard_map.46 = (f32[776,128]{1,0:T(8,128)S(1)}, f32[3080,128]{1,0:T(8,128)S(1)}) custom-call(f32[6,128,128]{2,1,0:T(8,128)} %bitcast.13, f32[24,128,128]{2,1,0:T(8,128)} %bitcast.12, s32[1,2,6]{2,1,0:T(2,128)} %refs_2_.1, s32[1,2,24]{2,1,0:T(2,128)} %refs_3_.1), custom_call_target="tpu_custom_call" | custom-call | tf_op jit(solution)/shard_map/pallas_call | solution.py:211
  1.8 3.0 %collective-permute-start.9 = (f32[3080,128]{1,0:T(8,128)S(1)}, f32[3080,128]{1,0:T(8,128)S(1)}, u32[]{:S(2)}, u32[]{:S(2)}) collective-permute-start(f32[3080,128]{1,0:T(8,128)S(1)} %get-tuple-element.8.refs_9_.refs_5_.refs_13_.refs_18_), channel_id=1, source_target_pairs={{0,1},{4,5},{8,9},{12,13},{16,17},{20,21},{24,25},{28,29},{1,0},{5... | collective-permute-start | bytes 4730888 | tf_op jit(solution)/shard_map/second/ppermute | solution.py:242
  4.8 2.6 %collective-permute-start.4 = (f32[776,128]{1,0:T(8,128)S(1)}, f32[776,128]{1,0:T(8,128)S(1)}, u32[]{:S(2)}, u32[]{:S(2)}) collective-permute-start(f32[776,128]{1,0:T(8,128)S(1)} %get-tuple-element.7), channel_id=1, source_target_pairs={{0,16},{4,20},{8,24},{12,28},{16,0},{20,4},{24,8},{28,12},{1,17},{... | collective-permute-start | bytes 1191944 | tf_op jit(solution)/shard_map/far/ppermute | solution.py:242
  7.4 0.7 %collective-permute-start = (f32[776,128]{1,0:T(8,128)S(1)}, f32[776,128]{1,0:T(8,128)S(1)}, u32[]{:S(2)}, u32[]{:S(2)}) collective-permute-start(f32[776,128]{1,0:T(8,128)S(1)} %get-tuple-element.7), channel_id=1, source_target_pairs={{0,0},{4,4},{8,2},{12,6},{16,16},{20,20},{24,18},{28,22},{1,1},{5,... | collective-permute-start | bytes 1191944 | tf_op jit(solution)/shard_map/share_0_0/ppermute | solution.py:242
  8.1 4.3 %collective-permute-start.2 = (f32[776,128]{1,0:T(8,128)S(1)}, f32[776,128]{1,0:T(8,128)S(1)}, u32[]{:S(2)}, u32[]{:S(2)}) collective-permute-start(f32[776,128]{1,0:T(8,128)S(1)} %get-tuple-element.7), channel_id=1, source_target_pairs={{0,8},{4,12},{8,10},{12,14},{16,24},{20,28},{24,26},{28,30},{1,9},... | collective-permute-start | bytes 1191944 | tf_op jit(solution)/shard_map/share_0_1/ppermute | solution.py:242
  12.4 12.6 %collective-permute-done.4 = f32[776,128]{1,0:T(8,128)S(1)} collective-permute-done((f32[776,128]{1,0:T(8,128)S(1)}, f32[776,128]{1,0:T(8,128)S(1)}, u32[]{:S(2)}, u32[]{:S(2)}) %collective-permute-start.4) | collective-permute-done | bytes 397344 | tf_op jit(solution)/shard_map/far/ppermute | solution.py:242
  25.0 0.7 %collective-permute-start.5 = (f32[776,128]{1,0:T(8,128)S(1)}, f32[776,128]{1,0:T(8,128)S(1)}, u32[]{:S(2)}, u32[]{:S(2)}) collective-permute-start(f32[776,128]{1,0:T(8,128)S(1)} %collective-permute-done.4), channel_id=1, source_target_pairs={{0,0},{4,4},{8,2},{12,6},{16,16},{20,20},{24,18},{28,22},{1,1},{5,... | collective-permute-start | bytes 1191944 | tf_op jit(solution)/shard_map/share_1_0/ppermute | solution.py:242
  25.7 4.3 %collective-permute-start.7 = (f32[776,128]{1,0:T(8,128)S(1)}, f32[776,128]{1,0:T(8,128)S(1)}, u32[]{:S(2)}, u32[]{:S(2)}) collective-permute-start(f32[776,128]{1,0:T(8,128)S(1)} %collective-permute-done.4), channel_id=1, source_target_pairs={{0,8},{4,12},{8,10},{12,14},{16,24},{20,28},{24,26},{28,30},{1,9},... | collective-permute-start | bytes 1191944 | tf_op jit(solution)/shard_map/share_1_1/ppermute | solution.py:242
  30.0 0.0 collective-permute-done.refs_1_.refs_5_.refs_2_.refs_10_
  30.0 0.0 collective-permute-start.1
  30.0 0.0 collective-permute-done.2.refs_3_.refs_7_.refs_4_.refs_12_
  30.0 0.5 collective-permute-start.3
  30.5 0.0 collective-permute-done.5.refs_5_.refs_1_.refs_9_.refs_6_.refs_14_
  30.5 0.1 collective-permute-start.6
  30.6 7.6 %collective-permute-done.7.refs_7_.refs_3_.refs_11_.refs_8_.refs_16_ = f32[776,128]{1,0:T(8,128)S(1)} collective-permute-done((f32[776,128]{1,0:T(8,128)S(1)}, f32[776,128]{1,0:T(8,128)S(1)}, u32[]{:S(2)}, u32[]{:S(2)}) %collective-permute-start.7) | collective-permute-done | bytes 397344 | tf_op jit(solution)/shard_map/share_1_1/ppermute | solution.py:242
  38.2 0.0 collective-permute-start.8
  38.2 0.0 collective-permute-done.1.refs_2_.refs_6_.refs_3_.refs_11_
  38.2 0.0 collective-permute-done.3.refs_4_.refs_8_.refs_5_.refs_13_
  38.2 1.5 %shard_map.49.refs_15_.refs_0_ = f32[4,128,128]{2,1,0:T(8,128)S(1)} custom-call(s32[1032]{0:T(1024)S(1)} %broadcast_1_refs_0__refs_1_.2.refs_0_.refs_1_, f32[776,128]{1,0:T(8,128)S(1)} %collective-permute-done.refs_1_.refs_5_.refs_2_.refs_10_, f32[776,128]{1,0:T(8,128)S(1)} %collective-permute-done.1.refs_2_.refs_6_.refs_3_.refs_11_, ...), custom_call_target="tpu_custom_call" | custom-call | flops 301989888 | bytes 4194304 | tf_op jit(solution)/shard_map/pallas_call | solution.py:149
  39.7 0.0 collective-permute-done.6.refs_6_.refs_2_.refs_10_.refs_7_.refs_15_
  39.7 0.2 collective-permute-done.8.refs_8_.refs_4_.refs_12_.refs_9_.refs_17_
  39.9 0.0 collective-permute-done.9.refs_9_.refs_14_.refs_19_
  39.9 2.6 %shard_map.50 = f32[4,128,128]{2,1,0:T(8,128)S(1)} custom-call(s32[1032]{0:T(1024)S(1)} %broadcast_1_refs_0__refs_1_.2.refs_0_.refs_1_, f32[776,128]{1,0:T(8,128)S(1)} %collective-permute-done.5.refs_5_.refs_1_.refs_9_.refs_6_.refs_14_, f32[776,128]{1,0:T(8,128)S(1)} %collective-permute-done.6.refs_6_.refs_2_.refs_10_.refs_7_.refs_15_, ...), custom_call_target="tpu_custom_call" | custom-call | flops 905969664 | bytes 4194304 | tf_op jit(solution)/shard_map/pallas_call | solution.py:149
  42.5 1.8 %collective-permute-start.10 = (f32[4,128,128]{2,1,0:T(8,128)S(1)}, f32[4,128,128]{2,1,0:T(8,128)S(1)}, u32[]{:S(2)}, u32[]{:S(2)}) collective-permute-start(f32[4,128,128]{2,1,0:T(8,128)S(1)} %shard_map.50), channel_id=1, source_target_pairs={{0,2},{4,6},{8,10},{12,14},{16,18},{20,22},{24,26},{28,30},{1,3},{... | collective-permute-start | bytes 786440 | tf_op jit(solution)/shard_map/window_1/ppermute | solution.py:242
  44.3 4.2 %shard_map.51 = f32[4,128,128]{2,1,0:T(8,128)S(1)} custom-call(f32[4,128,128]{2,1,0:T(8,128)S(1)} %shard_map.49.refs_15_.refs_0_, s32[1032]{0:T(1024)S(1)} %broadcast_1_refs_0__refs_1_.2.refs_0_.refs_1_, f32[776,128]{1,0:T(8,128)S(1)} %collective-permute-done.refs_1_.refs_5_.refs_2_.refs_10_, ...), custom_call_target="tpu_custom_call" | custom-call | flops 1207959552 | bytes 4194304 | tf_op jit(solution)/shard_map/pallas_call | solution.py:149
  48.5 0.1 collective-permute-start.11
  48.6 2.7 %shard_map.47.refs_10_ = f32[8,128,128]{2,1,0:T(8,128)S(1)} custom-call(s32[1032]{0:T(1024)S(1)} %broadcast_1_refs_0__refs_1_.2.refs_0_.refs_1_, f32[776,128]{1,0:T(8,128)S(1)} %collective-permute-done.refs_1_.refs_5_.refs_2_.refs_10_, f32[776,128]{1,0:T(8,128)S(1)} %collective-permute-done.1.refs_2_.refs_6_.refs_3_.refs_11_, ...), custom_call_target="tpu_custom_call" | custom-call | flops 1207959552 | bytes 4194304 | tf_op jit(solution)/shard_map/pallas_call | solution.py:149
  51.3 2.7 %shard_map.48 = f32[8,128,128]{2,1,0:T(8,128)S(1)} custom-call(s32[1032]{0:T(1024)S(1)} %broadcast_1_refs_0__refs_1_.2.refs_0_.refs_1_, f32[776,128]{1,0:T(8,128)S(1)} %collective-permute-done.refs_1_.refs_5_.refs_2_.refs_10_, f32[776,128]{1,0:T(8,128)S(1)} %collective-permute-done.1.refs_2_.refs_6_.refs_3_.refs_11_, ...), custom_call_target="tpu_custom_call" | custom-call | flops 1207959552 | bytes 4194304 | tf_op jit(solution)/shard_map/pallas_call | solution.py:149
  54.0 0.0 collective-permute-done.10
  54.0 2.7 %collective-permute-done.11 = f32[4,128,128]{2,1,0:T(8,128)S(1)} collective-permute-done((f32[4,128,128]{2,1,0:T(8,128)S(1)}, f32[4,128,128]{2,1,0:T(8,128)S(1)}, u32[]{:S(2)}, u32[]{:S(2)}) %collective-permute-start.11) | collective-permute-done | bytes 262176 | tf_op jit(solution)/shard_map/window_1/ppermute | solution.py:242
  56.7 0.9 %maximum_add_fusion = f32[1,2,1,4,128,128]{5,4,3,2,1,0:T(8,128)} fusion(f32[1,2,1,4,128,128]{5,4,3,2,1,0:T(8,128)S(1)} %bitcast.11, f32[1,2,1,2,128,128]{5,4,3,2,1,0:T(8,128)S(1)} %bitcast.15, f32[1,2,1,2,128,128]{5,4,3,2,1,0:T(8,128)S(1)} %bitcast.14), kind=kLoop, calls=%fused_computation | loop fusion | flops 262144 | bytes 1572864 | tf_op jit(solution)/shard_map/add | solution.py:278
  (1 shorter events, 0.0 us)
Async XLA Ops:
  1.8 38.1 %collective-permute-start.9 = (f32[3080,128]{1,0:T(8,128)S(1)}, f32[3080,128]{1,0:T(8,128)S(1)}, u32[]{:S(2)}, u32[]{:S(2)}) collective-permute-start(f32[3080,128]{1,0:T(8,128)S(1)} %get-tuple-element.8.refs_9_.refs_5_.refs_13_.refs_18_), channel_id=1, source_target_pairs={{0,1},{4,5},{8,9},{12,13},{16,17},{20,21},{24,25},{28,29},{1,0},{5... | collective-permute-start | bytes 4730888 | tf_op jit(solution)/shard_map/second/ppermute | solution.py:242
  4.8 20.2 %collective-permute-start.4 = (f32[776,128]{1,0:T(8,128)S(1)}, f32[776,128]{1,0:T(8,128)S(1)}, u32[]{:S(2)}, u32[]{:S(2)}) collective-permute-start(f32[776,128]{1,0:T(8,128)S(1)} %get-tuple-element.7), channel_id=1, source_target_pairs={{0,16},{4,20},{8,24},{12,28},{16,0},{20,4},{24,8},{28,12},{1,17},{... | collective-permute-start | bytes 1191944 | tf_op jit(solution)/shard_map/far/ppermute | solution.py:242
  7.4 22.5 %collective-permute-start = (f32[776,128]{1,0:T(8,128)S(1)}, f32[776,128]{1,0:T(8,128)S(1)}, u32[]{:S(2)}, u32[]{:S(2)}) collective-permute-start(f32[776,128]{1,0:T(8,128)S(1)} %get-tuple-element.7), channel_id=1, source_target_pairs={{0,0},{4,4},{8,2},{12,6},{16,16},{20,20},{24,18},{28,22},{1,1},{5,... | collective-permute-start | bytes 1191944 | tf_op jit(solution)/shard_map/share_0_0/ppermute | solution.py:242
  8.1 21.9 %collective-permute-start.2 = (f32[776,128]{1,0:T(8,128)S(1)}, f32[776,128]{1,0:T(8,128)S(1)}, u32[]{:S(2)}, u32[]{:S(2)}) collective-permute-start(f32[776,128]{1,0:T(8,128)S(1)} %get-tuple-element.7), channel_id=1, source_target_pairs={{0,8},{4,12},{8,10},{12,14},{16,24},{20,28},{24,26},{28,30},{1,9},... | collective-permute-start | bytes 1191944 | tf_op jit(solution)/shard_map/share_0_1/ppermute | solution.py:242
  25.0 5.5 %collective-permute-start.5 = (f32[776,128]{1,0:T(8,128)S(1)}, f32[776,128]{1,0:T(8,128)S(1)}, u32[]{:S(2)}, u32[]{:S(2)}) collective-permute-start(f32[776,128]{1,0:T(8,128)S(1)} %collective-permute-done.4), channel_id=1, source_target_pairs={{0,0},{4,4},{8,2},{12,6},{16,16},{20,20},{24,18},{28,22},{1,1},{5,... | collective-permute-start | bytes 1191944 | tf_op jit(solution)/shard_map/share_1_0/ppermute | solution.py:242
  25.7 12.5 %collective-permute-start.7 = (f32[776,128]{1,0:T(8,128)S(1)}, f32[776,128]{1,0:T(8,128)S(1)}, u32[]{:S(2)}, u32[]{:S(2)}) collective-permute-start(f32[776,128]{1,0:T(8,128)S(1)} %collective-permute-done.4), channel_id=1, source_target_pairs={{0,8},{4,12},{8,10},{12,14},{16,24},{20,28},{24,26},{28,30},{1,9},... | collective-permute-start | bytes 1191944 | tf_op jit(solution)/shard_map/share_1_1/ppermute | solution.py:242
  30.0 8.2 %collective-permute-start.1 = (f32[776,128]{1,0:T(8,128)S(1)}, f32[776,128]{1,0:T(8,128)S(1)}, u32[]{:S(2)}, u32[]{:S(2)}) collective-permute-start(f32[776,128]{1,0:T(8,128)S(1)} %collective-permute-done.refs_1_.refs_5_.refs_2_.refs_10_), channel_id=1, source_target_pairs={{0,4},{4,0},{8,12},{12,8},{16,20},{20,16},{24,28},{28,24},{1,5},{5... | collective-permute-start | bytes 1191944 | tf_op jit(solution)/shard_map/swap_0/ppermute | solution.py:242
  30.0 8.2 %collective-permute-start.3 = (f32[776,128]{1,0:T(8,128)S(1)}, f32[776,128]{1,0:T(8,128)S(1)}, u32[]{:S(2)}, u32[]{:S(2)}) collective-permute-start(f32[776,128]{1,0:T(8,128)S(1)} %collective-permute-done.2.refs_3_.refs_7_.refs_4_.refs_12_), channel_id=1, source_target_pairs={{0,4},{4,0},{8,12},{12,8},{16,20},{20,16},{24,28},{28,24},{1,5},{5... | collective-permute-start | bytes 1191944 | tf_op jit(solution)/shard_map/swap_0/ppermute | solution.py:242
  30.5 9.2 %collective-permute-start.6 = (f32[776,128]{1,0:T(8,128)S(1)}, f32[776,128]{1,0:T(8,128)S(1)}, u32[]{:S(2)}, u32[]{:S(2)}) collective-permute-start(f32[776,128]{1,0:T(8,128)S(1)} %collective-permute-done.5.refs_5_.refs_1_.refs_9_.refs_6_.refs_14_), channel_id=1, source_target_pairs={{0,4},{4,0},{8,12},{12,8},{16,20},{20,16},{24,28},{28,24},{1,5},{5... | collective-permute-start | bytes 1191944 | tf_op jit(solution)/shard_map/swap_1/ppermute | solution.py:242
  38.2 1.7 %collective-permute-start.8 = (f32[776,128]{1,0:T(8,128)S(1)}, f32[776,128]{1,0:T(8,128)S(1)}, u32[]{:S(2)}, u32[]{:S(2)}) collective-permute-start(f32[776,128]{1,0:T(8,128)S(1)} %collective-permute-done.7.refs_7_.refs_3_.refs_11_.refs_8_.refs_16_), channel_id=1, source_target_pairs={{0,4},{4,0},{8,12},{12,8},{16,20},{20,16},{24,28},{28,24},{1,5},{5... | collective-permute-start | bytes 1191944 | tf_op jit(solution)/shard_map/swap_1/ppermute | solution.py:242
  42.5 11.5 %collective-permute-start.10 = (f32[4,128,128]{2,1,0:T(8,128)S(1)}, f32[4,128,128]{2,1,0:T(8,128)S(1)}, u32[]{:S(2)}, u32[]{:S(2)}) collective-permute-start(f32[4,128,128]{2,1,0:T(8,128)S(1)} %shard_map.50), channel_id=1, source_target_pairs={{0,2},{4,6},{8,10},{12,14},{16,18},{20,22},{24,26},{28,30},{1,3},{... | collective-permute-start | bytes 786440 | tf_op jit(solution)/shard_map/window_1/ppermute | solution.py:242
  48.5 8.2 %collective-permute-start.11 = (f32[4,128,128]{2,1,0:T(8,128)S(1)}, f32[4,128,128]{2,1,0:T(8,128)S(1)}, u32[]{:S(2)}, u32[]{:S(2)}) collective-permute-start(f32[4,128,128]{2,1,0:T(8,128)S(1)} %shard_map.51), channel_id=1, source_target_pairs={{0,2},{4,6},{8,10},{12,14},{16,18},{20,22},{24,26},{28,30},{1,3},{... | collective-permute-start | bytes 786440 | tf_op jit(solution)/shard_map/window_1/ppermute | solution.py:242

commit v10 on v8

--- a/solution.py
+++ b/solution.py
@@ -154,18 +154,15 @@
     parts = [refs[n * arrays : (n + 1) * arrays] for n in range(7)]
     waits = []
     for blocks_hbm, index_hbm, out_hbm, tile_ref, index_ref, block_sem, index_sem in zip(*parts):
-        slots, edge, _ = blocks_hbm.shape
-        copies = [
-            pltpu.make_async_copy(blocks_hbm.at[slot], out_hbm.at[pl.ds(slot * edge, edge)], block_sem.at[slot])
-            for slot in range(slots)
-        ]
+        rows = blocks_hbm.shape[0]
+        copies = [pltpu.make_async_copy(blocks_hbm, out_hbm.at[pl.ds(0, rows)], block_sem.at[0])]
         index_copy = pltpu.make_async_copy(index_hbm, index_ref, index_sem)
         index_copy.start()
         for copy in copies:
             copy.start()
         waits += copies
     for blocks_hbm, index_hbm, out_hbm, tile_ref, index_ref, block_sem, index_sem in zip(*parts):
-        slots, edge, _ = blocks_hbm.shape
+        rows, slots = blocks_hbm.shape[0], index_hbm.shape[-1]
         pltpu.make_async_copy(index_hbm, index_ref, index_sem).wait()
         shape = tile_ref.shape
         row = lax.broadcasted_iota(jnp.int32, shape, 0)
@@ -175,7 +172,7 @@
             for slot in range(slots):
                 tile = jnp.where((row == n) & (column == slot), index_ref[0, n, slot].astype(jnp.float32), tile)
         tile_ref[...] = tile
-        tile_copy = pltpu.make_async_copy(tile_ref, out_hbm.at[pl.ds(slots * edge, PAD)], block_sem.at[slots])
+        tile_copy = pltpu.make_async_copy(tile_ref, out_hbm.at[pl.ds(rows, PAD)], block_sem.at[1])
         tile_copy.start()
         waits.append(tile_copy)
     for copy in waits:
@@ -187,13 +184,13 @@
     return pl.pallas_call(
         share_kernel,
         out_shape=tuple(
-            jax.ShapeDtypeStruct((value.shape[0] * value.shape[1] + PAD, value.shape[2]), jnp.float32) for value in blocks
+            jax.ShapeDtypeStruct((value.shape[0] + PAD, value.shape[1]), jnp.float32) for value in blocks
         ),
         in_specs=[anywhere] * (2 * len(blocks)),
         out_specs=(anywhere,) * len(blocks),
-        scratch_shapes=[pltpu.VMEM((PAD, value.shape[2]), jnp.float32) for value in blocks]
+        scratch_shapes=[pltpu.VMEM((PAD, value.shape[1]), jnp.float32) for value in blocks]
         + [pltpu.SMEM(value.shape, jnp.int32) for value in indices]
-        + [pltpu.SemaphoreType.DMA((value.shape[0] + 1,)) for value in blocks]
+        + [pltpu.SemaphoreType.DMA((2,)) for _ in blocks]
         + [pltpu.SemaphoreType.DMA for _ in blocks],
         compiler_params=pltpu.CompilerParams(vmem_limit_bytes=1024 * 1024),
     )(*[pltpu.with_memory_space_constraint(value, pltpu.HBM) for value in (*blocks, *indices)])
@@ -220,7 +217,7 @@
     def swap(name, value):
         return permute(name, value, lambda r, c: (r, c ^ 1))
 
-    share, second = build_shares((a_blocks[0], b_blocks[0]), (a_index, b_index))
+    share, second = build_shares((a_blocks.reshape(-1, edge), b_blocks.reshape(-1, edge)), (a_index, b_index))
     second_other = permute("second", second, lambda r, c: (r ^ 1, c))
 
     def spread(half, share, turn):

time: 58.3 us -> 58.1 us (level)
  no operation moved by 1% of the time
where the time goes in v10:
time: 58.1 us; the launch traced here: 57.9 us
  waiting for transfers between devices  23 us (40%)
  starting transfers between devices  18.2 us (31%)
  Pallas kernels  15.7 us (27%)
  other arithmetic  0.86 us (1%)
    ppermute x12, waiting for transfers between devices, permute(): return lax.ppermute(value, AXES, pairs)  23 us
    ppermute x12, starting transfers between devices, permute(): return lax.ppermute(value, AXES, pairs)  18.2 us
    pallas_call x5, Pallas kernels, product(): pl.pallas_call(functools.partial(product_kernel, edge, slots, narrow, wid...  14.1 us
    pallas_call x1, Pallas kernels, build_shares(): pl.pallas_call(share_kernel, out_shape=tuple((jax.ShapeDtypeStruct((value...  1.6 us
  transfers between devices with their start and end apart: 12, of which 4 were waited for; matrix products, arithmetic and copies ran while one was open for 0% of the time, Pallas kernels for 19%

profile of v10, /device:TPU:0, one launch (start us, length us, event | category | flops | bytes accessed | tf_op | source)
XLA Modules:
  0.0 57.9 jit_solution(5729816321110356088)
XLA Ops:
  0.0 1.6 %shard_map.46 = (f32[776,128]{1,0:T(8,128)S(1)}, f32[3080,128]{1,0:T(8,128)S(1)}) custom-call(f32[768,128]{1,0:T(8,128)} %bitcast.13, f32[3072,128]{1,0:T(8,128)} %bitcast.12, s32[1,2,6]{2,1,0:T(2,128)} %refs_2_.1, s32[1,2,24]{2,1,0:T(2,128)} %refs_3_.1), custom_call_target="tpu_custom_call" | custom-call | tf_op jit(solution)/shard_map/pallas_call | solution.py:184
  1.6 3.0 %collective-permute-start.9 = (f32[3080,128]{1,0:T(8,128)S(1)}, f32[3080,128]{1,0:T(8,128)S(1)}, u32[]{:S(2)}, u32[]{:S(2)}) collective-permute-start(f32[3080,128]{1,0:T(8,128)S(1)} %get-tuple-element.8.refs_9_.refs_5_.refs_13_.refs_18_), channel_id=1, source_target_pairs={{0,1},{4,5},{8,9},{12,13},{16,17},{20,21},{24,25},{28,29},{1,0},{5... | collective-permute-start | bytes 4730888 | tf_op jit(solution)/shard_map/second/ppermute | solution.py:215
  4.6 2.6 %collective-permute-start.4 = (f32[776,128]{1,0:T(8,128)S(1)}, f32[776,128]{1,0:T(8,128)S(1)}, u32[]{:S(2)}, u32[]{:S(2)}) collective-permute-start(f32[776,128]{1,0:T(8,128)S(1)} %get-tuple-element.7), channel_id=1, source_target_pairs={{0,16},{4,20},{8,24},{12,28},{16,0},{20,4},{24,8},{28,12},{1,17},{... | collective-permute-start | bytes 1191944 | tf_op jit(solution)/shard_map/far/ppermute | solution.py:215
  7.2 0.7 %collective-permute-start = (f32[776,128]{1,0:T(8,128)S(1)}, f32[776,128]{1,0:T(8,128)S(1)}, u32[]{:S(2)}, u32[]{:S(2)}) collective-permute-start(f32[776,128]{1,0:T(8,128)S(1)} %get-tuple-element.7), channel_id=1, source_target_pairs={{0,0},{4,4},{8,2},{12,6},{16,16},{20,20},{24,18},{28,22},{1,1},{5,... | collective-permute-start | bytes 1191944 | tf_op jit(solution)/shard_map/share_0_0/ppermute | solution.py:215
  7.9 4.3 %collective-permute-start.2 = (f32[776,128]{1,0:T(8,128)S(1)}, f32[776,128]{1,0:T(8,128)S(1)}, u32[]{:S(2)}, u32[]{:S(2)}) collective-permute-start(f32[776,128]{1,0:T(8,128)S(1)} %get-tuple-element.7), channel_id=1, source_target_pairs={{0,8},{4,12},{8,10},{12,14},{16,24},{20,28},{24,26},{28,30},{1,9},... | collective-permute-start | bytes 1191944 | tf_op jit(solution)/shard_map/share_0_1/ppermute | solution.py:215
  12.1 12.6 %collective-permute-done.4 = f32[776,128]{1,0:T(8,128)S(1)} collective-permute-done((f32[776,128]{1,0:T(8,128)S(1)}, f32[776,128]{1,0:T(8,128)S(1)}, u32[]{:S(2)}, u32[]{:S(2)}) %collective-permute-start.4) | collective-permute-done | bytes 397344 | tf_op jit(solution)/shard_map/far/ppermute | solution.py:215
  24.8 0.7 %collective-permute-start.5 = (f32[776,128]{1,0:T(8,128)S(1)}, f32[776,128]{1,0:T(8,128)S(1)}, u32[]{:S(2)}, u32[]{:S(2)}) collective-permute-start(f32[776,128]{1,0:T(8,128)S(1)} %collective-permute-done.4), channel_id=1, source_target_pairs={{0,0},{4,4},{8,2},{12,6},{16,16},{20,20},{24,18},{28,22},{1,1},{5,... | collective-permute-start | bytes 1191944 | tf_op jit(solution)/shard_map/share_1_0/ppermute | solution.py:215
  25.5 4.3 %collective-permute-start.7 = (f32[776,128]{1,0:T(8,128)S(1)}, f32[776,128]{1,0:T(8,128)S(1)}, u32[]{:S(2)}, u32[]{:S(2)}) collective-permute-start(f32[776,128]{1,0:T(8,128)S(1)} %collective-permute-done.4), channel_id=1, source_target_pairs={{0,8},{4,12},{8,10},{12,14},{16,24},{20,28},{24,26},{28,30},{1,9},... | collective-permute-start | bytes 1191944 | tf_op jit(solution)/shard_map/share_1_1/ppermute | solution.py:215
  29.7 0.0 collective-permute-done.refs_1_.refs_5_.refs_2_.refs_10_
  29.7 0.0 collective-permute-start.1
  29.7 0.0 collective-permute-done.2.refs_3_.refs_7_.refs_4_.refs_12_
  29.7 0.5 collective-permute-start.3
  30.2 0.0 collective-permute-done.5.refs_5_.refs_1_.refs_9_.refs_6_.refs_14_
  30.3 0.1 collective-permute-start.6
  30.3 7.6 %collective-permute-done.7.refs_7_.refs_3_.refs_11_.refs_8_.refs_16_ = f32[776,128]{1,0:T(8,128)S(1)} collective-permute-done((f32[776,128]{1,0:T(8,128)S(1)}, f32[776,128]{1,0:T(8,128)S(1)}, u32[]{:S(2)}, u32[]{:S(2)}) %collective-permute-start.7) | collective-permute-done | bytes 397344 | tf_op jit(solution)/shard_map/share_1_1/ppermute | solution.py:215
  37.9 0.0 collective-permute-start.8
  37.9 0.0 collective-permute-done.1.refs_2_.refs_6_.refs_3_.refs_11_
  37.9 0.0 collective-permute-done.3.refs_4_.refs_8_.refs_5_.refs_13_
  38.0 1.6 %shard_map.49.refs_15_.refs_0_ = f32[4,128,128]{2,1,0:T(8,128)S(1)} custom-call(s32[1032]{0:T(1024)S(1)} %broadcast_1_refs_0__refs_1_.2.refs_0_.refs_1_, f32[776,128]{1,0:T(8,128)S(1)} %collective-permute-done.refs_1_.refs_5_.refs_2_.refs_10_, f32[776,128]{1,0:T(8,128)S(1)} %collective-permute-done.1.refs_2_.refs_6_.refs_3_.refs_11_, ...), custom_call_target="tpu_custom_call" | custom-call | flops 301989888 | bytes 4194304 | tf_op jit(solution)/shard_map/pallas_call | solution.py:126
  39.6 0.0 collective-permute-done.6.refs_6_.refs_2_.refs_10_.refs_7_.refs_15_
  39.6 0.1 collective-permute-done.8.refs_8_.refs_4_.refs_12_.refs_9_.refs_17_
  39.7 0.0 collective-permute-done.9.refs_9_.refs_14_.refs_19_
  39.7 3.0 %shard_map.50 = f32[4,128,128]{2,1,0:T(8,128)S(1)} custom-call(s32[1032]{0:T(1024)S(1)} %broadcast_1_refs_0__refs_1_.2.refs_0_.refs_1_, f32[776,128]{1,0:T(8,128)S(1)} %collective-permute-done.5.refs_5_.refs_1_.refs_9_.refs_6_.refs_14_, f32[776,128]{1,0:T(8,128)S(1)} %collective-permute-done.6.refs_6_.refs_2_.refs_10_.refs_7_.refs_15_, ...), custom_call_target="tpu_custom_call" | custom-call | flops 905969664 | bytes 4194304 | tf_op jit(solution)/shard_map/pallas_call | solution.py:126
  42.6 1.8 %collective-permute-start.10 = (f32[4,128,128]{2,1,0:T(8,128)S(1)}, f32[4,128,128]{2,1,0:T(8,128)S(1)}, u32[]{:S(2)}, u32[]{:S(2)}) collective-permute-start(f32[4,128,128]{2,1,0:T(8,128)S(1)} %shard_map.50), channel_id=1, source_target_pairs={{0,2},{4,6},{8,10},{12,14},{16,18},{20,22},{24,26},{28,30},{1,3},{... | collective-permute-start | bytes 786440 | tf_op jit(solution)/shard_map/window_1/ppermute | solution.py:215
  44.5 4.0 %shard_map.51 = f32[4,128,128]{2,1,0:T(8,128)S(1)} custom-call(f32[4,128,128]{2,1,0:T(8,128)S(1)} %shard_map.49.refs_15_.refs_0_, s32[1032]{0:T(1024)S(1)} %broadcast_1_refs_0__refs_1_.2.refs_0_.refs_1_, f32[776,128]{1,0:T(8,128)S(1)} %collective-permute-done.refs_1_.refs_5_.refs_2_.refs_10_, ...), custom_call_target="tpu_custom_call" | custom-call | flops 1207959552 | bytes 4194304 | tf_op jit(solution)/shard_map/pallas_call | solution.py:126
  48.4 0.3 collective-permute-start.11
  48.8 2.8 %shard_map.47.refs_10_ = f32[8,128,128]{2,1,0:T(8,128)S(1)} custom-call(s32[1032]{0:T(1024)S(1)} %broadcast_1_refs_0__refs_1_.2.refs_0_.refs_1_, f32[776,128]{1,0:T(8,128)S(1)} %collective-permute-done.refs_1_.refs_5_.refs_2_.refs_10_, f32[776,128]{1,0:T(8,128)S(1)} %collective-permute-done.1.refs_2_.refs_6_.refs_3_.refs_11_, ...), custom_call_target="tpu_custom_call" | custom-call | flops 1207959552 | bytes 4194304 | tf_op jit(solution)/shard_map/pallas_call | solution.py:126
  51.5 2.8 %shard_map.48 = f32[8,128,128]{2,1,0:T(8,128)S(1)} custom-call(s32[1032]{0:T(1024)S(1)} %broadcast_1_refs_0__refs_1_.2.refs_0_.refs_1_, f32[776,128]{1,0:T(8,128)S(1)} %collective-permute-done.refs_1_.refs_5_.refs_2_.refs_10_, f32[776,128]{1,0:T(8,128)S(1)} %collective-permute-done.1.refs_2_.refs_6_.refs_3_.refs_11_, ...), custom_call_target="tpu_custom_call" | custom-call | flops 1207959552 | bytes 4194304 | tf_op jit(solution)/shard_map/pallas_call | solution.py:126
  54.4 0.0 collective-permute-done.10
  54.4 2.7 %collective-permute-done.11 = f32[4,128,128]{2,1,0:T(8,128)S(1)} collective-permute-done((f32[4,128,128]{2,1,0:T(8,128)S(1)}, f32[4,128,128]{2,1,0:T(8,128)S(1)}, u32[]{:S(2)}, u32[]{:S(2)}) %collective-permute-start.11) | collective-permute-done | bytes 262176 | tf_op jit(solution)/shard_map/window_1/ppermute | solution.py:215
  57.0 0.9 %maximum_add_fusion = f32[1,2,1,4,128,128]{5,4,3,2,1,0:T(8,128)} fusion(f32[1,2,1,4,128,128]{5,4,3,2,1,0:T(8,128)S(1)} %bitcast.11, f32[1,2,1,2,128,128]{5,4,3,2,1,0:T(8,128)S(1)} %bitcast.15, f32[1,2,1,2,128,128]{5,4,3,2,1,0:T(8,128)S(1)} %bitcast.14), kind=kLoop, calls=%fused_computation | loop fusion | flops 262144 | bytes 1572864 | tf_op jit(solution)/shard_map/add | solution.py:251
  (1 shorter events, 0.0 us)
Async XLA Ops:
  1.6 38.1 %collective-permute-start.9 = (f32[3080,128]{1,0:T(8,128)S(1)}, f32[3080,128]{1,0:T(8,128)S(1)}, u32[]{:S(2)}, u32[]{:S(2)}) collective-permute-start(f32[3080,128]{1,0:T(8,128)S(1)} %get-tuple-element.8.refs_9_.refs_5_.refs_13_.refs_18_), channel_id=1, source_target_pairs={{0,1},{4,5},{8,9},{12,13},{16,17},{20,21},{24,25},{28,29},{1,0},{5... | collective-permute-start | bytes 4730888 | tf_op jit(solution)/shard_map/second/ppermute | solution.py:215
  4.6 20.2 %collective-permute-start.4 = (f32[776,128]{1,0:T(8,128)S(1)}, f32[776,128]{1,0:T(8,128)S(1)}, u32[]{:S(2)}, u32[]{:S(2)}) collective-permute-start(f32[776,128]{1,0:T(8,128)S(1)} %get-tuple-element.7), channel_id=1, source_target_pairs={{0,16},{4,20},{8,24},{12,28},{16,0},{20,4},{24,8},{28,12},{1,17},{... | collective-permute-start | bytes 1191944 | tf_op jit(solution)/shard_map/far/ppermute | solution.py:215
  7.2 22.5 %collective-permute-start = (f32[776,128]{1,0:T(8,128)S(1)}, f32[776,128]{1,0:T(8,128)S(1)}, u32[]{:S(2)}, u32[]{:S(2)}) collective-permute-start(f32[776,128]{1,0:T(8,128)S(1)} %get-tuple-element.7), channel_id=1, source_target_pairs={{0,0},{4,4},{8,2},{12,6},{16,16},{20,20},{24,18},{28,22},{1,1},{5,... | collective-permute-start | bytes 1191944 | tf_op jit(solution)/shard_map/share_0_0/ppermute | solution.py:215
  7.9 21.9 %collective-permute-start.2 = (f32[776,128]{1,0:T(8,128)S(1)}, f32[776,128]{1,0:T(8,128)S(1)}, u32[]{:S(2)}, u32[]{:S(2)}) collective-permute-start(f32[776,128]{1,0:T(8,128)S(1)} %get-tuple-element.7), channel_id=1, source_target_pairs={{0,8},{4,12},{8,10},{12,14},{16,24},{20,28},{24,26},{28,30},{1,9},... | collective-permute-start | bytes 1191944 | tf_op jit(solution)/shard_map/share_0_1/ppermute | solution.py:215
  24.8 5.5 %collective-permute-start.5 = (f32[776,128]{1,0:T(8,128)S(1)}, f32[776,128]{1,0:T(8,128)S(1)}, u32[]{:S(2)}, u32[]{:S(2)}) collective-permute-start(f32[776,128]{1,0:T(8,128)S(1)} %collective-permute-done.4), channel_id=1, source_target_pairs={{0,0},{4,4},{8,2},{12,6},{16,16},{20,20},{24,18},{28,22},{1,1},{5,... | collective-permute-start | bytes 1191944 | tf_op jit(solution)/shard_map/share_1_0/ppermute | solution.py:215
  25.5 12.5 %collective-permute-start.7 = (f32[776,128]{1,0:T(8,128)S(1)}, f32[776,128]{1,0:T(8,128)S(1)}, u32[]{:S(2)}, u32[]{:S(2)}) collective-permute-start(f32[776,128]{1,0:T(8,128)S(1)} %collective-permute-done.4), channel_id=1, source_target_pairs={{0,8},{4,12},{8,10},{12,14},{16,24},{20,28},{24,26},{28,30},{1,9},... | collective-permute-start | bytes 1191944 | tf_op jit(solution)/shard_map/share_1_1/ppermute | solution.py:215
  29.7 8.2 %collective-permute-start.1 = (f32[776,128]{1,0:T(8,128)S(1)}, f32[776,128]{1,0:T(8,128)S(1)}, u32[]{:S(2)}, u32[]{:S(2)}) collective-permute-start(f32[776,128]{1,0:T(8,128)S(1)} %collective-permute-done.refs_1_.refs_5_.refs_2_.refs_10_), channel_id=1, source_target_pairs={{0,4},{4,0},{8,12},{12,8},{16,20},{20,16},{24,28},{28,24},{1,5},{5... | collective-permute-start | bytes 1191944 | tf_op jit(solution)/shard_map/swap_0/ppermute | solution.py:215
  29.7 8.2 %collective-permute-start.3 = (f32[776,128]{1,0:T(8,128)S(1)}, f32[776,128]{1,0:T(8,128)S(1)}, u32[]{:S(2)}, u32[]{:S(2)}) collective-permute-start(f32[776,128]{1,0:T(8,128)S(1)} %collective-permute-done.2.refs_3_.refs_7_.refs_4_.refs_12_), channel_id=1, source_target_pairs={{0,4},{4,0},{8,12},{12,8},{16,20},{20,16},{24,28},{28,24},{1,5},{5... | collective-permute-start | bytes 1191944 | tf_op jit(solution)/shard_map/swap_0/ppermute | solution.py:215
  30.3 9.3 %collective-permute-start.6 = (f32[776,128]{1,0:T(8,128)S(1)}, f32[776,128]{1,0:T(8,128)S(1)}, u32[]{:S(2)}, u32[]{:S(2)}) collective-permute-start(f32[776,128]{1,0:T(8,128)S(1)} %collective-permute-done.5.refs_5_.refs_1_.refs_9_.refs_6_.refs_14_), channel_id=1, source_target_pairs={{0,4},{4,0},{8,12},{12,8},{16,20},{20,16},{24,28},{28,24},{1,5},{5... | collective-permute-start | bytes 1191944 | tf_op jit(solution)/shard_map/swap_1/ppermute | solution.py:215
  37.9 1.7 %collective-permute-start.8 = (f32[776,128]{1,0:T(8,128)S(1)}, f32[776,128]{1,0:T(8,128)S(1)}, u32[]{:S(2)}, u32[]{:S(2)}) collective-permute-start(f32[776,128]{1,0:T(8,128)S(1)} %collective-permute-done.7.refs_7_.refs_3_.refs_11_.refs_8_.refs_16_), channel_id=1, source_target_pairs={{0,4},{4,0},{8,12},{12,8},{16,20},{20,16},{24,28},{28,24},{1,5},{5... | collective-permute-start | bytes 1191944 | tf_op jit(solution)/shard_map/swap_1/ppermute | solution.py:215
  42.6 11.7 %collective-permute-start.10 = (f32[4,128,128]{2,1,0:T(8,128)S(1)}, f32[4,128,128]{2,1,0:T(8,128)S(1)}, u32[]{:S(2)}, u32[]{:S(2)}) collective-permute-start(f32[4,128,128]{2,1,0:T(8,128)S(1)} %shard_map.50), channel_id=1, source_target_pairs={{0,2},{4,6},{8,10},{12,14},{16,18},{20,22},{24,26},{28,30},{1,3},{... | collective-permute-start | bytes 786440 | tf_op jit(solution)/shard_map/window_1/ppermute | solution.py:215
  48.4 8.6 %collective-permute-start.11 = (f32[4,128,128]{2,1,0:T(8,128)S(1)}, f32[4,128,128]{2,1,0:T(8,128)S(1)}, u32[]{:S(2)}, u32[]{:S(2)}) collective-permute-start(f32[4,128,128]{2,1,0:T(8,128)S(1)} %shard_map.51), channel_id=1, source_target_pairs={{0,2},{4,6},{8,10},{12,14},{16,18},{20,22},{24,26},{28,30},{1,3},{... | collective-permute-start | bytes 786440 | tf_op jit(solution)/shard_map/window_1/ppermute | solution.py:215

commit v11 on v9

--- a/solution.py
+++ b/solution.py
@@ -178,18 +178,15 @@
     parts = [refs[n * arrays : (n + 1) * arrays] for n in range(7)]
     waits = []
     for blocks_hbm, index_hbm, out_hbm, tile_ref, index_ref, block_sem, index_sem in zip(*parts):
-        slots, edge, _ = blocks_hbm.shape
-        copies = [
-            pltpu.make_async_copy(blocks_hbm.at[slot], out_hbm.at[pl.ds(slot * edge, edge)], block_sem.at[slot])
-            for slot in range(slots)
-        ]
+        rows = blocks_hbm.shape[0]
+        copies = [pltpu.make_async_copy(blocks_hbm, out_hbm.at[pl.ds(0, rows)], block_sem.at[0])]
         index_copy = pltpu.make_async_copy(index_hbm, index_ref, index_sem)
         index_copy.start()
         for copy in copies:
             copy.start()
         waits += copies
     for blocks_hbm, index_hbm, out_hbm, tile_ref, index_ref, block_sem, index_sem in zip(*parts):
-        slots, edge, _ = blocks_hbm.shape
+        rows, slots = blocks_hbm.shape[0], index_hbm.shape[-1]
         pltpu.make_async_copy(index_hbm, index_ref, index_sem).wait()
         shape = tile_ref.shape
         row = lax.broadcasted_iota(jnp.int32, shape, 0)
@@ -199,7 +196,7 @@
             for slot in range(slots):
                 tile = jnp.where((row == n) & (column == slot), index_ref[0, n, slot].astype(jnp.float32), tile)
         tile_ref[...] = tile
-        tile_copy = pltpu.make_async_copy(tile_ref, out_hbm.at[pl.ds(slots * edge, PAD)], block_sem.at[slots])
+        tile_copy = pltpu.make_async_copy(tile_ref, out_hbm.at[pl.ds(rows, PAD)], block_sem.at[1])
         tile_copy.start()
         waits.append(tile_copy)
     for copy in waits:
@@ -211,13 +208,13 @@
     return pl.pallas_call(
         share_kernel,
         out_shape=tuple(
-            jax.ShapeDtypeStruct((value.shape[0] * value.shape[1] + PAD, value.shape[2]), jnp.float32) for value in blocks
+            jax.ShapeDtypeStruct((value.shape[0] + PAD, value.shape[1]), jnp.float32) for value in blocks
         ),
         in_specs=[anywhere] * (2 * len(blocks)),
         out_specs=(anywhere,) * len(blocks),
-        scratch_shapes=[pltpu.VMEM((PAD, value.shape[2]), jnp.float32) for value in blocks]
+        scratch_shapes=[pltpu.VMEM((PAD, value.shape[1]), jnp.float32) for value in blocks]
         + [pltpu.SMEM(value.shape, jnp.int32) for value in indices]
-        + [pltpu.SemaphoreType.DMA((value.shape[0] + 1,)) for value in blocks]
+        + [pltpu.SemaphoreType.DMA((2,)) for _ in blocks]
         + [pltpu.SemaphoreType.DMA for _ in blocks],
         compiler_params=pltpu.CompilerParams(vmem_limit_bytes=1024 * 1024),
     )(*[pltpu.with_memory_space_constraint(value, pltpu.HBM) for value in (*blocks, *indices)])
@@ -244,7 +241,7 @@
     def swap(name, value):
         return permute(name, value, lambda r, c: (r, c ^ 1))
 
-    share, second = build_shares((a_blocks[0], b_blocks[0]), (a_index, b_index))
+    share, second = build_shares((a_blocks.reshape(-1, edge), b_blocks.reshape(-1, edge)), (a_index, b_index))
     second_other = permute("second", second, lambda r, c: (r ^ 1, c))
 
     def spread(half, share, turn):

time: 57.8 us -> 57.8 us (level)
  Pallas kernels: 15.5 us -> 14.3 us
  starting transfers between devices: 17.9 us -> 18.7 us
  waiting for transfers between devices: 23.2 us -> 23.9 us
    pallas_call x5, Pallas kernels: 13.7 us -> 12.7 us  [product(): pl.pallas_call(functools.partial(product_kernel, edge, slots, narrow, wid...]
    ppermute x12, starting transfers between devices: 17.9 us -> 18.7 us  [permute(): return lax.ppermute(value, AXES, pairs)]
    ppermute x12, waiting for transfers between devices: 23.2 us -> 23.9 us  [permute(): return lax.ppermute(value, AXES, pairs)]
  transfers between devices with their start and end apart: 12 -> 12, of which waited for: 4 -> 4; matrix products, arithmetic and copies ran while one was open for 0% -> 0% of each run, Pallas kernels for 19% -> 17%
where the time goes in v11:
time: 57.8 us
  waiting for transfers between devices  23.9 us (41%)
  starting transfers between devices  18.7 us (32%)
  Pallas kernels  14.3 us (25%)
  other arithmetic  0.86 us (1%)
    ppermute x12, waiting for transfers between devices, permute(): return lax.ppermute(value, AXES, pairs)  23.9 us
    ppermute x12, starting transfers between devices, permute(): return lax.ppermute(value, AXES, pairs)  18.7 us
    pallas_call x5, Pallas kernels, product(): pl.pallas_call(functools.partial(product_kernel, edge, slots, narrow, wid...  12.7 us
    pallas_call x1, Pallas kernels, build_shares(): pl.pallas_call(share_kernel, out_shape=tuple((jax.ShapeDtypeStruct((value...  1.6 us
  transfers between devices with their start and end apart: 12, of which 4 were waited for; matrix products, arithmetic and copies ran while one was open for 0% of the time, Pallas kernels for 17%

profile of v11, /device:TPU:0, one launch (start us, length us, event | category | flops | bytes accessed | tf_op | source)
XLA Modules:
  0.0 57.8 jit_solution(8763096523953777371)
XLA Ops:
  0.0 1.6 %shard_map.46 = (f32[776,128]{1,0:T(8,128)S(1)}, f32[3080,128]{1,0:T(8,128)S(1)}) custom-call(f32[768,128]{1,0:T(8,128)} %bitcast.13, f32[3072,128]{1,0:T(8,128)} %bitcast.12, s32[1,2,6]{2,1,0:T(2,128)} %refs_2_.1, s32[1,2,24]{2,1,0:T(2,128)} %refs_3_.1), custom_call_target="tpu_custom_call" | custom-call | tf_op jit(solution)/shard_map/pallas_call | solution.py:208
  1.6 3.0 %collective-permute-start.9 = (f32[3080,128]{1,0:T(8,128)S(1)}, f32[3080,128]{1,0:T(8,128)S(1)}, u32[]{:S(2)}, u32[]{:S(2)}) collective-permute-start(f32[3080,128]{1,0:T(8,128)S(1)} %get-tuple-element.8.refs_9_.refs_5_.refs_13_.refs_18_), channel_id=1, source_target_pairs={{0,1},{4,5},{8,9},{12,13},{16,17},{20,21},{24,25},{28,29},{1,0},{5... | collective-permute-start | bytes 4730888 | tf_op jit(solution)/shard_map/second/ppermute | solution.py:239
  4.6 2.6 %collective-permute-start.4 = (f32[776,128]{1,0:T(8,128)S(1)}, f32[776,128]{1,0:T(8,128)S(1)}, u32[]{:S(2)}, u32[]{:S(2)}) collective-permute-start(f32[776,128]{1,0:T(8,128)S(1)} %get-tuple-element.7), channel_id=1, source_target_pairs={{0,16},{4,20},{8,24},{12,28},{16,0},{20,4},{24,8},{28,12},{1,17},{... | collective-permute-start | bytes 1191944 | tf_op jit(solution)/shard_map/far/ppermute | solution.py:239
  7.2 0.7 %collective-permute-start = (f32[776,128]{1,0:T(8,128)S(1)}, f32[776,128]{1,0:T(8,128)S(1)}, u32[]{:S(2)}, u32[]{:S(2)}) collective-permute-start(f32[776,128]{1,0:T(8,128)S(1)} %get-tuple-element.7), channel_id=1, source_target_pairs={{0,0},{4,4},{8,2},{12,6},{16,16},{20,20},{24,18},{28,22},{1,1},{5,... | collective-permute-start | bytes 1191944 | tf_op jit(solution)/shard_map/share_0_0/ppermute | solution.py:239
  7.9 4.3 %collective-permute-start.2 = (f32[776,128]{1,0:T(8,128)S(1)}, f32[776,128]{1,0:T(8,128)S(1)}, u32[]{:S(2)}, u32[]{:S(2)}) collective-permute-start(f32[776,128]{1,0:T(8,128)S(1)} %get-tuple-element.7), channel_id=1, source_target_pairs={{0,8},{4,12},{8,10},{12,14},{16,24},{20,28},{24,26},{28,30},{1,9},... | collective-permute-start | bytes 1191944 | tf_op jit(solution)/shard_map/share_0_1/ppermute | solution.py:239
  12.1 12.6 %collective-permute-done.4 = f32[776,128]{1,0:T(8,128)S(1)} collective-permute-done((f32[776,128]{1,0:T(8,128)S(1)}, f32[776,128]{1,0:T(8,128)S(1)}, u32[]{:S(2)}, u32[]{:S(2)}) %collective-permute-start.4) | collective-permute-done | bytes 397344 | tf_op jit(solution)/shard_map/far/ppermute | solution.py:239
  24.8 0.7 %collective-permute-start.5 = (f32[776,128]{1,0:T(8,128)S(1)}, f32[776,128]{1,0:T(8,128)S(1)}, u32[]{:S(2)}, u32[]{:S(2)}) collective-permute-start(f32[776,128]{1,0:T(8,128)S(1)} %collective-permute-done.4), channel_id=1, source_target_pairs={{0,0},{4,4},{8,2},{12,6},{16,16},{20,20},{24,18},{28,22},{1,1},{5,... | collective-permute-start | bytes 1191944 | tf_op jit(solution)/shard_map/share_1_0/ppermute | solution.py:239
  25.5 4.3 %collective-permute-start.7 = (f32[776,128]{1,0:T(8,128)S(1)}, f32[776,128]{1,0:T(8,128)S(1)}, u32[]{:S(2)}, u32[]{:S(2)}) collective-permute-start(f32[776,128]{1,0:T(8,128)S(1)} %collective-permute-done.4), channel_id=1, source_target_pairs={{0,8},{4,12},{8,10},{12,14},{16,24},{20,28},{24,26},{28,30},{1,9},... | collective-permute-start | bytes 1191944 | tf_op jit(solution)/shard_map/share_1_1/ppermute | solution.py:239
  29.7 0.0 collective-permute-done.refs_1_.refs_5_.refs_2_.refs_10_
  29.7 0.0 collective-permute-start.1
  29.7 0.0 collective-permute-done.2.refs_3_.refs_7_.refs_4_.refs_12_
  29.7 0.5 collective-permute-start.3
  30.2 0.0 collective-permute-done.5.refs_5_.refs_1_.refs_9_.refs_6_.refs_14_
  30.3 0.1 collective-permute-start.6
  30.3 7.6 %collective-permute-done.7.refs_7_.refs_3_.refs_11_.refs_8_.refs_16_ = f32[776,128]{1,0:T(8,128)S(1)} collective-permute-done((f32[776,128]{1,0:T(8,128)S(1)}, f32[776,128]{1,0:T(8,128)S(1)}, u32[]{:S(2)}, u32[]{:S(2)}) %collective-permute-start.7) | collective-permute-done | bytes 397344 | tf_op jit(solution)/shard_map/share_1_1/ppermute | solution.py:239
  37.9 0.0 collective-permute-start.8
  37.9 0.0 collective-permute-done.1.refs_2_.refs_6_.refs_3_.refs_11_
  37.9 0.0 collective-permute-done.3.refs_4_.refs_8_.refs_5_.refs_13_
  38.0 1.5 %shard_map.49.refs_15_.refs_0_ = f32[4,128,128]{2,1,0:T(8,128)S(1)} custom-call(s32[1032]{0:T(1024)S(1)} %broadcast_1_refs_0__refs_1_.2.refs_0_.refs_1_, f32[776,128]{1,0:T(8,128)S(1)} %collective-permute-done.refs_1_.refs_5_.refs_2_.refs_10_, f32[776,128]{1,0:T(8,128)S(1)} %collective-permute-done.1.refs_2_.refs_6_.refs_3_.refs_11_, ...), custom_call_target="tpu_custom_call" | custom-call | flops 301989888 | bytes 4194304 | tf_op jit(solution)/shard_map/pallas_call | solution.py:149
  39.5 0.0 collective-permute-done.6.refs_6_.refs_2_.refs_10_.refs_7_.refs_15_
  39.5 0.2 collective-permute-done.8.refs_8_.refs_4_.refs_12_.refs_9_.refs_17_
  39.7 0.0 collective-permute-done.9.refs_9_.refs_14_.refs_19_
  39.7 2.6 %shard_map.50 = f32[4,128,128]{2,1,0:T(8,128)S(1)} custom-call(s32[1032]{0:T(1024)S(1)} %broadcast_1_refs_0__refs_1_.2.refs_0_.refs_1_, f32[776,128]{1,0:T(8,128)S(1)} %collective-permute-done.5.refs_5_.refs_1_.refs_9_.refs_6_.refs_14_, f32[776,128]{1,0:T(8,128)S(1)} %collective-permute-done.6.refs_6_.refs_2_.refs_10_.refs_7_.refs_15_, ...), custom_call_target="tpu_custom_call" | custom-call | flops 905969664 | bytes 4194304 | tf_op jit(solution)/shard_map/pallas_call | solution.py:149
  42.2 1.8 %collective-permute-start.10 = (f32[4,128,128]{2,1,0:T(8,128)S(1)}, f32[4,128,128]{2,1,0:T(8,128)S(1)}, u32[]{:S(2)}, u32[]{:S(2)}) collective-permute-start(f32[4,128,128]{2,1,0:T(8,128)S(1)} %shard_map.50), channel_id=1, source_target_pairs={{0,2},{4,6},{8,10},{12,14},{16,18},{20,22},{24,26},{28,30},{1,3},{... | collective-permute-start | bytes 786440 | tf_op jit(solution)/shard_map/window_1/ppermute | solution.py:239
  44.0 3.3 %shard_map.51 = f32[4,128,128]{2,1,0:T(8,128)S(1)} custom-call(f32[4,128,128]{2,1,0:T(8,128)S(1)} %shard_map.49.refs_15_.refs_0_, s32[1032]{0:T(1024)S(1)} %broadcast_1_refs_0__refs_1_.2.refs_0_.refs_1_, f32[776,128]{1,0:T(8,128)S(1)} %collective-permute-done.refs_1_.refs_5_.refs_2_.refs_10_, ...), custom_call_target="tpu_custom_call" | custom-call | flops 1207959552 | bytes 4194304 | tf_op jit(solution)/shard_map/pallas_call | solution.py:149
  47.3 0.9 %collective-permute-start.11 = (f32[4,128,128]{2,1,0:T(8,128)S(1)}, f32[4,128,128]{2,1,0:T(8,128)S(1)}, u32[]{:S(2)}, u32[]{:S(2)}) collective-permute-start(f32[4,128,128]{2,1,0:T(8,128)S(1)} %shard_map.51), channel_id=1, source_target_pairs={{0,2},{4,6},{8,10},{12,14},{16,18},{20,22},{24,26},{28,30},{1,3},{... | collective-permute-start | bytes 786440 | tf_op jit(solution)/shard_map/window_1/ppermute | solution.py:239
  48.2 2.7 %shard_map.47.refs_10_ = f32[8,128,128]{2,1,0:T(8,128)S(1)} custom-call(s32[1032]{0:T(1024)S(1)} %broadcast_1_refs_0__refs_1_.2.refs_0_.refs_1_, f32[776,128]{1,0:T(8,128)S(1)} %collective-permute-done.refs_1_.refs_5_.refs_2_.refs_10_, f32[776,128]{1,0:T(8,128)S(1)} %collective-permute-done.1.refs_2_.refs_6_.refs_3_.refs_11_, ...), custom_call_target="tpu_custom_call" | custom-call | flops 1207959552 | bytes 4194304 | tf_op jit(solution)/shard_map/pallas_call | solution.py:149
  50.8 2.7 %shard_map.48 = f32[8,128,128]{2,1,0:T(8,128)S(1)} custom-call(s32[1032]{0:T(1024)S(1)} %broadcast_1_refs_0__refs_1_.2.refs_0_.refs_1_, f32[776,128]{1,0:T(8,128)S(1)} %collective-permute-done.refs_1_.refs_5_.refs_2_.refs_10_, f32[776,128]{1,0:T(8,128)S(1)} %collective-permute-done.1.refs_2_.refs_6_.refs_3_.refs_11_, ...), custom_call_target="tpu_custom_call" | custom-call | flops 1207959552 | bytes 4194304 | tf_op jit(solution)/shard_map/pallas_call | solution.py:149
  53.5 0.0 collective-permute-done.10
  53.5 3.4 %collective-permute-done.11 = f32[4,128,128]{2,1,0:T(8,128)S(1)} collective-permute-done((f32[4,128,128]{2,1,0:T(8,128)S(1)}, f32[4,128,128]{2,1,0:T(8,128)S(1)}, u32[]{:S(2)}, u32[]{:S(2)}) %collective-permute-start.11) | collective-permute-done | bytes 262176 | tf_op jit(solution)/shard_map/window_1/ppermute | solution.py:239
  57.0 0.9 %maximum_add_fusion = f32[1,2,1,4,128,128]{5,4,3,2,1,0:T(8,128)} fusion(f32[1,2,1,4,128,128]{5,4,3,2,1,0:T(8,128)S(1)} %bitcast.11, f32[1,2,1,2,128,128]{5,4,3,2,1,0:T(8,128)S(1)} %bitcast.15, f32[1,2,1,2,128,128]{5,4,3,2,1,0:T(8,128)S(1)} %bitcast.14), kind=kLoop, calls=%fused_computation | loop fusion | flops 262144 | bytes 1572864 | tf_op jit(solution)/shard_map/add | solution.py:275
  (1 shorter events, 0.0 us)
Async XLA Ops:
  1.6 38.1 %collective-permute-start.9 = (f32[3080,128]{1,0:T(8,128)S(1)}, f32[3080,128]{1,0:T(8,128)S(1)}, u32[]{:S(2)}, u32[]{:S(2)}) collective-permute-start(f32[3080,128]{1,0:T(8,128)S(1)} %get-tuple-element.8.refs_9_.refs_5_.refs_13_.refs_18_), channel_id=1, source_target_pairs={{0,1},{4,5},{8,9},{12,13},{16,17},{20,21},{24,25},{28,29},{1,0},{5... | collective-permute-start | bytes 4730888 | tf_op jit(solution)/shard_map/second/ppermute | solution.py:239
  4.6 20.2 %collective-permute-start.4 = (f32[776,128]{1,0:T(8,128)S(1)}, f32[776,128]{1,0:T(8,128)S(1)}, u32[]{:S(2)}, u32[]{:S(2)}) collective-permute-start(f32[776,128]{1,0:T(8,128)S(1)} %get-tuple-element.7), channel_id=1, source_target_pairs={{0,16},{4,20},{8,24},{12,28},{16,0},{20,4},{24,8},{28,12},{1,17},{... | collective-permute-start | bytes 1191944 | tf_op jit(solution)/shard_map/far/ppermute | solution.py:239
  7.2 22.5 %collective-permute-start = (f32[776,128]{1,0:T(8,128)S(1)}, f32[776,128]{1,0:T(8,128)S(1)}, u32[]{:S(2)}, u32[]{:S(2)}) collective-permute-start(f32[776,128]{1,0:T(8,128)S(1)} %get-tuple-element.7), channel_id=1, source_target_pairs={{0,0},{4,4},{8,2},{12,6},{16,16},{20,20},{24,18},{28,22},{1,1},{5,... | collective-permute-start | bytes 1191944 | tf_op jit(solution)/shard_map/share_0_0/ppermute | solution.py:239
  7.9 21.9 %collective-permute-start.2 = (f32[776,128]{1,0:T(8,128)S(1)}, f32[776,128]{1,0:T(8,128)S(1)}, u32[]{:S(2)}, u32[]{:S(2)}) collective-permute-start(f32[776,128]{1,0:T(8,128)S(1)} %get-tuple-element.7), channel_id=1, source_target_pairs={{0,8},{4,12},{8,10},{12,14},{16,24},{20,28},{24,26},{28,30},{1,9},... | collective-permute-start | bytes 1191944 | tf_op jit(solution)/shard_map/share_0_1/ppermute | solution.py:239
  24.8 5.5 %collective-permute-start.5 = (f32[776,128]{1,0:T(8,128)S(1)}, f32[776,128]{1,0:T(8,128)S(1)}, u32[]{:S(2)}, u32[]{:S(2)}) collective-permute-start(f32[776,128]{1,0:T(8,128)S(1)} %collective-permute-done.4), channel_id=1, source_target_pairs={{0,0},{4,4},{8,2},{12,6},{16,16},{20,20},{24,18},{28,22},{1,1},{5,... | collective-permute-start | bytes 1191944 | tf_op jit(solution)/shard_map/share_1_0/ppermute | solution.py:239
  25.5 12.5 %collective-permute-start.7 = (f32[776,128]{1,0:T(8,128)S(1)}, f32[776,128]{1,0:T(8,128)S(1)}, u32[]{:S(2)}, u32[]{:S(2)}) collective-permute-start(f32[776,128]{1,0:T(8,128)S(1)} %collective-permute-done.4), channel_id=1, source_target_pairs={{0,8},{4,12},{8,10},{12,14},{16,24},{20,28},{24,26},{28,30},{1,9},... | collective-permute-start | bytes 1191944 | tf_op jit(solution)/shard_map/share_1_1/ppermute | solution.py:239
  29.7 8.2 %collective-permute-start.1 = (f32[776,128]{1,0:T(8,128)S(1)}, f32[776,128]{1,0:T(8,128)S(1)}, u32[]{:S(2)}, u32[]{:S(2)}) collective-permute-start(f32[776,128]{1,0:T(8,128)S(1)} %collective-permute-done.refs_1_.refs_5_.refs_2_.refs_10_), channel_id=1, source_target_pairs={{0,4},{4,0},{8,12},{12,8},{16,20},{20,16},{24,28},{28,24},{1,5},{5... | collective-permute-start | bytes 1191944 | tf_op jit(solution)/shard_map/swap_0/ppermute | solution.py:239
  29.7 8.2 %collective-permute-start.3 = (f32[776,128]{1,0:T(8,128)S(1)}, f32[776,128]{1,0:T(8,128)S(1)}, u32[]{:S(2)}, u32[]{:S(2)}) collective-permute-start(f32[776,128]{1,0:T(8,128)S(1)} %collective-permute-done.2.refs_3_.refs_7_.refs_4_.refs_12_), channel_id=1, source_target_pairs={{0,4},{4,0},{8,12},{12,8},{16,20},{20,16},{24,28},{28,24},{1,5},{5... | collective-permute-start | bytes 1191944 | tf_op jit(solution)/shard_map/swap_0/ppermute | solution.py:239
  30.3 9.2 %collective-permute-start.6 = (f32[776,128]{1,0:T(8,128)S(1)}, f32[776,128]{1,0:T(8,128)S(1)}, u32[]{:S(2)}, u32[]{:S(2)}) collective-permute-start(f32[776,128]{1,0:T(8,128)S(1)} %collective-permute-done.5.refs_5_.refs_1_.refs_9_.refs_6_.refs_14_), channel_id=1, source_target_pairs={{0,4},{4,0},{8,12},{12,8},{16,20},{20,16},{24,28},{28,24},{1,5},{5... | collective-permute-start | bytes 1191944 | tf_op jit(solution)/shard_map/swap_1/ppermute | solution.py:239
  37.9 1.7 %collective-permute-start.8 = (f32[776,128]{1,0:T(8,128)S(1)}, f32[776,128]{1,0:T(8,128)S(1)}, u32[]{:S(2)}, u32[]{:S(2)}) collective-permute-start(f32[776,128]{1,0:T(8,128)S(1)} %collective-permute-done.7.refs_7_.refs_3_.refs_11_.refs_8_.refs_16_), channel_id=1, source_target_pairs={{0,4},{4,0},{8,12},{12,8},{16,20},{20,16},{24,28},{28,24},{1,5},{5... | collective-permute-start | bytes 1191944 | tf_op jit(solution)/shard_map/swap_1/ppermute | solution.py:239
  42.2 11.3 %collective-permute-start.10 = (f32[4,128,128]{2,1,0:T(8,128)S(1)}, f32[4,128,128]{2,1,0:T(8,128)S(1)}, u32[]{:S(2)}, u32[]{:S(2)}) collective-permute-start(f32[4,128,128]{2,1,0:T(8,128)S(1)} %shard_map.50), channel_id=1, source_target_pairs={{0,2},{4,6},{8,10},{12,14},{16,18},{20,22},{24,26},{28,30},{1,3},{... | collective-permute-start | bytes 786440 | tf_op jit(solution)/shard_map/window_1/ppermute | solution.py:239
  47.3 9.6 %collective-permute-start.11 = (f32[4,128,128]{2,1,0:T(8,128)S(1)}, f32[4,128,128]{2,1,0:T(8,128)S(1)}, u32[]{:S(2)}, u32[]{:S(2)}) collective-permute-start(f32[4,128,128]{2,1,0:T(8,128)S(1)} %shard_map.51), channel_id=1, source_target_pairs={{0,2},{4,6},{8,10},{12,14},{16,18},{20,22},{24,26},{28,30},{1,3},{... | collective-permute-start | bytes 786440 | tf_op jit(solution)/shard_map/window_1/ppermute | solution.py:239
